TPU v7x, 32 devices: a whole 2x2x4 slice. The times are simulated.
32 devices in a mesh: img: 8 (over z, core), seq: 4 (over y, x).
Axes of the slice: x: 2, y: 2, z: 4, core: 2. Of those that a mesh axis runs over, the one named last changes fastest.
Arguments:
- images: bfloat16 [32, 28, 224, 256], P('img', 'seq'), may hold values from -6 to 6
- cotangent: bfloat16 [32, 28, 224, 256], P('img', 'seq'), may hold values from -6 to 6
- valid_mask: int32 [32, 224], P('img'), may hold values from 0 to 1, as said below
- qkv_weight: float32 [256, 768], P('seq'), may hold values from -0.375 to 0.375
- out_weight: float32 [256, 256], P('seq'), may hold values from -3.5 to 3.5
- expand_weight: float32 [256, 1024], P('seq'), may hold values from -0.375 to 0.375
- shrink_weight: float32 [1024, 256], P('seq'), may hold values from -0.1875 to 0.1875
- small_params: float32 [16, 256], P(None, 'seq')
- expand_bias: float32 [1024], P('seq'), may hold values from -0.8 to 0.8
- first_qkv: float32 [256, 768], P('seq'), may hold values from -0.00067439064 to 0.00067439064
- first_out: float32 [256, 256], P('seq'), may hold values from -0.00067439064 to 0.00067439064
- first_expand: float32 [256, 1024], P('seq'), may hold values from -0.00067439064 to 0.00067439064
- first_shrink: float32 [1024, 256], P('seq'), may hold values from -0.00067439064 to 0.00067439064
- first_small: float32 [16, 256], P(None, 'seq'), may hold values from -0.00067439064 to 0.00067439064
- first_bias: float32 [1024], P('seq'), may hold values from -0.00067439064 to 0.00067439064
- second_qkv: float32 [256, 768], P('seq'), may hold values from 1.2633409e-09 to 5.0533635e-09
- second_out: float32 [256, 256], P('seq'), may hold values from 1.5791761e-10 to 6.3167044e-10
- second_expand: float32 [256, 1024], P('seq'), may hold values from 1.2633409e-09 to 5.0533635e-09
- second_shrink: float32 [1024, 256], P('seq'), may hold values from 1.2633409e-09 to 5.0533635e-09
- second_small: float32 [16, 256], P(None, 'seq'), may hold values from 1.2633409e-09 to 5.0533635e-09
- second_bias: float32 [1024], P('seq'), may hold values from 1.5791761e-10 to 6.3167044e-10
Outputs:
- block_out: float32 [32, 28, 224, 256], P('img', 'seq')
- input_grad: float32 [32, 28, 224, 256], P('img', 'seq')
- grad_norm: float32 [], replicated
- new_first_qkv: float32 [256, 768], P('seq')
- new_first_out: float32 [256, 256], P('seq')
- new_first_expand: float32 [256, 1024], P('seq')
- new_first_shrink: float32 [1024, 256], P('seq')
- new_first_small: float32 [16, 256], P(None, 'seq')
- new_first_bias: float32 [1024], P('seq')
- new_second_qkv: float32 [256, 768], P('seq')
- new_second_out: float32 [256, 256], P('seq')
- new_second_expand: float32 [256, 1024], P('seq')
- new_second_shrink: float32 [1024, 256], P('seq')
- new_second_small: float32 [16, 256], P(None, 'seq')
- new_second_bias: float32 [1024], P('seq')
- new_qkv_weight: float32 [256, 768], P('seq')
- new_out_weight: float32 [256, 256], P('seq')
- new_expand_weight: float32 [256, 1024], P('seq')
- new_shrink_weight: float32 [1024, 256], P('seq')
- new_small_params: float32 [16, 256], P(None, 'seq')
- new_expand_bias: float32 [1024], P('seq')
Inputs may be any that keep to these rules, and one draw needn't show every extreme that they name: `valid_mask`: every image has exactly 168 ones, and every aligned group of 7 columns holds at least one.
All inputs are finite; a program needn't handle non-finite values.
Results may differ from a plain program's by a relative error of at most 0.012.
The roundings to bfloat16 on the way count: a program that leaves them out, or rounds other values in their place, can miss the bound.
Values may be sent and summed in bfloat16 or wider, within the bound.
No kernel may reach another device: no remote copies, remote signals or barrier semaphores. Data moves between devices by JAX's collectives and lax.ppermute only.
A program may use at most 320 MiB of HBM per device.

v0:
```python
import jax
import jax.numpy as jnp
from jax import lax
from jax.sharding import PartitionSpec as P

HEADS = 8
STRIPE = 7
STEP = 10


EPS_NORM = 1e-05
NEG_FILL = -1000000000.0
BETA_ONE = 0.9
BETA_TWO = 0.999
ADAM_EPS = 1e-08
WEIGHT_DECAY = 0.05
CLIP_NORM = 1.0
RATE_MATRIX = 0.1
RATE_OUTPUT = 0.5
RATE_SMALL = 0.3
INV_ROOT_TWO = 0.7071067811865476
INV_ROOT_TAU = 0.3989422804014327


def layer_norm(values, gain_row, offset_row):
    center = values - jnp.mean(values, axis=-1, keepdims=True)
    spread = jnp.mean(center * center, axis=-1, keepdims=True)
    recip = lax.rsqrt(spread + EPS_NORM)
    scaled = center * recip
    return (scaled * gain_row + offset_row, scaled, recip)


def layer_norm_back(grad_out, scaled, recip, gain_row):
    grad_gain = jnp.sum(grad_out * scaled, axis=0)
    grad_offset = jnp.sum(grad_out, axis=0)
    grad_scaled = grad_out * gain_row
    inner_one = jnp.mean(grad_scaled, axis=-1, keepdims=True)
    inner_two = jnp.mean(grad_scaled * scaled, axis=-1, keepdims=True)
    return (recip * (grad_scaled - inner_one - scaled * inner_two), grad_gain, grad_offset)


def masked_scores(queries, key_part, valid_keys, score_scale):
    raw_scores = jnp.einsum(
        "wqhd,wkhd->whqk", queries, key_part, preferred_element_type=jnp.float32
    )
    return jnp.where(valid_keys[:, None, None, :], raw_scores * score_scale, NEG_FILL)


def attend_forward(queries, key_part, value_part, valid_keys, score_scale):
    scores = masked_scores(queries, key_part, valid_keys, score_scale)
    highest = jnp.max(scores, axis=-1, keepdims=True)
    weights = jnp.exp(scores - highest)
    totals = jnp.sum(weights, axis=-1, keepdims=True)
    weights_low = (weights / totals).astype(jnp.bfloat16)
    result = jnp.einsum(
        "whqk,wkhd->wqhd", weights_low, value_part, preferred_element_type=jnp.float32
    )
    return (result, highest, totals)


def attend_backward(
    queries, key_part, value_part, valid_keys, score_scale, highest, totals, grad_out
):
    scores = masked_scores(queries, key_part, valid_keys, score_scale)
    weights = jnp.exp(scores - highest) / totals
    weights_low = weights.astype(jnp.bfloat16)
    grad_values = jnp.einsum(
        "whqk,wqhd->wkhd", weights_low, grad_out, preferred_element_type=jnp.float32
    )
    grad_weights = jnp.einsum(
        "wqhd,wkhd->whqk", grad_out, value_part, preferred_element_type=jnp.float32
    )
    inner_sum = jnp.sum(grad_weights * weights, axis=-1, keepdims=True)
    grad_scores = (weights * (grad_weights - inner_sum)).astype(jnp.bfloat16)
    grad_queries = (
        jnp.einsum("whqk,wkhd->wqhd", grad_scores, key_part, preferred_element_type=jnp.float32)
        * score_scale
    )
    grad_keys = (
        jnp.einsum("whqk,wqhd->wkhd", grad_scores, queries, preferred_element_type=jnp.float32)
        * score_scale
    )
    return (grad_queries, grad_keys, grad_values)


def position_forward(value_grid, tap_rows, offset_row):
    size_a, size_b = (value_grid.shape[1], value_grid.shape[2])
    padded = jnp.pad(value_grid, ((0, 0), (1, 1), (1, 1), (0, 0)))
    result = jnp.zeros(value_grid.shape, jnp.float32)
    for tap_row in range(3):
        for tap_col in range(3):
            result = (
                result
                + padded[:, tap_row : tap_row + size_a, tap_col : tap_col + size_b, :]
                * tap_rows[3 * tap_row + tap_col]
            )
    return result + offset_row


def position_back(value_grid, tap_rows, grad_grid):
    size_a, size_b = (value_grid.shape[1], value_grid.shape[2])
    pad_spec = ((0, 0), (1, 1), (1, 1), (0, 0))
    padded_value = jnp.pad(value_grid, pad_spec)
    padded_grad = jnp.pad(grad_grid, pad_spec)
    value_grad = jnp.zeros(value_grid.shape, jnp.float32)
    tap_grads = []
    for tap_row in range(3):
        for tap_col in range(3):
            shifted = padded_value[:, tap_row : tap_row + size_a, tap_col : tap_col + size_b, :]
            tap_grads.append(jnp.sum(shifted * grad_grid, axis=(0, 1, 2)))
            moved = padded_grad[
                :, 2 - tap_row : 2 - tap_row + size_a, 2 - tap_col : 2 - tap_col + size_b, :
            ]
            value_grad = value_grad + moved * tap_rows[3 * tap_row + tap_col]
    return (value_grad, jnp.stack(tap_grads), jnp.sum(grad_grid, axis=(0, 1, 2)))


def adam_update(weight, first_old, second_old, grad_value, rate_value, decay_value):
    new_first = BETA_ONE * first_old + (1.0 - BETA_ONE) * grad_value
    new_second = BETA_TWO * second_old + (1.0 - BETA_TWO) * grad_value * grad_value
    first_hat = new_first / (1.0 - BETA_ONE**STEP)
    second_hat = new_second / (1.0 - BETA_TWO**STEP)
    new_weight = weight - rate_value * (
        first_hat / (jnp.sqrt(second_hat) + ADAM_EPS) + decay_value * weight
    )
    return (new_first, new_second, new_weight)


def on_device(
    images,
    cotangent,
    valid_mask,
    qkv_weight,
    out_weight,
    expand_weight,
    shrink_weight,
    small_params,
    expand_bias,
    first_qkv,
    first_out,
    first_expand,
    first_shrink,
    first_small,
    first_bias,
    second_qkv,
    second_out,
    second_expand,
    second_shrink,
    second_small,
    second_bias,
):
    low_dtype = jnp.bfloat16
    gathered = (
        lax.all_gather(qkv_weight.astype(low_dtype), "seq", axis=0, tiled=True),
        lax.all_gather(out_weight.astype(low_dtype), "seq", axis=0, tiled=True),
        lax.all_gather(expand_weight.astype(low_dtype), "seq", axis=0, tiled=True),
        lax.all_gather(shrink_weight.astype(low_dtype), "seq", axis=0, tiled=True),
        lax.all_gather(small_params.astype(low_dtype), "seq", axis=1, tiled=True),
        lax.all_gather(expand_bias.astype(low_dtype), "seq", axis=0, tiled=True),
    )
    qkv_low, out_low, expand_low, shrink_low, small_low, bias_low = gathered
    small_full = small_low.astype(jnp.float32)
    bias_full = bias_low.astype(jnp.float32)
    row_count, grid_width, channels = (images.shape[1], images.shape[2], images.shape[3])
    half_width = channels // 2
    head_count = HEADS // 2
    head_size = half_width // head_count
    score_scale = head_size ** (-0.5)
    seq_count = lax.axis_size("seq")
    height = row_count * seq_count
    width_dev = grid_width // seq_count
    stripes_dev = width_dev // STRIPE
    tokens = row_count * grid_width
    taps_across = small_full[0:9, :half_width]
    taps_down = small_full[0:9, half_width:]
    column_start = lax.axis_index("seq") * width_dev
    qkv_across = qkv_low[:, : 3 * half_width]
    qkv_down = qkv_low[:, 3 * half_width :]

    def micro_batch(summed, item_pack):
        image_rows, back_rows, mask_row = item_pack
        column_valid = mask_row > 0
        image_flat = image_rows.reshape(tokens, channels).astype(jnp.float32)
        normed, scaled_one, recip_one = layer_norm(image_flat, small_full[9], small_full[10])
        normed_low = normed.astype(low_dtype)
        across_mixed = jnp.dot(normed_low, qkv_across, preferred_element_type=jnp.float32).astype(
            low_dtype
        )
        across_mixed = across_mixed.reshape(row_count, grid_width, 3 * half_width)
        across_valid = jnp.broadcast_to(column_valid[None, :], (row_count, grid_width)).reshape(
            1, tokens
        )
        across_parts = across_mixed.reshape(1, tokens, 3, head_count, head_size)
        across_query = across_parts[:, :, 0]
        across_key = across_parts[:, :, 1]
        across_value = across_parts[:, :, 2]
        across_attn, across_top, across_total = attend_forward(
            across_query, across_key, across_value, across_valid, score_scale
        )
        across_grid = (
            across_mixed[..., 2 * half_width :]
            .astype(jnp.float32)
            .reshape(1, row_count, grid_width, half_width)
        )
        across_out = across_attn.reshape(1, row_count, grid_width, half_width) + position_forward(
            across_grid, taps_across, small_full[11, :half_width]
        )
        down_local = jnp.dot(normed_low, qkv_down, preferred_element_type=jnp.float32).astype(
            low_dtype
        )
        columns = lax.all_to_all(
            down_local.reshape(row_count, grid_width, 3 * half_width),
            "seq",
            split_axis=1,
            concat_axis=0,
            tiled=True,
        )
        down_grid = columns.reshape(height, stripes_dev, STRIPE, 3 * half_width).transpose(
            1, 0, 2, 3
        )
        local_valid = lax.dynamic_slice_in_dim(column_valid, column_start, width_dev)
        down_valid = jnp.broadcast_to(
            local_valid.reshape(stripes_dev, 1, STRIPE), (stripes_dev, height, STRIPE)
        ).reshape(stripes_dev, height * STRIPE)
        down_parts = down_grid.reshape(stripes_dev, height * STRIPE, 3, head_count, head_size)
        down_query = down_parts[:, :, 0]
        down_key = down_parts[:, :, 1]
        down_value = down_parts[:, :, 2]
        down_attn, down_top, down_total = attend_forward(
            down_query, down_key, down_value, down_valid, score_scale
        )
        down_values_grid = down_grid[..., 2 * half_width :].astype(jnp.float32)
        down_out = down_attn.reshape(stripes_dev, height, STRIPE, half_width) + position_forward(
            down_values_grid, taps_down, small_full[11, half_width:]
        )
        down_cols_low = (
            down_out.transpose(1, 0, 2, 3).reshape(height, width_dev, half_width).astype(low_dtype)
        )
        down_rows = lax.all_to_all(down_cols_low, "seq", split_axis=0, concat_axis=1, tiled=True)
        joined = jnp.concatenate(
            [across_out.reshape(row_count, grid_width, half_width).astype(low_dtype), down_rows],
            axis=-1,
        ).reshape(tokens, channels)
        attended_out = jnp.dot(joined, out_low, preferred_element_type=jnp.float32) + small_full[12]
        middle = image_flat + attended_out
        normed_two, scaled_two, recip_two = layer_norm(middle, small_full[13], small_full[14])
        normed_two_low = normed_two.astype(low_dtype)
        hidden = jnp.dot(normed_two_low, expand_low, preferred_element_type=jnp.float32) + bias_full
        active = jax.nn.gelu(hidden, approximate=False).astype(low_dtype)
        block_rows = middle + (
            jnp.dot(active, shrink_low, preferred_element_type=jnp.float32) + small_full[15]
        )
        back_flat = back_rows.reshape(tokens, channels).astype(jnp.float32)
        back_low = back_flat.astype(low_dtype)
        grad_shrink = jnp.einsum("tf,tc->fc", active, back_low, preferred_element_type=jnp.float32)
        grad_last_bias = jnp.sum(back_low.astype(jnp.float32), axis=0)
        grad_active = jnp.einsum(
            "tc,fc->tf", back_low, shrink_low, preferred_element_type=jnp.float32
        )
        erf_part = 0.5 * (1.0 + lax.erf(hidden * INV_ROOT_TWO))
        density = jnp.exp(-0.5 * hidden * hidden) * INV_ROOT_TAU
        grad_hidden = (grad_active * (erf_part + hidden * density)).astype(low_dtype)
        grad_expand = jnp.einsum(
            "tc,tf->cf", normed_two_low, grad_hidden, preferred_element_type=jnp.float32
        )
        grad_bias = jnp.sum(grad_hidden.astype(jnp.float32), axis=0)
        grad_normed_two = jnp.einsum(
            "tf,cf->tc", grad_hidden, expand_low, preferred_element_type=jnp.float32
        )
        grad_middle_norm, grad_gain_two, grad_offset_two = layer_norm_back(
            grad_normed_two, scaled_two, recip_two, small_full[13]
        )
        grad_middle = back_flat + grad_middle_norm
        grad_attended = grad_middle.astype(low_dtype)
        grad_out_weight = jnp.einsum(
            "tc,te->ce", joined, grad_attended, preferred_element_type=jnp.float32
        )
        grad_out_bias = jnp.sum(grad_attended.astype(jnp.float32), axis=0)
        grad_joined = jnp.einsum(
            "te,ce->tc", grad_attended, out_low, preferred_element_type=jnp.float32
        ).astype(low_dtype)
        grad_joined = grad_joined.reshape(row_count, grid_width, channels)
        grad_across = grad_joined[..., :half_width]
        across_dq, across_dk, across_dv = attend_backward(
            across_query,
            across_key,
            across_value,
            across_valid,
            score_scale,
            across_top,
            across_total,
            grad_across.reshape(1, tokens, head_count, head_size),
        )
        across_pos_grad, across_tap_grad, across_offset_grad = position_back(
            across_grid,
            taps_across,
            grad_across.astype(jnp.float32).reshape(1, row_count, grid_width, half_width),
        )
        across_value_grad = across_dv.reshape(
            row_count, grid_width, half_width
        ) + across_pos_grad.reshape(row_count, grid_width, half_width)
        across_mixed_grad = jnp.concatenate(
            [
                across_dq.reshape(row_count, grid_width, half_width),
                across_dk.reshape(row_count, grid_width, half_width),
                across_value_grad,
            ],
            axis=-1,
        ).astype(low_dtype)
        across_mixed_flat = across_mixed_grad.reshape(tokens, 3 * half_width)
        grad_down_cols = lax.all_to_all(
            grad_joined[..., half_width:], "seq", split_axis=1, concat_axis=0, tiled=True
        )
        grad_down_grid = grad_down_cols.reshape(height, stripes_dev, STRIPE, half_width).transpose(
            1, 0, 2, 3
        )
        down_dq, down_dk, down_dv = attend_backward(
            down_query,
            down_key,
            down_value,
            down_valid,
            score_scale,
            down_top,
            down_total,
            grad_down_grid.reshape(stripes_dev, height * STRIPE, head_count, head_size),
        )
        down_pos_grad, down_tap_grad, down_offset_grad = position_back(
            down_values_grid, taps_down, grad_down_grid.astype(jnp.float32)
        )
        grid_shape = (stripes_dev, height, STRIPE, half_width)
        down_mixed_grad = jnp.concatenate(
            [
                down_dq.reshape(grid_shape),
                down_dk.reshape(grid_shape),
                down_dv.reshape(grid_shape) + down_pos_grad,
            ],
            axis=-1,
        )
        down_mixed_low = (
            down_mixed_grad.transpose(1, 0, 2, 3)
            .reshape(height, width_dev, 3 * half_width)
            .astype(low_dtype)
        )
        grad_qkv_across = jnp.einsum(
            "tc,tf->cf", normed_low, across_mixed_flat, preferred_element_type=jnp.float32
        )
        grad_normed_across = jnp.einsum(
            "tf,cf->tc", across_mixed_flat, qkv_across, preferred_element_type=jnp.float32
        )
        down_mixed_rows = lax.all_to_all(
            down_mixed_low, "seq", split_axis=0, concat_axis=1, tiled=True
        )
        down_rows_flat = down_mixed_rows.reshape(tokens, 3 * half_width)
        grad_qkv_down = jnp.einsum(
            "tc,tf->cf", normed_low, down_rows_flat, preferred_element_type=jnp.float32
        )
        partial_rows = jnp.einsum(
            "tf,cf->tc", down_rows_flat, qkv_down, preferred_element_type=jnp.float32
        ).astype(low_dtype)
        grad_qkv = jnp.concatenate([grad_qkv_across, grad_qkv_down], axis=1)
        grad_normed = grad_normed_across + partial_rows.astype(jnp.float32)
        grad_image_norm, grad_gain_one, grad_offset_one = layer_norm_back(
            grad_normed, scaled_one, recip_one, small_full[9]
        )
        image_grad = grad_middle + grad_image_norm
        tap_grad = jnp.concatenate([across_tap_grad, down_tap_grad], axis=1)
        offset_grad = jnp.concatenate([across_offset_grad, down_offset_grad], axis=0)
        grad_small = jnp.concatenate(
            [
                tap_grad,
                jnp.stack(
                    [
                        grad_gain_one,
                        grad_offset_one,
                        offset_grad,
                        grad_out_bias,
                        grad_gain_two,
                        grad_offset_two,
                        grad_last_bias,
                    ]
                ),
            ],
            axis=0,
        )
        fresh = (grad_qkv, grad_out_weight, grad_expand, grad_shrink, grad_small, grad_bias)
        summed = tuple((old_sum + new_term for old_sum, new_term in zip(summed, fresh)))
        return (
            summed,
            (
                block_rows.reshape(row_count, grid_width, channels),
                image_grad.reshape(row_count, grid_width, channels),
            ),
        )

    zeros_init = (
        jnp.zeros(qkv_low.shape, jnp.float32),
        jnp.zeros(out_low.shape, jnp.float32),
        jnp.zeros(expand_low.shape, jnp.float32),
        jnp.zeros(shrink_low.shape, jnp.float32),
        jnp.zeros(small_low.shape, jnp.float32),
        jnp.zeros(bias_low.shape, jnp.float32),
    )
    summed, (block_out, input_grad) = lax.scan(
        micro_batch, zeros_init, (images, cotangent, valid_mask)
    )
    sum_qkv, sum_out, sum_expand, sum_shrink, sum_small, sum_bias = summed
    params = (qkv_weight, out_weight, expand_weight, shrink_weight, small_params, expand_bias)
    shard_dims = (0, 0, 0, 0, 1, 0)
    full_grads = lax.psum(
        (sum_qkv, sum_out, sum_expand, sum_shrink, sum_small, sum_bias), ("img", "seq")
    )
    squared = jnp.float32(0.0)
    for full_grad in full_grads:
        squared = squared + jnp.sum(full_grad * full_grad)
    owner = lax.axis_index("seq")
    shares = tuple(
        (
            lax.dynamic_slice_in_dim(
                full_grad, owner * local_part.shape[dim_idx], local_part.shape[dim_idx], dim_idx
            )
            for full_grad, local_part, dim_idx in zip(full_grads, params, shard_dims)
        )
    )
    grad_norm = jnp.sqrt(squared)
    factor = CLIP_NORM / jnp.maximum(grad_norm, CLIP_NORM)
    rates = (RATE_MATRIX, RATE_OUTPUT, RATE_MATRIX, RATE_MATRIX, RATE_SMALL, RATE_MATRIX)
    decays = (WEIGHT_DECAY, WEIGHT_DECAY, WEIGHT_DECAY, WEIGHT_DECAY, 0.0, 0.0)
    firsts = (first_qkv, first_out, first_expand, first_shrink, first_small, first_bias)
    seconds = (second_qkv, second_out, second_expand, second_shrink, second_small, second_bias)
    updated = [
        adam_update(
            params[index],
            firsts[index],
            seconds[index],
            shares[index] * factor,
            rates[index],
            decays[index],
        )
        for index in range(6)
    ]
    return (
        block_out,
        input_grad,
        grad_norm,
        updated[0][0],
        updated[1][0],
        updated[2][0],
        updated[3][0],
        updated[4][0],
        updated[5][0],
        updated[0][1],
        updated[1][1],
        updated[2][1],
        updated[3][1],
        updated[4][1],
        updated[5][1],
        updated[0][2],
        updated[1][2],
        updated[2][2],
        updated[3][2],
        updated[4][2],
        updated[5][2],
    )


def solution(mesh):
    placed = (
        P("img", "seq", None, None),
        P("img", "seq", None, None),
        P("img", None),
        P("seq", None),
        P("seq", None),
        P("seq", None),
        P("seq", None),
        P(None, "seq"),
        P("seq"),
        P("seq", None),
        P("seq", None),
        P("seq", None),
        P("seq", None),
        P(None, "seq"),
        P("seq"),
        P("seq", None),
        P("seq", None),
        P("seq", None),
        P("seq", None),
        P(None, "seq"),
        P("seq"),
    )
    return jax.shard_map(
        on_device,
        mesh=mesh,
        in_specs=placed,
        out_specs=(
            P("img", "seq", None, None),
            P("img", "seq", None, None),
            P(),
            P("seq", None),
            P("seq", None),
            P("seq", None),
            P("seq", None),
            P(None, "seq"),
            P("seq"),
            P("seq", None),
            P("seq", None),
            P("seq", None),
            P("seq", None),
            P(None, "seq"),
            P("seq"),
            P("seq", None),
            P("seq", None),
            P("seq", None),
            P("seq", None),
            P(None, "seq"),
            P("seq"),
        ),
        check_vma=False,
    )
```

profile of v0, /device:TPU:0, one launch (start us, length us, event | category | flops | bytes accessed | tf_op | source)
XLA Modules:
  0.0 1736.4 jit_solution(2342299207104912622)
XLA Ops:
  70.3 1497.7 %while.27 = (s32[]{:T(128)}, f32[256,768]{1,0:T(8,128)}, f32[256,256]{1,0:T(8,128)}, f32[256,1024]{1,0:T(8,128)}, f32[1024,256]{1,0:T(8,128)}, /*index=5*/f32[16...) while((s32[]{:T(128)}, f32[256,768]{1,0:T(8,128)}, ...), condition=%wide.region_42.43_spmd.clone, body=%wide.region_0.42_spmd.clone.sunk | while | flops 12017894400 | bytes 761613760 | solution.py:403
  89.1 19.0 %exponential_reduce_fusion.2 = (f32[4,1568]{1,0:T(4,128)S(1)}, f32[4,1568,1568]{1,2,0:T(8,128)}) fusion(pred[1568]{0:T(1024)(128)(4,1)S(1)} %broadcast_in_dim.181, bf16[1,1568,3,4,32]{1,4,3,2,0:T(8,128)(2,1)S(1)} %bitcast.573), kind=kOutput, calls=%fused_computation.7.clone.1 | convolution fusion | flops 668747264 | bytes 40217088 | tf_op jit(solution)/shard_map/while/body/eval_jaxpr/sub | solution.py:65
  108.1 16.9 fusion.328
  204.2 16.5 fusion.331
  232.5 16.6 fusion.338
  249.2 26.6 %multiply_reduce_fusion.24 = (f32[4,1568]{1,0:T(4,128)S(1)}, f32[4,1568,1568]{1,2,0:T(8,128)}) fusion(f32[4,1568]{1,0:T(4,128)S(1)} %get-tuple-element.773, f32[4,1568,1568]{1,2,0:T(8,128)} %get-tuple-element.772, bf16[1568,4,32]{0,2,1:T(8,128)(2,1)S(1)} %reshape.579, bf16[1,1568,3,4,32]{1,4,3,2,0:T(8,128)(2,1)S(1)} %bitcast.575), kind=kOutput, calls=%fused_computation.4.clone.1 | convolution fusion | flops 658904960 | bytes 79579648 | tf_op jit(solution)/shard_map/while/body/eval_jaxpr/wqhd,wkhd->whqk/dot_general | solution.py:70
  275.7 33.4 %multiply_convert_fusion.5 = bf16[4,1568,1568]{1,2,0:T(8,128)(2,1)} fusion(f32[4,1568,1568]{1,2,0:T(8,128)} %get-tuple-element.800, f32[4,1568]{1,0:T(4,128)S(1)} %get-tuple-element.801, f32[4,1568]{1,0:T(4,128)S(1)} %get-tuple-element.773, f32[4,1568,1568]{1,2,0:T(8,128)} %get-tuple-element.772), kind=kLoop, calls=%fused_computation.3.clone.1 | loop fusion | flops 39337984 | bytes 98395136 | tf_op jit(solution)/shard_map/while/body/eval_jaxpr/convert_element_type | solution.py:74
  346.8 12.3 fusion.339
  463.0 19.0 %exponential_reduce_fusion.2 = (f32[4,1568]{1,0:T(4,128)S(1)}, f32[4,1568,1568]{1,2,0:T(8,128)}) fusion(pred[1568]{0:T(1024)(128)(4,1)S(1)} %broadcast_in_dim.181, bf16[1,1568,3,4,32]{1,4,3,2,0:T(8,128)(2,1)S(1)} %bitcast.573), kind=kOutput, calls=%fused_computation.7.clone.1 | convolution fusion | flops 668747264 | bytes 40217088 | tf_op jit(solution)/shard_map/while/body/eval_jaxpr/sub | solution.py:65
  482.1 16.9 fusion.328
  578.0 16.5 fusion.331
  606.2 16.6 fusion.338
  622.9 26.6 %multiply_reduce_fusion.24 = (f32[4,1568]{1,0:T(4,128)S(1)}, f32[4,1568,1568]{1,2,0:T(8,128)}) fusion(f32[4,1568]{1,0:T(4,128)S(1)} %get-tuple-element.773, f32[4,1568,1568]{1,2,0:T(8,128)} %get-tuple-element.772, bf16[1568,4,32]{0,2,1:T(8,128)(2,1)S(1)} %reshape.579, bf16[1,1568,3,4,32]{1,4,3,2,0:T(8,128)(2,1)S(1)} %bitcast.575), kind=kOutput, calls=%fused_computation.4.clone.1 | convolution fusion | flops 658904960 | bytes 79579648 | tf_op jit(solution)/shard_map/while/body/eval_jaxpr/wqhd,wkhd->whqk/dot_general | solution.py:70
  649.4 33.4 %multiply_convert_fusion.5 = bf16[4,1568,1568]{1,2,0:T(8,128)(2,1)} fusion(f32[4,1568,1568]{1,2,0:T(8,128)} %get-tuple-element.800, f32[4,1568]{1,0:T(4,128)S(1)} %get-tuple-element.801, f32[4,1568]{1,0:T(4,128)S(1)} %get-tuple-element.773, f32[4,1568,1568]{1,2,0:T(8,128)} %get-tuple-element.772), kind=kLoop, calls=%fused_computation.3.clone.1 | loop fusion | flops 39337984 | bytes 98395136 | tf_op jit(solution)/shard_map/while/body/eval_jaxpr/convert_element_type | solution.py:74
  693.2 11.5 fusion.341
  720.6 12.3 fusion.339
  836.8 19.0 %exponential_reduce_fusion.2 = (f32[4,1568]{1,0:T(4,128)S(1)}, f32[4,1568,1568]{1,2,0:T(8,128)}) fusion(pred[1568]{0:T(1024)(128)(4,1)S(1)} %broadcast_in_dim.181, bf16[1,1568,3,4,32]{1,4,3,2,0:T(8,128)(2,1)S(1)} %bitcast.573), kind=kOutput, calls=%fused_computation.7.clone.1 | convolution fusion | flops 668747264 | bytes 40217088 | tf_op jit(solution)/shard_map/while/body/eval_jaxpr/sub | solution.py:65
  855.8 16.9 fusion.328
  951.7 16.5 fusion.331
  980.0 16.6 fusion.338
  996.6 26.6 %multiply_reduce_fusion.24 = (f32[4,1568]{1,0:T(4,128)S(1)}, f32[4,1568,1568]{1,2,0:T(8,128)}) fusion(f32[4,1568]{1,0:T(4,128)S(1)} %get-tuple-element.773, f32[4,1568,1568]{1,2,0:T(8,128)} %get-tuple-element.772, bf16[1568,4,32]{0,2,1:T(8,128)(2,1)S(1)} %reshape.579, bf16[1,1568,3,4,32]{1,4,3,2,0:T(8,128)(2,1)S(1)} %bitcast.575), kind=kOutput, calls=%fused_computation.4.clone.1 | convolution fusion | flops 658904960 | bytes 79579648 | tf_op jit(solution)/shard_map/while/body/eval_jaxpr/wqhd,wkhd->whqk/dot_general | solution.py:70
  1023.2 33.4 %multiply_convert_fusion.5 = bf16[4,1568,1568]{1,2,0:T(8,128)(2,1)} fusion(f32[4,1568,1568]{1,2,0:T(8,128)} %get-tuple-element.800, f32[4,1568]{1,0:T(4,128)S(1)} %get-tuple-element.801, f32[4,1568]{1,0:T(4,128)S(1)} %get-tuple-element.773, f32[4,1568,1568]{1,2,0:T(8,128)} %get-tuple-element.772), kind=kLoop, calls=%fused_computation.3.clone.1 | loop fusion | flops 39337984 | bytes 98395136 | tf_op jit(solution)/shard_map/while/body/eval_jaxpr/convert_element_type | solution.py:74
  1094.3 12.3 fusion.339
  1210.6 19.0 %exponential_reduce_fusion.2 = (f32[4,1568]{1,0:T(4,128)S(1)}, f32[4,1568,1568]{1,2,0:T(8,128)}) fusion(pred[1568]{0:T(1024)(128)(4,1)S(1)} %broadcast_in_dim.181, bf16[1,1568,3,4,32]{1,4,3,2,0:T(8,128)(2,1)S(1)} %bitcast.573), kind=kOutput, calls=%fused_computation.7.clone.1 | convolution fusion | flops 668747264 | bytes 40217088 | tf_op jit(solution)/shard_map/while/body/eval_jaxpr/sub | solution.py:65
  1229.6 16.9 fusion.328
  1325.5 16.5 fusion.331
  1353.7 16.6 fusion.338
  1370.4 26.6 %multiply_reduce_fusion.24 = (f32[4,1568]{1,0:T(4,128)S(1)}, f32[4,1568,1568]{1,2,0:T(8,128)}) fusion(f32[4,1568]{1,0:T(4,128)S(1)} %get-tuple-element.773, f32[4,1568,1568]{1,2,0:T(8,128)} %get-tuple-element.772, bf16[1568,4,32]{0,2,1:T(8,128)(2,1)S(1)} %reshape.579, bf16[1,1568,3,4,32]{1,4,3,2,0:T(8,128)(2,1)S(1)} %bitcast.575), kind=kOutput, calls=%fused_computation.4.clone.1 | convolution fusion | flops 658904960 | bytes 79579648 | tf_op jit(solution)/shard_map/while/body/eval_jaxpr/wqhd,wkhd->whqk/dot_general | solution.py:70
  1396.9 33.4 %multiply_convert_fusion.5 = bf16[4,1568,1568]{1,2,0:T(8,128)(2,1)} fusion(f32[4,1568,1568]{1,2,0:T(8,128)} %get-tuple-element.800, f32[4,1568]{1,0:T(4,128)S(1)} %get-tuple-element.801, f32[4,1568]{1,0:T(4,128)S(1)} %get-tuple-element.773, f32[4,1568,1568]{1,2,0:T(8,128)} %get-tuple-element.772), kind=kLoop, calls=%fused_computation.3.clone.1 | loop fusion | flops 39337984 | bytes 98395136 | tf_op jit(solution)/shard_map/while/body/eval_jaxpr/convert_element_type | solution.py:74
  1468.1 12.3 fusion.339
  1568.1 40.0 %all-reduce.4 = (f32[16,256]{1,0:T(8,128)S(1)}, f32[1024]{0:T(1024)S(1)}) all-reduce(f32[16,256]{1,0:T(8,128)} %get-tuple-element.307, f32[1024]{0:T(1024)} %get-tuple-element.308), channel_id=1, replica_groups=mesh['img'=8,'seq'=4] {'img','seq'}, use_global_device_ids=true, to_apply=%region_51.52 | all-reduce | flops 5120 | bytes 40960 | tf_op jit(solution)/shard_map/psum | solution.py:409
  1609.4 98.2 %all-reduce.8.cloned.1.call-done = (f32[256,768]{1,0:T(8,128)}, f32[256,256]{1,0:T(8,128)}, f32[256,1024]{1,0:T(8,128)}, f32[1024,256]{1,0:T(8,128)}) async-done(((f32[256,768]{1,0:T(8,128)}, f32[256,256]{1,0:T(8,128)}, f32[256,1024]{1,0:T(8,128)}, f32[1024,256]{1,0:T(8,128)}), (f32[256,768]{1,0:T(8,128)}, f32[256,256]{1,0:T(8,128)}, f32[256,1024]{1,0:T(8,128)}, ...) | async-done | bytes 3145744 | tf_op jit(solution)/shard_map/psum | solution.py:409
  (1587 shorter events, 991.4 us)
Async XLA Ops:
  7.2 1700.3 %all-reduce.8.cloned.1.call-start = ((), (), s32[]{:S(2)}) async-start(), calls=%async_computation.4 | async-start | bytes 6291456 | tf_op jit(solution)/shard_map/psum | solution.py:409
  73.2 128.7 %copy-start = (f32[1,7,224,256]{3,2,1,0:T(8,128)}, f32[1,7,224,256]{3,2,1,0:T(8,128)S(1)}, u32[]{:S(2)}) copy-start(f32[1,7,224,256]{3,2,1,0:T(8,128)S(1)} %dynamic-slice_convert_fusion.2) | copy-start | bytes 4816900 | tf_op jit(solution)/shard_map/while
  73.8 124.4 %copy-start.60 = (f32[1,256]{1,0:T(1,128)}, f32[1,256]{1,0:T(1,128)S(1)}, u32[]{:S(2)}) copy-start(f32[1,256]{1,0:T(1,128)S(1)} %get-tuple-element.752) | copy-start | bytes 3076 | tf_op jit(solution)/shard_map/while
  80.2 52.4 %all-to-all-start = ((bf16[7,224,384]{2,0,1:T(8,128)(2,1)}), bf16[7,224,384]{2,0,1:T(8,128)(2,1)}, u32[]{:S(2)}, u32[]{:S(2)}) async-start(bf16[7,224,384]{2,0,1:T(8,128)(2,1)} %copy.252), calls=%async_computation | async-start | bytes 2752512 | tf_op jit(solution)/shard_map/while/body/eval_jaxpr/all_to_all | solution.py:211
  186.4 14.5 all-to-all-start.1
  340.7 28.1 %all-to-all-start.2 = ((bf16[7,224,128]{2,0,1:T(8,128)(2,1)}), bf16[7,224,128]{2,0,1:T(8,128)(2,1)}, u32[]{:S(2)}, u32[]{:S(2)}) async-start(bf16[7,224,128]{2,0,1:T(8,128)(2,1)} %copy.263), calls=%async_computation.2 | async-start | bytes 917504 | tf_op jit(solution)/shard_map/while/body/eval_jaxpr/all_to_all | solution.py:311
  414.8 14.8 all-to-all-start.3
  447.3 128.4 %copy-start = (f32[1,7,224,256]{3,2,1,0:T(8,128)}, f32[1,7,224,256]{3,2,1,0:T(8,128)S(1)}, u32[]{:S(2)}) copy-start(f32[1,7,224,256]{3,2,1,0:T(8,128)S(1)} %dynamic-slice_convert_fusion.2) | copy-start | bytes 4816900 | tf_op jit(solution)/shard_map/while
  447.9 124.1 %copy-start.60 = (f32[1,256]{1,0:T(1,128)}, f32[1,256]{1,0:T(1,128)S(1)}, u32[]{:S(2)}) copy-start(f32[1,256]{1,0:T(1,128)S(1)} %get-tuple-element.752) | copy-start | bytes 3076 | tf_op jit(solution)/shard_map/while
  454.2 52.3 %all-to-all-start = ((bf16[7,224,384]{2,0,1:T(8,128)(2,1)}), bf16[7,224,384]{2,0,1:T(8,128)(2,1)}, u32[]{:S(2)}, u32[]{:S(2)}) async-start(bf16[7,224,384]{2,0,1:T(8,128)(2,1)} %copy.252), calls=%async_computation | async-start | bytes 2752512 | tf_op jit(solution)/shard_map/while/body/eval_jaxpr/all_to_all | solution.py:211
  560.1 14.4 all-to-all-start.1
  714.4 28.1 %all-to-all-start.2 = ((bf16[7,224,128]{2,0,1:T(8,128)(2,1)}), bf16[7,224,128]{2,0,1:T(8,128)(2,1)}, u32[]{:S(2)}, u32[]{:S(2)}) async-start(bf16[7,224,128]{2,0,1:T(8,128)(2,1)} %copy.263), calls=%async_computation.2 | async-start | bytes 917504 | tf_op jit(solution)/shard_map/while/body/eval_jaxpr/all_to_all | solution.py:311
  788.6 14.8 all-to-all-start.3
  821.0 128.4 %copy-start = (f32[1,7,224,256]{3,2,1,0:T(8,128)}, f32[1,7,224,256]{3,2,1,0:T(8,128)S(1)}, u32[]{:S(2)}) copy-start(f32[1,7,224,256]{3,2,1,0:T(8,128)S(1)} %dynamic-slice_convert_fusion.2) | copy-start | bytes 4816900 | tf_op jit(solution)/shard_map/while
  821.7 124.1 %copy-start.60 = (f32[1,256]{1,0:T(1,128)}, f32[1,256]{1,0:T(1,128)S(1)}, u32[]{:S(2)}) copy-start(f32[1,256]{1,0:T(1,128)S(1)} %get-tuple-element.752) | copy-start | bytes 3076 | tf_op jit(solution)/shard_map/while
  828.0 52.3 %all-to-all-start = ((bf16[7,224,384]{2,0,1:T(8,128)(2,1)}), bf16[7,224,384]{2,0,1:T(8,128)(2,1)}, u32[]{:S(2)}, u32[]{:S(2)}) async-start(bf16[7,224,384]{2,0,1:T(8,128)(2,1)} %copy.252), calls=%async_computation | async-start | bytes 2752512 | tf_op jit(solution)/shard_map/while/body/eval_jaxpr/all_to_all | solution.py:211
  933.9 14.4 all-to-all-start.1
  1088.1 28.1 %all-to-all-start.2 = ((bf16[7,224,128]{2,0,1:T(8,128)(2,1)}), bf16[7,224,128]{2,0,1:T(8,128)(2,1)}, u32[]{:S(2)}, u32[]{:S(2)}) async-start(bf16[7,224,128]{2,0,1:T(8,128)(2,1)} %copy.263), calls=%async_computation.2 | async-start | bytes 917504 | tf_op jit(solution)/shard_map/while/body/eval_jaxpr/all_to_all | solution.py:311
  1162.3 14.8 all-to-all-start.3
  1194.8 128.4 %copy-start = (f32[1,7,224,256]{3,2,1,0:T(8,128)}, f32[1,7,224,256]{3,2,1,0:T(8,128)S(1)}, u32[]{:S(2)}) copy-start(f32[1,7,224,256]{3,2,1,0:T(8,128)S(1)} %dynamic-slice_convert_fusion.2) | copy-start | bytes 4816900 | tf_op jit(solution)/shard_map/while
  1195.4 124.1 %copy-start.60 = (f32[1,256]{1,0:T(1,128)}, f32[1,256]{1,0:T(1,128)S(1)}, u32[]{:S(2)}) copy-start(f32[1,256]{1,0:T(1,128)S(1)} %get-tuple-element.752) | copy-start | bytes 3076 | tf_op jit(solution)/shard_map/while
  1201.7 52.3 %all-to-all-start = ((bf16[7,224,384]{2,0,1:T(8,128)(2,1)}), bf16[7,224,384]{2,0,1:T(8,128)(2,1)}, u32[]{:S(2)}, u32[]{:S(2)}) async-start(bf16[7,224,384]{2,0,1:T(8,128)(2,1)} %copy.252), calls=%async_computation | async-start | bytes 2752512 | tf_op jit(solution)/shard_map/while/body/eval_jaxpr/all_to_all | solution.py:211
  1307.6 14.4 all-to-all-start.1
  1461.9 28.1 %all-to-all-start.2 = ((bf16[7,224,128]{2,0,1:T(8,128)(2,1)}), bf16[7,224,128]{2,0,1:T(8,128)(2,1)}, u32[]{:S(2)}, u32[]{:S(2)}) async-start(bf16[7,224,128]{2,0,1:T(8,128)(2,1)} %copy.263), calls=%async_computation.2 | async-start | bytes 917504 | tf_op jit(solution)/shard_map/while/body/eval_jaxpr/all_to_all | solution.py:311
  1536.1 14.8 all-to-all-start.3
  1568.0 151.4 %copy-start.51 = (f32[64,1024]{1,0:T(8,128)S(1)}, f32[64,1024]{1,0:T(8,128)}, u32[]{:S(2)}) copy-start(f32[64,1024]{1,0:T(8,128)} %param.28) | copy-start | bytes 786436
  1568.0 151.4 %copy-start.64 = (f32[64,1024]{1,0:T(8,128)S(1)}, f32[64,1024]{1,0:T(8,128)}, u32[]{:S(2)}) copy-start(f32[64,1024]{1,0:T(8,128)} %param.40) | copy-start | bytes 786436
  1568.0 151.4 %copy-start.65 = (f32[64,1024]{1,0:T(8,128)S(1)}, f32[64,1024]{1,0:T(8,128)}, u32[]{:S(2)}) copy-start(f32[64,1024]{1,0:T(8,128)} %param.34) | copy-start | bytes 786436
  1568.1 153.4 %copy-start.55 = (f32[64,768]{1,0:T(8,128)S(1)}, f32[64,768]{1,0:T(8,128)}, u32[]{:S(2)}) copy-start(f32[64,768]{1,0:T(8,128)} %param.26) | copy-start | bytes 589828
  1568.1 153.4 %copy-start.71 = (f32[64,768]{1,0:T(8,128)S(1)}, f32[64,768]{1,0:T(8,128)}, u32[]{:S(2)}) copy-start(f32[64,768]{1,0:T(8,128)} %param.38) | copy-start | bytes 589828
  1568.1 153.4 %copy-start.72 = (f32[64,768]{1,0:T(8,128)S(1)}, f32[64,768]{1,0:T(8,128)}, u32[]{:S(2)}) copy-start(f32[64,768]{1,0:T(8,128)} %param.32) | copy-start | bytes 589828
  1608.1 115.1 %copy-start.120 = (f32[64,256]{1,0:T(8,128)S(1)}, f32[64,256]{1,0:T(8,128)}, u32[]{:S(2)}) copy-start(f32[64,256]{1,0:T(8,128)} %param.33) | copy-start | bytes 196612
  (515 other events, 4827.9 us)
Sparse Core Ops, SparseCore 0:
  1568.2 139.3 all-reduce.7
where the time goes:
time: 1750 us; the launch traced here: 1740 us
  matrix products  684 us (39%)
  other arithmetic  379 us (22%)
  local copies, waits for them, and re-layouts  365 us (21%)
  waiting for transfers between devices  110 us (6%)
  blocking collectives  97.1 us (6%)
  starting transfers between devices  71.8 us (4%)
  between operations  19.6 us (1%)
    convert_element_type x8, other arithmetic, attend_backward(): grad_scores = (weights * (grad_weights - inner_sum)).astype(jnp.bfloat16)  151 us
    dot_general x8, matrix products, attend_backward(): jnp.einsum('wqhd,wkhd->whqk', grad_out, value_part, preferred_element_typ...  134 us
    psum x1, waiting for transfers between devices, on_device(): lax.psum((sum_qkv, sum_out, sum_expand, sum_shrink, sum_small, sum_bias),...  98.2 us
    dot_general x8, matrix products, attend_backward(): jnp.einsum('whqk,wqhd->wkhd', weights_low, grad_out, preferred_element_ty...  86.8 us
    dot_general x8, matrix products, attend_forward(): jnp.einsum('whqk,wkhd->wqhd', weights_low, value_part, preferred_element_...  83 us
    sub x4, matrix products, attend_backward(): weights = jnp.exp(scores - highest) / totals  76.1 us
    dot_general x4, matrix products, micro_batch(): jnp.dot(normed_two_low, expand_low, preferred_element_type=jnp.float32)  65.9 us
    while x1048, local copies, waits for them, and re-layouts  62.4 us
  transfers between devices with their start and end apart: 17, of which 5 were waited for; matrix products, arithmetic and copies ran while one was open for 20% of the time, Pallas kernels for 0%

commit v1 on v0

v1 whole, which is shorter than its diff:
```python
import functools

import jax
import jax.numpy as jnp
from jax import lax
from jax.experimental import pallas as pl
from jax.experimental.pallas import tpu as pltpu
from jax.sharding import PartitionSpec as P

HEADS = 8
STRIPE = 7
STEP = 10
VALID = 168

EPS_NORM = 1e-05
BETA_ONE = 0.9
BETA_TWO = 0.999
ADAM_EPS = 1e-08
WEIGHT_DECAY = 0.05
CLIP_NORM = 1.0
RATE_MATRIX = 0.1
RATE_OUTPUT = 0.5
RATE_SMALL = 0.3
INV_ROOT_TWO = 0.7071067811865476
INV_ROOT_TAU = 0.3989422804014327
LOG2E = 1.4426950408889634

BF = jnp.bfloat16
F32 = jnp.float32
HALF = 128
BRANCH_HEADS = 4
HEAD_DIM = 32
SCALE = HEAD_DIM**-0.5
GROUP = 8
MASKED = -1e38
EXPONENT_BOUND = 60.0
VMEM_LIMIT = 60 * 2**20


def dot(left, right):
    return jnp.dot(left, right, preferred_element_type=F32)


def dot_nt(left, right):
    return lax.dot_general(left, right, (((1,), (1,)), ((), ())), preferred_element_type=F32)


def dot_tn(left, right):
    return lax.dot_general(left, right, (((0,), (0,)), ((), ())), preferred_element_type=F32)


def iota(shape, dim):
    return lax.broadcasted_iota(jnp.int32, shape, dim)


def one_hot(condition):
    return jnp.where(condition, 1.0, 0.0).astype(BF)


def expand_condition(wide, width):
    e, c = iota((wide, width), 0), iota((wide, width), 1)
    return ((e & 7) < STRIPE) & (c == STRIPE * (e >> 3) + (e & 7))


def contract_matrix(width, wide):
    c, e = iota((width, wide), 0), iota((width, wide), 1)
    return one_hot(((e & 7) < STRIPE) & (c == STRIPE * (e >> 3) + (e & 7)))


def normalize(values, gain_row, offset_row):
    center = values - jnp.mean(values, axis=-1, keepdims=True)
    spread = jnp.mean(center * center, axis=-1, keepdims=True)
    recip = lax.rsqrt(spread + EPS_NORM)
    scaled = center * recip
    return scaled * gain_row + offset_row, scaled, recip


def normalize_back(grad_out, scaled, recip, gain_row):
    grad_scaled = grad_out * gain_row
    inner_one = jnp.mean(grad_scaled, axis=-1, keepdims=True)
    inner_two = jnp.mean(grad_scaled * scaled, axis=-1, keepdims=True)
    return recip * (grad_scaled - inner_one - scaled * inner_two)


def fold_rows(values):
    rows, columns = values.shape
    return jnp.sum(values.reshape(rows // 8, 8, columns), axis=0)


def pieces_of(values):
    first = values.astype(BF).astype(F32)
    rest = values - first
    second = rest.astype(BF).astype(F32)
    return first, second, (rest - second).astype(BF).astype(F32)


def lane_place(rows, head):
    lane = iota((rows, HALF), 1)
    return ((lane >> 5) - head) & 3


def lane_sub(rows):
    return iota((rows, HALF), 1) & 31


def head_key(keys, keys_rolled, bias, head):
    rows = keys.shape[0]
    place, sub = lane_place(rows, head), lane_sub(rows)
    extra = jnp.where(sub < 3, 1.0, jnp.where(sub == 3, bias, 0.0))
    return jnp.where(
        place == 0, keys, jnp.where(place == 1, keys_rolled, jnp.where(place == 2, extra, 0.0))
    ).astype(BF)


def head_value(values, head):
    place = lane_place(values.shape[0], head)
    return jnp.where(place == 0, values, jnp.where(place == 1, 1.0, 0.0)).astype(BF)


def query_parts(queries, shift):
    rows = queries.shape[0]
    scaled = queries * (SCALE * LOG2E)
    high = scaled.astype(BF).astype(F32)
    low = pltpu.roll(scaled - high, HEAD_DIM, 1)
    one, two, three = pieces_of(-pltpu.roll(shift, 2 * HEAD_DIM, 1))
    sub = lane_sub(rows)
    extra = jnp.where(
        sub == 0,
        one,
        jnp.where(sub == 1, two, jnp.where(sub == 2, three, jnp.where(sub == 3, 1.0, 0.0))),
    )
    return high, low, extra


def head_query(parts, head):
    high, low, extra = parts
    place = lane_place(high.shape[0], head)
    return jnp.where(
        place == 0, high, jnp.where(place == 1, low, jnp.where(place == 2, extra, 0.0))
    ).astype(BF)


def grad_parts(grad, attended):
    rows = grad.shape[0]
    product = grad * attended
    block = one_hot((iota((HALF, HALF), 0) >> 5) == (iota((HALF, HALF), 1) >> 5))
    first, second, third = pieces_of(product)
    inner = dot(first.astype(BF), block) + dot(second.astype(BF), block) + dot(third.astype(BF), block)
    one, two, three = pieces_of(-pltpu.roll(inner, HEAD_DIM, 1))
    sub = lane_sub(rows)
    extra = jnp.where(sub == 0, one, jnp.where(sub == 1, two, jnp.where(sub == 2, three, 0.0)))
    return grad, extra


def head_grad(parts, head):
    grad, extra = parts
    place = lane_place(grad.shape[0], head)
    return jnp.where(place == 0, grad, jnp.where(place == 1, extra, 0.0)).astype(BF)


def head_norms(values):
    block = one_hot((iota((HALF, HALF), 0) >> 5) == (iota((HALF, HALF), 1) >> 5))
    sums = dot((values * values * 1.02).astype(BF), block)
    return jnp.max(sums, axis=0, keepdims=True)


def exceeds(query_norms, key_norms):
    bound = jnp.max(query_norms * key_norms)
    return jnp.logical_not(bound <= EXPONENT_BOUND * EXPONENT_BOUND)


def attend_heads(query_rows, shift, keys_of, values_of):
    rows = query_rows.shape[0]
    parts = query_parts(query_rows, shift)
    attended = jnp.zeros((rows, HALF), F32)
    log_total = jnp.zeros((rows, HALF), F32)
    for head in range(BRANCH_HEADS):
        scores = dot_nt(head_query(parts, head), keys_of(head))
        weights = jnp.exp2(scores).astype(BF)
        result = dot(weights, values_of(head))
        totals = pltpu.roll(result, HALF - HEAD_DIM, 1)
        mine = lane_place(rows, head) == 0
        attended = jnp.where(mine, result / totals, attended)
        log_total = jnp.where(mine, jnp.log(totals) * LOG2E + shift, log_total)
    return attended, log_total


def highest_scores(query_rows, keys_of):
    rows = query_rows.shape[0]
    parts = query_parts(query_rows, jnp.zeros((rows, HALF), F32))
    shift = jnp.zeros((rows, HALF), F32)
    for head in range(BRANCH_HEADS):
        scores = dot_nt(head_query(parts, head), keys_of(head))
        highest = jnp.max(scores, axis=-1, keepdims=True)
        shift = jnp.where(lane_place(rows, head) == 0, highest, shift)
    return shift


def attend_heads_back(query_rows, grad_rows, attended, log_total, keys_of, values_of):
    rows = query_rows.shape[0]
    eye = one_hot(iota((HALF, HALF), 0) == iota((HALF, HALF), 1))
    query_turned = dot_nt(eye, query_rows.astype(BF)).astype(BF)
    grad_turned = dot_nt(eye, grad_rows.astype(BF)).astype(BF)
    parts = query_parts(query_rows, log_total)
    back_parts = grad_parts(grad_rows, attended)
    grad_queries = jnp.zeros((rows, HALF), F32)
    grad_keys, grad_values = [], []
    for head in range(BRANCH_HEADS):
        keys, values = keys_of(head), values_of(head)
        weights = jnp.exp2(dot_nt(head_query(parts, head), keys))
        weights_low = weights.astype(BF)
        grad_weights = dot_nt(head_grad(back_parts, head), values)
        grad_scores = (weights * grad_weights).astype(BF)
        lanes = slice(head * HEAD_DIM, (head + 1) * HEAD_DIM)
        grad_values.append(dot(grad_turned[lanes], weights_low))
        grad_keys.append(dot(query_turned[lanes], grad_scores))
        mine = lane_place(rows, head) == 0
        grad_queries = jnp.where(mine, dot(grad_scores, keys), grad_queries)
    return grad_queries * SCALE, grad_keys, grad_values


def shift_down(values):
    rows = values.shape[0]
    return jnp.where(iota(values.shape, 0) == 0, 0.0, pltpu.roll(values, 1, 0))


def shift_up(values):
    rows = values.shape[0]
    return jnp.where(iota(values.shape, 0) == rows - 1, 0.0, pltpu.roll(values, rows - 1, 0))


def project_kernel(dims, ways, *refs):
    rows, width, wide, wide_part = dims
    me_ref, x_ref, small_ref, weight_ref, across_ref = refs[:5]
    down_refs = refs[5 : 5 + ways]
    down_ref = refs[5 + ways]
    gain, offset = small_ref[9:10], small_ref[10:11]
    expand = one_hot(expand_condition(wide, width))
    for row in range(rows):
        span = slice(row * width, (row + 1) * width)
        normed, _, _ = normalize(x_ref[0, span].astype(F32), gain, offset)
        normed = normed.astype(BF)
        across_ref[0, span] = dot(normed, weight_ref[:, : 3 * HALF]).astype(BF)
        spread = dot(expand, normed).astype(BF)
        down = dot(spread, weight_ref[:, 3 * HALF :]).astype(BF)
        down_ref[row] = down
        for distance in range(ways):
            start = pl.multiple_of((me_ref[0] ^ distance) * wide_part, wide_part)
            down_refs[distance][0, row] = down_ref[row, pl.ds(start, wide_part)]


def rank_row(mask_row, width):
    lower = one_hot(iota((width, width), 0) <= iota((width, width), 1))
    counted = dot(jnp.broadcast_to(mask_row, (8, width)).astype(BF), lower)[0:1]
    return jnp.where(mask_row > 0.0, counted - 1.0, -1.0)


def across_kernel(
    dims,
    across_ref,
    mask_ref,
    small_ref,
    joined_ref,
    attended_ref,
    total_ref,
    keys_ref,
    values_ref,
    shift_ref,
):
    rows, width, kept, key_rows, chunk = dims
    tokens = rows * width
    image = pl.program_id(0)
    ranks = rank_row(mask_ref[pl.ds(image, 1)].astype(F32), width)
    select = one_hot(iota((kept, width), 0).astype(F32) == ranks)
    bias = jnp.where(iota((kept, HALF), 0) >= VALID, MASKED, 0.0)
    key_norms = jnp.zeros((1, HALF), F32)
    for row in range(rows):
        picked = dot(select, across_ref[0, row * width : (row + 1) * width, HALF:])
        keys, values = picked[:, :HALF], picked[:, HALF:]
        rolled = pltpu.roll(keys, HEAD_DIM, 1)
        key_norms = jnp.maximum(key_norms, head_norms(keys))
        span = slice(row * kept, (row + 1) * kept)
        for head in range(BRANCH_HEADS):
            keys_ref[0, head, span] = head_key(keys, rolled, bias, head)
            values_ref[0, head, span] = head_value(values, head)
    spare = key_rows - rows * kept
    if spare:
        nothing = jnp.zeros((spare, HALF), F32)
        for head in range(BRANCH_HEADS):
            keys_ref[0, head, rows * kept :] = head_key(
                nothing, nothing, jnp.full((spare, HALF), MASKED, F32), head
            )
            values_ref[0, head, rows * kept :] = nothing.astype(BF)

    query_norms = head_norms(across_ref[0, :, :HALF].astype(F32) * (SCALE * LOG2E))
    large = exceeds(query_norms, key_norms)

    @pl.when(image == 0)
    def _():
        shift_ref[...] = jnp.zeros_like(shift_ref)

    def rows_of(step):
        return pl.ds(pl.multiple_of(step * chunk, 16), chunk)

    def keys_of(head):
        return keys_ref[0, head]

    def values_of(head):
        return values_ref[0, head]

    @pl.when(large)
    def _():
        def highest(step, carry):
            span = rows_of(step)
            shift_ref[span] = highest_scores(across_ref[0, span, :HALF].astype(F32), keys_of)
            return carry

        lax.fori_loop(0, tokens // chunk, highest, 0)

    def attend(step, carry):
        span = rows_of(step)
        attended, log_total = attend_heads(
            across_ref[0, span, :HALF].astype(F32), shift_ref[span], keys_of, values_of
        )
        attended_ref[0, span] = attended
        total_ref[0, span] = log_total
        return carry

    lax.fori_loop(0, tokens // chunk, attend, 0)

    @pl.when(large)
    def _():
        shift_ref[...] = jnp.zeros_like(shift_ref)

    def value_row(row):
        return across_ref[0, row * width : (row + 1) * width, 2 * HALF :].astype(F32)

    for row in range(rows):
        sums = [jnp.zeros((width, HALF), F32) for _ in range(3)]
        for tap_row in range(3):
            source = row + tap_row - 1
            if 0 <= source < rows:
                values = value_row(source)
                for tap_col in range(3):
                    tap = 3 * tap_row + tap_col
                    sums[tap_col] = sums[tap_col] + values * small_ref[tap : tap + 1, :HALF]
        local = shift_down(sums[0]) + sums[1] + shift_up(sums[2]) + small_ref[11:12, :HALF]
        span = slice(row * width, (row + 1) * width)
        joined_ref[0, span] = (attended_ref[0, span] + local).astype(BF)


def assemble(me_ref, pieces, target_ref, dim, step):
    for distance, piece in enumerate(pieces):
        place = me_ref[0] ^ distance
        if dim == 0:
            target_ref[pl.ds(place * step, step)] = piece[0].astype(target_ref.dtype)
        else:
            target_ref[:, pl.ds(pl.multiple_of(place * step, step), step)] = piece[0].astype(
                target_ref.dtype
            )


def down_setup(me_ref, mask_ref, column_ref, width, wide, wide_part):
    image = pl.program_id(0)
    mask_row = mask_ref[pl.ds(image, 1)].astype(F32)
    valid = one_hot(expand_condition(wide, width) & (mask_row > 0.0))
    column_ref[...] = dot(valid, jnp.ones((width, HALF), BF))
    return pl.multiple_of(me_ref[0] * wide_part, GROUP)


def window_bias(column_ref, start, window, height):
    valid = column_ref[pl.ds(start + pl.multiple_of(window * GROUP, GROUP), GROUP)]
    bias = jnp.where(valid > 0.5, 0.0, MASKED)
    return jnp.broadcast_to(bias[None], (height, GROUP, HALF)).reshape(height * GROUP, HALF)


def pad_keys(block, spare, fill):
    if not spare:
        return block
    return jnp.concatenate([block, jnp.full((spare, HALF), 0.0, F32) + fill], axis=0)


def window_operands(keys, values, bias, spare):
    rolled = pltpu.roll(keys, HEAD_DIM, 1)
    keys_in = pad_keys(keys, spare, 0.0)
    rolled_in = pad_keys(rolled, spare, 0.0)
    bias_in = pad_keys(bias, spare, MASKED)
    values_in = pad_keys(values, spare, 0.0)
    key_list = [head_key(keys_in, rolled_in, bias_in, head) for head in range(BRANCH_HEADS)]
    value_list = [head_value(values_in, head) for head in range(BRANCH_HEADS)]
    return key_list, value_list


def grid_shift(values, amount):
    return pltpu.roll(values, amount % GROUP, 1)


def grid_stack(values):
    edge = jnp.zeros((1,) + values.shape[1:], F32)
    return jnp.concatenate([edge, values, edge], axis=0)


def down_kernel(dims, ways, *refs):
    height, width, wide, wide_part, spare = dims
    me_ref, mask_ref, small_ref = refs[:3]
    pieces_in = refs[3 : 3 + ways]
    joined_refs = refs[3 + ways : 3 + 2 * ways]
    attended_ref, total_ref, mixed_ref, joined_ref, column_ref, shift_ref = refs[3 + 2 * ways :]
    rows = height // ways
    start = down_setup(me_ref, mask_ref, column_ref, width, wide, wide_part)
    assemble(me_ref, pieces_in, mixed_ref, 0, rows)
    tokens = height * GROUP
    windows = wide_part // GROUP

    @pl.when(pl.program_id(0) == 0)
    def _():
        shift_ref[...] = jnp.zeros_like(shift_ref)

    everything = mixed_ref[...].reshape(height * wide_part, 3 * HALF)
    large = exceeds(
        head_norms(everything[:, :HALF] * (SCALE * LOG2E)), head_norms(everything[:, HALF : 2 * HALF])
    )

    def one_window(window, carry):
        span = pl.ds(pl.multiple_of(window * GROUP, GROUP), GROUP)
        grid = mixed_ref[:, span]
        flat = grid.reshape(tokens, 3 * HALF)
        queries, keys, values = (flat[:, part * HALF : (part + 1) * HALF] for part in range(3))
        bias = window_bias(column_ref, start, window, height)
        key_list, value_list = window_operands(keys, values, bias, spare)

        @pl.when(large)
        def _():
            shift_ref[...] = highest_scores(queries, lambda head: key_list[head])

        attended, log_total = attend_heads(
            queries, shift_ref[...], lambda head: key_list[head], lambda head: value_list[head]
        )
        attended_ref[0, :, span] = attended.reshape(height, GROUP, HALF)
        total_ref[0, :, span] = log_total.reshape(height, GROUP, HALF)
        stacked = grid_stack(values.reshape(height, GROUP, HALF))
        sums = [jnp.zeros((height, GROUP, HALF), F32) for _ in range(3)]
        for tap_row in range(3):
            for tap_col in range(3):
                tap = 3 * tap_row + tap_col
                sums[tap_col] = sums[tap_col] + stacked[tap_row : tap_row + height] * small_ref[
                    tap : tap + 1, HALF:
                ].reshape(1, 1, HALF)
        local = grid_shift(sums[0], 1) + sums[1] + grid_shift(sums[2], -1)
        local = local + small_ref[11:12, HALF:].reshape(1, 1, HALF)
        joined_ref[:, span] = attended.reshape(height, GROUP, HALF) + local
        return carry

    lax.fori_loop(0, windows, one_window, 0)

    @pl.when(large)
    def _():
        shift_ref[...] = jnp.zeros_like(shift_ref)

    for distance in range(ways):
        place = me_ref[0] ^ distance
        joined_refs[distance][0] = joined_ref[pl.ds(place * rows, rows)].astype(BF)


def gelu_parts(hidden):
    size = jnp.abs(hidden) * INV_ROOT_TWO
    ratio = 1.0 / (1.0 + 0.3275911 * size)
    poly = ratio * (
        0.127414796
        + ratio * (-0.142248368 + ratio * (0.7107068705 + ratio * (-0.7265760135 + ratio * 0.5307027145)))
    )
    decay = jnp.exp2(hidden * hidden * (-0.5 * LOG2E))
    tail = poly * decay
    return jnp.where(hidden >= 0.0, 1.0 - tail, tail), decay * INV_ROOT_TAU


def middle_kernel(dims, ways, *refs):
    rows, width, wide, wide_part, chunk, hidden_part = dims
    me_ref, x_ref, cot_ref, across_ref = refs[:4]
    pieces_in = refs[4 : 4 + ways]
    out_ref, expand_ref, shrink_ref, small_ref, bias_ref = refs[4 + ways : 9 + ways]
    block_ref, middle_ref, grad_across_ref = refs[9 + ways : 12 + ways]
    grad_refs = refs[12 + ways : 12 + 2 * ways]
    dout_ref, dexpand_ref, dshrink_ref, dbias_ref, dsmall_ref = refs[12 + 2 * ways : 17 + 2 * ways]
    wide_ref, joined_ref, normed_ref, active_ref, hidden_ref, attended_ref, down_ref, gwide_ref = refs[
        17 + 2 * ways :
    ]
    tokens = rows * width
    hidden_width = expand_ref.shape[1]

    @pl.when(pl.program_id(0) == 0)
    def _():
        for ref in (dout_ref, dexpand_ref, dshrink_ref, dbias_ref, dsmall_ref):
            ref[...] = jnp.zeros_like(ref)

    assemble(me_ref, pieces_in, wide_ref, 1, wide_part)
    contract = contract_matrix(width, wide)
    for row in range(rows):
        span = slice(row * width, (row + 1) * width)
        joined_ref[span, :HALF] = across_ref[0, span]
        joined_ref[span, HALF:] = dot(contract, wide_ref[row]).astype(BF)

    def token_rows(step, carry):
        span = pl.ds(pl.multiple_of(step * chunk, 16), chunk)
        joined = joined_ref[span]
        attended_out = dot(joined, out_ref[...]) + small_ref[12:13]
        middle = x_ref[0, span].astype(F32) + attended_out
        normed, scaled, recip = normalize(middle, small_ref[13:14], small_ref[14:15])
        normed_low = normed.astype(BF)
        normed_ref[span] = normed_low
        back = cot_ref[0, span]
        result = middle + small_ref[15:16]
        grad_normed = jnp.zeros((chunk, 2 * HALF), F32)
        for part in range(0, hidden_width, hidden_part):
            lanes = slice(part, part + hidden_part)
            hidden = dot(normed_low, expand_ref[:, lanes]) + bias_ref[:, lanes]
            upper, density = gelu_parts(hidden)
            active = (hidden * upper).astype(BF)
            active_ref[span, lanes] = active
            result = result + dot(active, shrink_ref[lanes])
            grad_active = dot_nt(back, shrink_ref[lanes])
            grad_hidden = grad_active * (upper + hidden * density)
            grad_hidden = grad_hidden.astype(BF)
            hidden_ref[span, lanes] = grad_hidden
            dbias_ref[:, lanes] += fold_rows(grad_hidden.astype(F32))
            grad_normed = grad_normed + dot_nt(grad_hidden, expand_ref[:, lanes])
        block_ref[0, span] = result
        back_wide = back.astype(F32)
        grad_middle = back_wide + normalize_back(grad_normed, scaled, recip, small_ref[13:14])
        middle_ref[0, span] = grad_middle
        grad_attended = grad_middle.astype(BF)
        attended_ref[span] = grad_attended
        grad_joined = dot_nt(grad_attended, out_ref[...]).astype(BF)
        grad_across_ref[0, span] = grad_joined[:, :HALF]
        down_ref[span] = grad_joined[:, HALF:]
        dsmall_ref[0:8] += fold_rows(grad_attended.astype(F32))
        dsmall_ref[8:16] += fold_rows(grad_normed * scaled)
        dsmall_ref[16:24] += fold_rows(grad_normed)
        dsmall_ref[24:32] += fold_rows(back_wide)
        return carry

    lax.fori_loop(0, tokens // chunk, token_rows, 0)
    expand = one_hot(expand_condition(wide, width))
    for row in range(rows):
        gwide_ref[row] = dot(expand, down_ref[row * width : (row + 1) * width]).astype(BF)
    for distance in range(ways):
        place = me_ref[0] ^ distance
        grad_refs[distance][0] = gwide_ref[
            :, pl.ds(pl.multiple_of(place * wide_part, wide_part), wide_part)
        ]
    dout_ref[...] += dot_tn(joined_ref[...], attended_ref[...])
    dexpand_ref[...] += dot_tn(normed_ref[...], hidden_ref[...])
    dshrink_ref[...] += dot_tn(cot_ref[0], active_ref[...])


def across_back_kernel(
    dims,
    across_ref,
    grad_ref,
    attended_ref,
    total_ref,
    keys_ref,
    values_ref,
    mask_ref,
    small_ref,
    mixed_ref,
    taps_ref,
    dkeys_ref,
    dvalues_ref,
    local_ref,
):
    rows, width, kept, key_rows, chunk = dims
    tokens = rows * width
    image = pl.program_id(0)

    @pl.when(image == 0)
    def _():
        taps_ref[...] = jnp.zeros_like(taps_ref)

    dkeys_ref[...] = jnp.zeros_like(dkeys_ref)
    dvalues_ref[...] = jnp.zeros_like(dvalues_ref)

    def attend(step, carry):
        span = pl.ds(pl.multiple_of(step * chunk, 16), chunk)
        grad_queries, grad_keys, grad_values = attend_heads_back(
            across_ref[0, span, :HALF].astype(F32),
            grad_ref[0, span].astype(F32),
            attended_ref[0, span],
            total_ref[0, span],
            lambda head: keys_ref[0, head],
            lambda head: values_ref[0, head],
        )
        mixed_ref[0, span, :HALF] = grad_queries.astype(BF)
        for head in range(BRANCH_HEADS):
            lanes = slice(head * HEAD_DIM, (head + 1) * HEAD_DIM)
            dkeys_ref[lanes] += grad_keys[head]
            dvalues_ref[lanes] += grad_values[head]
        return carry

    lax.fori_loop(0, tokens // chunk, attend, 0)

    local_ref[...] = jnp.zeros_like(local_ref)
    for row in range(rows):
        grad = grad_ref[0, row * width : (row + 1) * width].astype(F32)
        taps_ref[72:80] += fold_rows(grad)
        for tap_col, moved in enumerate((shift_up(grad), grad, shift_down(grad))):
            for tap_row in range(3):
                target = row + tap_row - 1
                if 0 <= target < rows:
                    tap = 3 * tap_row + tap_col
                    span = slice(target * width, (target + 1) * width)
                    values = across_ref[0, span, 2 * HALF :].astype(F32)
                    taps_ref[8 * tap : 8 * tap + 8] += fold_rows(values * moved)
                    local_ref[span] += moved * small_ref[tap : tap + 1, :HALF]

    ranks = rank_row(mask_ref[pl.ds(image, 1)].astype(F32), width)
    place = jnp.transpose(jnp.broadcast_to(ranks, (HALF, width)))
    spread = one_hot(iota((width, HALF), 1).astype(F32) == place)
    spread_more = one_hot((iota((width, kept - HALF), 1) + HALF).astype(F32) == place[:, : kept - HALF])
    spread = jnp.concatenate([spread, spread_more], axis=1)
    grad_keys = jnp.transpose(dkeys_ref[...]) * SCALE
    grad_values = jnp.transpose(dvalues_ref[...])
    high = grad_values.astype(BF)
    low = (grad_values - high.astype(F32)).astype(BF)
    grad_keys = grad_keys.astype(BF)
    for row in range(rows):
        span = slice(row * kept, (row + 1) * kept)
        packed = jnp.concatenate([grad_keys[span], high[span], low[span]], axis=1)
        unpacked = dot(spread, packed)
        target = slice(row * width, (row + 1) * width)
        mixed_ref[0, target, HALF : 2 * HALF] = unpacked[:, :HALF].astype(BF)
        whole = unpacked[:, HALF : 2 * HALF] + unpacked[:, 2 * HALF :] + local_ref[target]
        mixed_ref[0, target, 2 * HALF :] = whole.astype(BF)


def down_back_kernel(dims, ways, *refs):
    height, width, wide, wide_part, spare = dims
    me_ref, mask_ref, small_ref, attended_ref, total_ref = refs[:5]
    pieces_in = refs[5 : 5 + ways]
    grads_in = refs[5 + ways : 5 + 2 * ways]
    out_refs = refs[5 + 2 * ways : 5 + 3 * ways]
    taps_ref, mixed_ref, grad_ref, out_ref, column_ref = refs[5 + 3 * ways :]
    rows = height // ways
    start = down_setup(me_ref, mask_ref, column_ref, width, wide, wide_part)
    assemble(me_ref, pieces_in, mixed_ref, 0, rows)
    assemble(me_ref, grads_in, grad_ref, 0, rows)
    tokens = height * GROUP
    windows = wide_part // GROUP

    @pl.when(pl.program_id(0) == 0)
    def _():
        taps_ref[...] = jnp.zeros_like(taps_ref)

    def one_window(window, carry):
        span = pl.ds(pl.multiple_of(window * GROUP, GROUP), GROUP)
        flat = mixed_ref[:, span].reshape(tokens, 3 * HALF)
        queries, keys, values = (flat[:, part * HALF : (part + 1) * HALF] for part in range(3))
        grad_grid = grad_ref[:, span]
        grad = grad_grid.reshape(tokens, HALF)
        bias = window_bias(column_ref, start, window, height)
        key_list, value_list = window_operands(keys, values, bias, spare)
        grad_queries, grad_keys, grad_values = attend_heads_back(
            queries,
            grad,
            attended_ref[0, :, span].reshape(tokens, HALF),
            total_ref[0, :, span].reshape(tokens, HALF),
            lambda head: key_list[head],
            lambda head: value_list[head],
        )
        grad_keys = jnp.transpose(jnp.concatenate(grad_keys, axis=0))[:tokens] * SCALE
        grad_values = jnp.transpose(jnp.concatenate(grad_values, axis=0))[:tokens]
        values_grid = values.reshape(height, GROUP, HALF)
        local = jnp.zeros((height, GROUP, HALF), F32)
        taps_ref[72:80] += jnp.sum(grad_grid, axis=0)
        shifted = (grid_shift(grad_grid, -1), grad_grid, grid_shift(grad_grid, 1))
        for tap_col, moved in enumerate(shifted):
            stacked = grid_stack(moved)
            for tap_row in range(3):
                tap = 3 * tap_row + tap_col
                source = stacked[2 - tap_row : 2 - tap_row + height]
                taps_ref[8 * tap : 8 * tap + 8] += jnp.sum(source * values_grid, axis=0)
                local = local + source * small_ref[tap : tap + 1, HALF:].reshape(1, 1, HALF)
        shape = (height, GROUP, HALF)
        out_ref[:, span, :HALF] = grad_queries.reshape(shape)
        out_ref[:, span, HALF : 2 * HALF] = grad_keys.reshape(shape)
        out_ref[:, span, 2 * HALF :] = grad_values.reshape(shape) + local
        return carry

    lax.fori_loop(0, windows, one_window, 0)
    for distance in range(ways):
        place = me_ref[0] ^ distance
        out_refs[distance][0] = out_ref[pl.ds(place * rows, rows)].astype(BF)


def final_kernel(dims, ways, *refs):
    rows, width, wide, wide_part, chunk = dims
    me_ref, x_ref, middle_ref, across_ref = refs[:4]
    pieces_in = refs[4 : 4 + ways]
    small_ref, weight_ref, grad_ref, dweight_ref, dsmall_ref, wide_ref, mixed_ref, normed_ref = refs[
        4 + ways :
    ]
    tokens = rows * width

    @pl.when(pl.program_id(0) == 0)
    def _():
        dweight_ref[...] = jnp.zeros_like(dweight_ref)
        dsmall_ref[...] = jnp.zeros_like(dsmall_ref)

    assemble(me_ref, pieces_in, wide_ref, 1, wide_part)
    contract = contract_matrix(width, wide)
    for row in range(rows):
        span = slice(row * width, (row + 1) * width)
        mixed_ref[span, : 3 * HALF] = across_ref[0, span]
        mixed_ref[span, 3 * HALF :] = dot(contract, wide_ref[row]).astype(BF)

    def token_rows(step, carry):
        span = pl.ds(pl.multiple_of(step * chunk, 16), chunk)
        normed, scaled, recip = normalize(
            x_ref[0, span].astype(F32), small_ref[9:10], small_ref[10:11]
        )
        normed_ref[span] = normed.astype(BF)
        mixed = mixed_ref[span]
        grad_normed = dot_nt(mixed[:, : 3 * HALF], weight_ref[:, : 3 * HALF])
        grad_down = dot_nt(mixed[:, 3 * HALF :], weight_ref[:, 3 * HALF :])
        grad_normed = grad_normed + grad_down.astype(BF).astype(F32)
        dsmall_ref[0:8] += fold_rows(grad_normed * scaled)
        dsmall_ref[8:16] += fold_rows(grad_normed)
        grad_ref[0, span] = middle_ref[0, span] + normalize_back(
            grad_normed, scaled, recip, small_ref[9:10]
        )
        return carry

    lax.fori_loop(0, tokens // chunk, token_rows, 0)
    dweight_ref[...] += dot_tn(normed_ref[...], mixed_ref[...])


def image_block(*shape):
    return pl.BlockSpec((1,) + shape, lambda image: (image,) + (0,) * len(shape))


def whole_block(*shape):
    return pl.BlockSpec(shape, lambda image: (0,) * len(shape))


def scalar_block():
    return pl.BlockSpec(memory_space=pltpu.SMEM)


def run_kernel(body, images, in_specs, out_specs, out_shapes, scratch, flops, operands):
    return pl.pallas_call(
        body,
        grid=(images,),
        in_specs=in_specs,
        out_specs=out_specs,
        out_shape=out_shapes,
        scratch_shapes=scratch,
        compiler_params=pltpu.CompilerParams(vmem_limit_bytes=VMEM_LIMIT),
        cost_estimate=pl.CostEstimate(
            flops=int(flops), bytes_accessed=int(flops / 300), transcendentals=0
        ),
    )(*operands)


def adam_update(weight, first_old, second_old, grad_value, rate_value, decay_value):
    new_first = BETA_ONE * first_old + (1.0 - BETA_ONE) * grad_value
    new_second = BETA_TWO * second_old + (1.0 - BETA_TWO) * grad_value * grad_value
    first_hat = new_first / (1.0 - BETA_ONE**STEP)
    second_hat = new_second / (1.0 - BETA_TWO**STEP)
    new_weight = weight - rate_value * (
        first_hat / (jnp.sqrt(second_hat) + ADAM_EPS) + decay_value * weight
    )
    return (new_first, new_second, new_weight)


def exchange(pieces, ways):
    received = [pieces[0]]
    for distance in range(1, ways):
        pairs = [(place, place ^ distance) for place in range(ways)]
        received.append(lax.ppermute(pieces[distance], "seq", pairs))
    return received


def on_device(
    images,
    cotangent,
    valid_mask,
    qkv_weight,
    out_weight,
    expand_weight,
    shrink_weight,
    small_params,
    expand_bias,
    first_qkv,
    first_out,
    first_expand,
    first_shrink,
    first_small,
    first_bias,
    second_qkv,
    second_out,
    second_expand,
    second_shrink,
    second_small,
    second_bias,
):
    ways = lax.axis_size("seq")
    owner = lax.axis_index("seq")
    me = owner.astype(jnp.int32).reshape(1)
    count, rows, width, channels = images.shape
    tokens = rows * width
    height = rows * ways
    wide = width // STRIPE * GROUP
    wide_part = wide // ways
    kept = -(-VALID // 16) * 16
    key_rows = -(-rows * kept // 256) * 256
    window_tokens = height * GROUP
    spare = -window_tokens % 128
    hidden_width = expand_weight.shape[1]
    chunk = width

    gathered = (
        lax.all_gather(qkv_weight.astype(BF), "seq", axis=0, tiled=True),
        lax.all_gather(out_weight.astype(BF), "seq", axis=0, tiled=True),
        lax.all_gather(expand_weight.astype(BF), "seq", axis=0, tiled=True),
        lax.all_gather(shrink_weight.astype(BF), "seq", axis=0, tiled=True),
        lax.all_gather(small_params.astype(BF), "seq", axis=1, tiled=True),
        lax.all_gather(expand_bias.astype(BF), "seq", axis=0, tiled=True),
    )
    qkv_low, out_low, expand_low, shrink_low, small_low, bias_low = gathered
    small_full = small_low.astype(F32)
    bias_full = bias_low.astype(F32).reshape(1, hidden_width)
    x = images.reshape(count, tokens, channels)
    cot = cotangent.reshape(count, tokens, channels)

    def shape(dims, dtype):
        return jax.ShapeDtypeStruct(dims, dtype)

    small_spec = whole_block(*small_full.shape)
    mask_spec = whole_block(*valid_mask.shape)
    piece_qkv = (rows, wide_part, 3 * HALF)
    piece_out = (rows, wide_part, HALF)

    across_mixed, *down_pieces = run_kernel(
        functools.partial(project_kernel, (rows, width, wide, wide_part), ways),
        count,
        [scalar_block(), image_block(tokens, channels), small_spec, whole_block(*qkv_low.shape)],
        [image_block(tokens, 3 * HALF)] + [image_block(*piece_qkv)] * ways,
        [shape((count, tokens, 3 * HALF), BF)] + [shape((count,) + piece_qkv, BF)] * ways,
        [pltpu.VMEM((rows, wide, 3 * HALF), BF)],
        2.2 * count * tokens * channels * 6 * HALF,
        (me, x, small_full, qkv_low),
    )
    down_mixed = exchange(down_pieces, ways)

    attention_dims = (rows, width, kept, key_rows, chunk)
    key_shape = (BRANCH_HEADS, key_rows, HALF)
    joined_across, across_attended, across_total, across_keys, across_values = run_kernel(
        functools.partial(across_kernel, attention_dims),
        count,
        [image_block(tokens, 3 * HALF), mask_spec, small_spec],
        [
            image_block(tokens, HALF),
            image_block(tokens, HALF),
            image_block(tokens, HALF),
            image_block(*key_shape),
            image_block(*key_shape),
        ],
        [
            shape((count, tokens, HALF), BF),
            shape((count, tokens, HALF), F32),
            shape((count, tokens, HALF), F32),
            shape((count,) + key_shape, BF),
            shape((count,) + key_shape, BF),
        ],
        [pltpu.VMEM((tokens, HALF), F32)],
        4.0 * count * BRANCH_HEADS * tokens * key_rows * 256,
        (across_mixed, valid_mask, small_full),
    )

    down_dims = (height, width, wide, wide_part, spare)
    grid_f32 = (height, wide_part, HALF)
    down_results = run_kernel(
        functools.partial(down_kernel, down_dims, ways),
        count,
        [scalar_block(), mask_spec, small_spec] + [image_block(*piece_qkv)] * ways,
        [image_block(*piece_out)] * ways + [image_block(*grid_f32)] * 2,
        [shape((count,) + piece_out, BF)] * ways + [shape((count,) + grid_f32, F32)] * 2,
        [
            pltpu.VMEM((height, wide_part, 3 * HALF), F32),
            pltpu.VMEM(grid_f32, F32),
            pltpu.VMEM((wide, HALF), F32),
            pltpu.VMEM((window_tokens, HALF), F32),
        ],
        4.0 * count * wide_part * BRANCH_HEADS * height * (window_tokens + spare) * 256,
        (me, valid_mask, small_full, *down_mixed),
    )
    down_attended, down_total = down_results[ways:]
    joined_down = exchange(down_results[:ways], ways)

    middle_results = run_kernel(
        functools.partial(middle_kernel, (rows, width, wide, wide_part, chunk, 2 * HALF), ways),
        count,
        [
            scalar_block(),
            image_block(tokens, channels),
            image_block(tokens, channels),
            image_block(tokens, HALF),
        ]
        + [image_block(*piece_out)] * ways
        + [
            whole_block(*out_low.shape),
            whole_block(*expand_low.shape),
            whole_block(*shrink_low.shape),
            small_spec,
            whole_block(1, hidden_width),
        ],
        [
            image_block(tokens, channels),
            image_block(tokens, channels),
            image_block(tokens, HALF),
        ]
        + [image_block(*piece_out)] * ways
        + [
            whole_block(channels, channels),
            whole_block(channels, hidden_width),
            whole_block(channels, hidden_width),
            whole_block(8, hidden_width),
            whole_block(32, channels),
        ],
        [
            shape((count, tokens, channels), F32),
            shape((count, tokens, channels), F32),
            shape((count, tokens, HALF), BF),
        ]
        + [shape((count,) + piece_out, BF)] * ways
        + [
            shape((channels, channels), F32),
            shape((channels, hidden_width), F32),
            shape((channels, hidden_width), F32),
            shape((8, hidden_width), F32),
            shape((32, channels), F32),
        ],
        [
            pltpu.VMEM((rows, wide, HALF), BF),
            pltpu.VMEM((tokens, channels), BF),
            pltpu.VMEM((tokens, channels), BF),
            pltpu.VMEM((tokens, hidden_width), BF),
            pltpu.VMEM((tokens, hidden_width), BF),
            pltpu.VMEM((tokens, channels), BF),
            pltpu.VMEM((tokens, HALF), BF),
            pltpu.VMEM((rows, wide, HALF), BF),
        ],
        6.0 * count * tokens * channels * (channels + 2 * hidden_width),
        (me, x, cot, joined_across, *joined_down, out_low, expand_low, shrink_low, small_full, bias_full),
    )
    block_out, grad_middle, grad_across = middle_results[:3]
    sum_out, sum_expand, sum_shrink, bias_part, small_part = middle_results[3 + ways :]
    grad_down = exchange(middle_results[3 : 3 + ways], ways)

    across_mixed_grad, across_taps = run_kernel(
        functools.partial(across_back_kernel, attention_dims),
        count,
        [
            image_block(tokens, 3 * HALF),
            image_block(tokens, HALF),
            image_block(tokens, HALF),
            image_block(tokens, HALF),
            image_block(*key_shape),
            image_block(*key_shape),
            mask_spec,
            small_spec,
        ],
        [image_block(tokens, 3 * HALF), whole_block(80, HALF)],
        [shape((count, tokens, 3 * HALF), BF), shape((80, HALF), F32)],
        [
            pltpu.VMEM((HALF, key_rows), F32),
            pltpu.VMEM((HALF, key_rows), F32),
            pltpu.VMEM((tokens, HALF), F32),
        ],
        10.0 * count * BRANCH_HEADS * tokens * key_rows * 256,
        (
            across_mixed,
            grad_across,
            across_attended,
            across_total,
            across_keys,
            across_values,
            valid_mask,
            small_full,
        ),
    )

    down_back_results = run_kernel(
        functools.partial(down_back_kernel, down_dims, ways),
        count,
        [scalar_block(), mask_spec, small_spec]
        + [image_block(*grid_f32)] * 2
        + [image_block(*piece_qkv)] * ways
        + [image_block(*piece_out)] * ways,
        [image_block(*piece_qkv)] * ways + [whole_block(80, HALF)],
        [shape((count,) + piece_qkv, BF)] * ways + [shape((80, HALF), F32)],
        [
            pltpu.VMEM((height, wide_part, 3 * HALF), F32),
            pltpu.VMEM(grid_f32, F32),
            pltpu.VMEM((height, wide_part, 3 * HALF), F32),
            pltpu.VMEM((wide, HALF), F32),
        ],
        10.0 * count * wide_part * BRANCH_HEADS * height * (window_tokens + spare) * 256,
        (me, valid_mask, small_full, down_attended, down_total, *down_mixed, *grad_down),
    )
    down_taps = down_back_results[ways]
    down_mixed_grad = exchange(down_back_results[:ways], ways)

    input_grad, sum_qkv, norm_part = run_kernel(
        functools.partial(final_kernel, (rows, width, wide, wide_part, chunk), ways),
        count,
        [
            scalar_block(),
            image_block(tokens, channels),
            image_block(tokens, channels),
            image_block(tokens, 3 * HALF),
        ]
        + [image_block(*piece_qkv)] * ways
        + [small_spec, whole_block(*qkv_low.shape)],
        [
            image_block(tokens, channels),
            whole_block(channels, 6 * HALF),
            whole_block(16, channels),
        ],
        [
            shape((count, tokens, channels), F32),
            shape((channels, 6 * HALF), F32),
            shape((16, channels), F32),
        ],
        [
            pltpu.VMEM((rows, wide, 3 * HALF), BF),
            pltpu.VMEM((tokens, 6 * HALF), BF),
            pltpu.VMEM((tokens, channels), BF),
        ],
        4.0 * count * tokens * channels * 6 * HALF,
        (me, x, grad_middle, across_mixed_grad, *down_mixed_grad, small_full, qkv_low),
    )

    taps = jnp.concatenate([across_taps, down_taps], axis=1).reshape(10, 8, channels).sum(axis=1)
    norm_rows = norm_part.reshape(2, 8, channels).sum(axis=1)
    mid_rows = small_part.reshape(4, 8, channels).sum(axis=1)
    sum_small = jnp.concatenate([taps[:9], norm_rows, taps[9:], mid_rows], axis=0)
    sum_bias = bias_part.sum(axis=0)

    params = (qkv_weight, out_weight, expand_weight, shrink_weight, small_params, expand_bias)
    shard_dims = (0, 0, 0, 1, 1, 0)
    full_grads = lax.psum(
        (sum_qkv, sum_out, sum_expand, sum_shrink, sum_small, sum_bias), ("img", "seq")
    )
    squared = jnp.float32(0.0)
    for full_grad in full_grads:
        squared = squared + jnp.sum(full_grad * full_grad)
    sizes = [part.shape[dim] for part, dim in zip(params, shard_dims)]
    sizes[3] = shrink_weight.shape[0]
    shares = [
        lax.dynamic_slice_in_dim(full_grad, owner * size, size, dim)
        for full_grad, size, dim in zip(full_grads, sizes, shard_dims)
    ]
    shares[3] = shares[3].T
    grad_norm = jnp.sqrt(squared)
    factor = CLIP_NORM / jnp.maximum(grad_norm, CLIP_NORM)
    rates = (RATE_MATRIX, RATE_OUTPUT, RATE_MATRIX, RATE_MATRIX, RATE_SMALL, RATE_MATRIX)
    decays = (WEIGHT_DECAY, WEIGHT_DECAY, WEIGHT_DECAY, WEIGHT_DECAY, 0.0, 0.0)
    firsts = (first_qkv, first_out, first_expand, first_shrink, first_small, first_bias)
    seconds = (second_qkv, second_out, second_expand, second_shrink, second_small, second_bias)
    updated = [
        adam_update(
            params[index],
            firsts[index],
            seconds[index],
            shares[index] * factor,
            rates[index],
            decays[index],
        )
        for index in range(6)
    ]
    return (
        block_out.reshape(images.shape),
        input_grad.reshape(images.shape),
        grad_norm,
        *(entry[0] for entry in updated),
        *(entry[1] for entry in updated),
        *(entry[2] for entry in updated),
    )


def solution(mesh):
    sharded = (
        P("seq", None),
        P("seq", None),
        P("seq", None),
        P("seq", None),
        P(None, "seq"),
        P("seq"),
    )
    grid = P("img", "seq", None, None)
    return jax.shard_map(
        on_device,
        mesh=mesh,
        in_specs=(grid, grid, P("img", None)) + sharded * 3,
        out_specs=(grid, grid, P()) + sharded * 3,
        check_vma=False,
    )
```

time: 1750 us -> 676 us (0.39)
  matrix products: 684 us -> 0 us
  other arithmetic: 379 us -> 15.7 us
  local copies, waits for them, and re-layouts: 365 us -> 11.1 us
  Pallas kernels: 0 us -> 350 us
  starting transfers between devices: 71.8 us -> 14.2 us
  waiting for transfers between devices: 110 us -> 162 us
    dot_general x100 -> x0, matrix products: 590 us -> none  [the longest x8 134 us: attend_backward(): jnp.einsum('wqhd,wkhd->whqk', grad_out, value_part, preferred_element_typ...]
    pallas_call x0 -> x7, Pallas kernels: none -> 350 us  [run_kernel(): pl.pallas_call(body, grid=(images,), in_specs=in_specs, out_specs=out_spe...]
    convert_element_type x46 -> x5, other arithmetic: 232 us -> 0.98 us  [the longest x1 0.94 us: on_device(): qkv_weight.astype(BF)]
    reshape x56 -> x0, local copies, waits for them, and re-layouts: 122 us -> none  [the longest x4 29.9 us: micro_batch(): down_grid.reshape(stripes_dev, height * STRIPE, 3, head_count, head_size)]
    sub x8 -> x0, matrix products: 94.1 us -> none  [the longest x4 76.1 us: attend_backward(): weights = jnp.exp(scores - highest) / totals]
    reduce_sum x28 -> x4, other arithmetic: 90.8 us -> 0.08 us  [the longest x1 0.03 us: on_device(): jnp.concatenate([across_taps, down_taps], axis=1).reshape(10, 8, channels)]
    all_to_all x16 -> x0, starting transfers between devices: 71.8 us -> none  [the longest x4 18.4 us: micro_batch(): lax.all_to_all(down_local.reshape(row_count, grid_width, 3 * half_width),...]
    ppermute x0 -> x12, waiting for transfers between devices: none -> 66.2 us  [exchange(): received.append(lax.ppermute(pieces[distance], 'seq', pairs))]
  transfers between devices with their start and end apart: 17 -> 13, of which waited for: 5 -> 5; matrix products, arithmetic and copies ran while one was open for 20% -> 0% of each run, Pallas kernels for 0% -> 22%
where the time goes in v1:
time: 676 us; the launch traced here: 672 us
  Pallas kernels  350 us (52%)
  waiting for transfers between devices  162 us (24%)
  blocking collectives  99.6 us (15%)
  between operations  19.6 us (3%)
  other arithmetic  15.7 us (2%)
  starting transfers between devices  14.2 us (2%)
  local copies, waits for them, and re-layouts  11.1 us (2%)
    pallas_call x7, Pallas kernels, run_kernel(): pl.pallas_call(body, grid=(images,), in_specs=in_specs, out_specs=out_spe...  350 us
    psum x1, waiting for transfers between devices, on_device(): lax.psum((sum_qkv, sum_out, sum_expand, sum_shrink, sum_small, sum_bias),...  95.5 us
    ppermute x12, waiting for transfers between devices, exchange(): received.append(lax.ppermute(pieces[distance], 'seq', pairs))  66.2 us
    psum x1, blocking collectives, on_device(): lax.psum((sum_qkv, sum_out, sum_expand, sum_shrink, sum_small, sum_bias),...  41.3 us
    ppermute x12, starting transfers between devices, exchange(): received.append(lax.ppermute(pieces[distance], 'seq', pairs))  14.1 us
  transfers between devices with their start and end apart: 13, of which 5 were waited for; matrix products, arithmetic and copies ran while one was open for 0% of the time, Pallas kernels for 22%

profile of v1, /device:TPU:0, one launch (start us, length us, event | category | flops | bytes accessed | tf_op | source)
XLA Modules:
  0.0 671.9 jit_solution(8322773393731114537)
XLA Ops:
  7.9 9.6 %all-gather = bf16[4,64,16]{1,2,0:T(8,128)(2,1)S(1)} all-gather(bf16[1,64,16]{1,2,0:T(8,128)(2,1)S(1)} %convert_bitcast_fusion), channel_id=1, replica_groups=mesh['img'=8,'seq'=4] {'seq'}, dimensions={0}, use_global_device_ids=true | all-gather | bytes 10240 | tf_op jit(solution)/shard_map/all_gather | solution.py:826
  19.2 10.4 %all_gather.19.refs_3_.refs_9_ = bf16[256,768]{1,0:T(8,128)(2,1)} all-gather(bf16[64,768]{1,0:T(8,128)(2,1)S(1)} %convert_element_type.24), channel_id=1, replica_groups=mesh['img'=8,'seq'=4] {'seq'}, dimensions={0}, use_global_device_ids=true | all-gather | bytes 491520 | tf_op jit(solution)/shard_map/all_gather | solution.py:822
  29.6 11.8 %shard_map.364 = (bf16[4,1568,384]{2,1,0:T(8,128)(2,1)}, bf16[4,7,64,384]{3,2,1,0:T(8,128)(2,1)}, bf16[4,7,64,384]{3,2,1,0:T(8,128)(2,1)}, bf16[4,7,64,384]{3,2,1,0:T(8,128)(2,1)}, bf16[4,7,64,384]{3,2,1,0:T(8,128)(2,1)}) custom-call(s32[1]{0:T(128)} %bitcast.refs_0_, bf16[4,1568,256]{2,1,0:T(8,128)(2,1)} %bitcast.30, f32[16,256]{1,0:T(8,128)} %bitcast.34, ...), custom_call_target="tpu_custom_call" | custom-call | flops 2712875776 | bytes 9042919 | tf_op jit(solution)/shard_map/pallas_call | solution.py:750
  42.3 1.2 collective-permute-start.1
  43.5 1.4 collective-permute-start.2
  44.9 29.8 %collective-permute-done.refs_4_.refs_6_ = bf16[4,7,64,384]{3,2,1,0:T(8,128)(2,1)S(1)} collective-permute-done((bf16[4,7,64,384]{3,2,1,0:T(8,128)(2,1)}, bf16[4,7,64,384]{3,2,1,0:T(8,128)(2,1)S(1)}, u32[]{:S(2)}, u32[]{:S(2)}) %collective-permute-start) | collective-permute-done | bytes 1376288 | tf_op jit(solution)/shard_map/ppermute | solution.py:779
  74.8 25.2 %collective-permute-done.1.refs_5_.refs_7_ = bf16[4,7,64,384]{3,2,1,0:T(8,128)(2,1)S(1)} collective-permute-done((bf16[4,7,64,384]{3,2,1,0:T(8,128)(2,1)}, bf16[4,7,64,384]{3,2,1,0:T(8,128)(2,1)S(1)}, u32[]{:S(2)}, u32[]{:S(2)}) %collective-permute-start.1) | collective-permute-done | bytes 1376288 | tf_op jit(solution)/shard_map/ppermute | solution.py:779
  100.0 1.1 copy-done.33
  101.1 36.1 %shard_map.366 = (bf16[4,7,64,128]{3,2,1,0:T(8,128)(2,1)}, bf16[4,7,64,128]{3,2,1,0:T(8,128)(2,1)}, bf16[4,7,64,128]{3,2,1,0:T(8,128)(2,1)}, bf16[4,7,64,128]{3,...) custom-call(s32[1]{0:T(128)} %bitcast.refs_0_, s32[4,224]{1,0:T(4,128)} %refs_1_.3, ...), custom_call_target="tpu_custom_call" | custom-call | flops 7516192768 | bytes 25053976 | tf_op jit(solution)/shard_map/pallas_call | solution.py:750
  137.2 1.1 collective-permute-start.3
  139.3 1.5 collective-permute-start.5
  140.8 56.2 %shard_map.365 = (bf16[4,1568,128]{2,1,0:T(8,128)(2,1)}, f32[4,1568,128]{2,1,0:T(8,128)}, f32[4,1568,128]{2,1,0:T(8,128)}, bf16[4,4,1280,128]{3,2,1,0:T(8,128)(2,1)}, bf16[4,4,1280,128]{3,2,1,0:T(8,128)(2,1)}) custom-call(bf16[4,1568,384]{2,1,0:T(8,128)(2,1)} %get-tuple-element.59.across_ref, s32[4,224]{1,0:T(4,128)} %refs_1_.3, f32[16,256]{1,0:T(8,128)} %bitcast.36), custom_call_target="tpu_custom_call" | custom-call | flops 32883343360 | bytes 109611144 | tf_op jit(solution)/shard_map/pallas_call | solution.py:750
  197.1 7.6 %all-gather.1 = bf16[4,1,256]{2,1,0:T(2,128)(2,1)S(1)} all-gather(bf16[1,1,256]{2,1,0:T(2,128)(2,1)S(1)} %reshape.85), channel_id=1, replica_groups=mesh['img'=8,'seq'=4] {'seq'}, dimensions={0}, use_global_device_ids=true | all-gather | bytes 2560 | tf_op jit(solution)/shard_map/all_gather | solution.py:827
  205.3 9.0 %all_gather.20.refs_8_ = bf16[256,256]{1,0:T(8,128)(2,1)} all-gather(bf16[64,256]{1,0:T(8,128)(2,1)S(1)} %convert_element_type.25), channel_id=1, replica_groups=mesh['img'=8,'seq'=4] {'seq'}, dimensions={0}, use_global_device_ids=true | all-gather | bytes 163840 | tf_op jit(solution)/shard_map/all_gather | solution.py:823
  214.3 11.4 %all_gather.21.refs_9_ = bf16[256,1024]{1,0:T(8,128)(2,1)} all-gather(bf16[64,1024]{1,0:T(8,128)(2,1)S(1)} %convert_element_type.26), channel_id=1, replica_groups=mesh['img'=8,'seq'=4] {'seq'}, dimensions={0}, use_global_device_ids=true | all-gather | bytes 655360 | tf_op jit(solution)/shard_map/all_gather | solution.py:824
  225.7 10.3 %all_gather.22.refs_10_ = bf16[1024,256]{1,0:T(8,128)(2,1)} all-gather(bf16[256,256]{1,0:T(8,128)(2,1)S(1)} %convert_element_type.27), channel_id=1, replica_groups=mesh['img'=8,'seq'=4] {'seq'}, dimensions={0}, use_global_device_ids=true | all-gather | bytes 655360 | tf_op jit(solution)/shard_map/all_gather | solution.py:825
  237.1 73.9 %shard_map.367 = (f32[4,1568,256]{2,1,0:T(8,128)}, f32[4,1568,256]{2,1,0:T(8,128)}, bf16[4,1568,128]{2,1,0:T(8,128)(2,1)}, bf16[4,7,64,128]{3,2,1,0:T(8,128)(2,1...) custom-call(s32[1]{0:T(128)} %bitcast.refs_0_, ...), custom_call_target="tpu_custom_call" | custom-call | flops 22196256768 | bytes 73987520 | tf_op jit(solution)/shard_map/pallas_call | solution.py:750
  311.0 1.1 collective-permute-start.6
  313.1 1.5 collective-permute-start.8
  314.6 5.2 collective-permute-done.6.refs_10_
  319.8 5.9 collective-permute-done.7.refs_11_
  326.7 55.8 %shard_map.369 = (bf16[4,7,64,384]{3,2,1,0:T(8,128)(2,1)}, bf16[4,7,64,384]{3,2,1,0:T(8,128)(2,1)}, bf16[4,7,64,384]{3,2,1,0:T(8,128)(2,1)}, bf16[4,7,64,384]{3,2,1,0:T(8,128)(2,1)}, f32[80,128]{1,0:T(8,128)}) custom-call(s32[1]{0:T(128)} %bitcast.refs_0_, s32[4,224]{1,0:T(4,128)} %refs_1_.3, f32[16,256]{1,0:T(8,128)} %bitcast.38, ...), custom_call_target="tpu_custom_call" | custom-call | flops 18790481920 | bytes 62634940 | tf_op jit(solution)/shard_map/pallas_call | solution.py:750
  384.5 1.5 collective-permute-start.11
  386.0 93.7 %shard_map.368 = (bf16[4,1568,384]{2,1,0:T(8,128)(2,1)}, f32[80,128]{1,0:T(8,128)}) custom-call(bf16[4,1568,384]{2,1,0:T(8,128)(2,1)} %get-tuple-element.59.across_ref, bf16[4,1568,128]{2,1,0:T(8,128)(2,1)} %get-tuple-element.71.grad_ref, f32[4,1568,128]{2,1,0:T(8,128)} %get-tuple-element.72.attended_ref, f32[4,1568,128]{2,1,0:T(8,128)} %get-tuple-element.73.total_ref, ...), custom_call_target="tpu_custom_call" | custom-call | flops 82208358400 | bytes 274027872 | tf_op jit(solution)/shard_map/pallas_call | solution.py:750
  481.7 22.5 %shard_map.370 = (f32[4,1568,256]{2,1,0:T(8,128)}, f32[256,768]{1,0:T(8,128)}, f32[16,256]{1,0:T(8,128)}) custom-call(s32[1]{0:T(128)} %bitcast.refs_0_, bf16[4,1568,256]{2,1,0:T(8,128)(2,1)} %bitcast.32, f32[4,1568,256]{2,1,0:T(8,128)} %get-tuple-element.70.refs_2_, bf16[4,1568,384]{2,1,0:T(8,128)(2,1)} %get-tuple-element.76.refs_3_, ...), custom_call_target="tpu_custom_call" | custom-call | flops 4932501504 | bytes 16441671 | tf_op jit(solution)/shard_map/pallas_call | solution.py:750
  506.1 41.3 %all-reduce = (f32[16,256]{1,0:T(8,128)S(1)}, f32[1024]{0:T(1024)S(1)}) all-reduce(f32[16,256]{1,0:T(8,128)S(1)} %pad_maximum_fusion, f32[1024]{0:T(1024)S(1)} %reduce_sum.98), channel_id=1, replica_groups=mesh['img'=8,'seq'=4] {'img','seq'}, use_global_device_ids=true, to_apply=%region_11.0 | all-reduce | flops 5120 | bytes 40960 | tf_op jit(solution)/shard_map/psum | solution.py:1052
  548.6 95.5 %all-reduce.4.cloned.1.call-done = (f32[256,768]{1,0:T(8,128)}, f32[256,256]{1,0:T(8,128)}, f32[256,1024]{1,0:T(8,128)}, f32[256,1024]{1,0:T(8,128)}) async-done(((f32[256,768]{1,0:T(8,128)}, f32[256,256]{1,0:T(8,128)}, f32[256,1024]{1,0:T(8,128)}, f32[256,1024]{1,0:T(8,128)}), (f32[256,768]{1,0:T(8,128)}, f32[256,256]{1,0:T(8,128)}, f32[256,1024]{1,0:T(8,128)}, ...) | async-done | bytes 3145744 | tf_op jit(solution)/shard_map/psum | solution.py:1052
  644.1 2.1 multiply_reduce_fusion.2
  646.2 1.6 multiply_reduce_fusion.3
  654.5 1.9 copy.55
  658.1 1.9 multiply_subtract_fusion.2
  660.0 1.5 multiply_subtract_fusion.3
  (123 shorter events, 21.6 us)
Async XLA Ops:
  7.2 636.9 %all-reduce.4.cloned.1.call-start = ((), (), s32[]{:S(2)}) async-start(), calls=%async_computation | async-start | bytes 6291456 | tf_op jit(solution)/shard_map/psum | solution.py:1052
  41.4 33.3 %collective-permute-start = (bf16[4,7,64,384]{3,2,1,0:T(8,128)(2,1)}, bf16[4,7,64,384]{3,2,1,0:T(8,128)(2,1)S(1)}, u32[]{:S(2)}, u32[]{:S(2)}) collective-permute-start(bf16[4,7,64,384]{3,2,1,0:T(8,128)(2,1)} %get-tuple-element.62), channel_id=1, source_target_pairs={{0,1},{1,0},{2,3},{3,2},{4,5},{5,4},{6,7},{7,6},{8,9},{9,8},{10,11... | collective-permute-start | bytes 4128776 | tf_op jit(solution)/shard_map/ppermute | solution.py:779
  42.3 57.7 %collective-permute-start.1 = (bf16[4,7,64,384]{3,2,1,0:T(8,128)(2,1)}, bf16[4,7,64,384]{3,2,1,0:T(8,128)(2,1)S(1)}, u32[]{:S(2)}, u32[]{:S(2)}) collective-permute-start(bf16[4,7,64,384]{3,2,1,0:T(8,128)(2,1)} %get-tuple-element.63), channel_id=1, source_target_pairs={{0,2},{1,3},{2,0},{3,1},{4,6},{5,7},{6,4},{7,5},{8,10},{9,11},{10,... | collective-permute-start | bytes 4128776 | tf_op jit(solution)/shard_map/ppermute | solution.py:779
  43.5 56.5 %collective-permute-start.2 = (bf16[4,7,64,384]{3,2,1,0:T(8,128)(2,1)}, bf16[4,7,64,384]{3,2,1,0:T(8,128)(2,1)}, u32[]{:S(2)}, u32[]{:S(2)}) collective-permute-start(bf16[4,7,64,384]{3,2,1,0:T(8,128)(2,1)} %get-tuple-element.64), channel_id=1, source_target_pairs={{0,3},{1,2},{2,1},{3,0},{4,7},{5,6},{6,5},{7,4},{8,11},{9,10},{10,... | collective-permute-start | bytes 4128776 | tf_op jit(solution)/shard_map/ppermute | solution.py:779
  74.7 25.2 %copy-start.32 = (bf16[4,7,64,384]{3,2,1,0:T(8,128)(2,1)}, bf16[4,7,64,384]{3,2,1,0:T(8,128)(2,1)S(1)}, u32[]{:S(2)}) copy-start(bf16[4,7,64,384]{3,2,1,0:T(8,128)(2,1)S(1)} %collective-permute-done.refs_4_.refs_6_) | copy-start | bytes 4128772
  137.2 98.8 %collective-permute-start.3 = (bf16[4,7,64,128]{3,2,1,0:T(8,128)(2,1)}, bf16[4,7,64,128]{3,2,1,0:T(8,128)(2,1)S(1)}, u32[]{:S(2)}, u32[]{:S(2)}) collective-permute-start(bf16[4,7,64,128]{3,2,1,0:T(8,128)(2,1)} %get-tuple-element.66), channel_id=1, source_target_pairs={{0,1},{1,0},{2,3},{3,2},{4,5},{5,4},{6,7},{7,6},{8,9},{9,8},{10,11... | collective-permute-start | bytes 1376264 | tf_op jit(solution)/shard_map/ppermute | solution.py:779
  138.3 97.7 %collective-permute-start.4 = (bf16[4,7,64,128]{3,2,1,0:T(8,128)(2,1)}, bf16[4,7,64,128]{3,2,1,0:T(8,128)(2,1)S(1)}, u32[]{:S(2)}, u32[]{:S(2)}) collective-permute-start(bf16[4,7,64,128]{3,2,1,0:T(8,128)(2,1)} %get-tuple-element.67), channel_id=1, source_target_pairs={{0,2},{1,3},{2,0},{3,1},{4,6},{5,7},{6,4},{7,5},{8,10},{9,11},{10,... | collective-permute-start | bytes 1376264 | tf_op jit(solution)/shard_map/ppermute | solution.py:779
  139.3 96.8 %collective-permute-start.5 = (bf16[4,7,64,128]{3,2,1,0:T(8,128)(2,1)}, bf16[4,7,64,128]{3,2,1,0:T(8,128)(2,1)S(1)}, u32[]{:S(2)}, u32[]{:S(2)}) collective-permute-start(bf16[4,7,64,128]{3,2,1,0:T(8,128)(2,1)} %get-tuple-element.68), channel_id=1, source_target_pairs={{0,3},{1,2},{2,1},{3,0},{4,7},{5,6},{6,5},{7,4},{8,11},{9,10},{10,... | collective-permute-start | bytes 1376264 | tf_op jit(solution)/shard_map/ppermute | solution.py:779
  140.7 56.2 %copy-start.12 = (f32[64,256]{1,0:T(8,128)S(1)}, f32[64,256]{1,0:T(8,128)}, u32[]{:S(2)}) copy-start(f32[64,256]{1,0:T(8,128)} %param.25) | copy-start | bytes 196612
  140.7 56.3 %copy-start.5 = (f32[64,1024]{1,0:T(8,128)S(1)}, f32[64,1024]{1,0:T(8,128)}, u32[]{:S(2)}) copy-start(f32[64,1024]{1,0:T(8,128)} %param.26) | copy-start | bytes 786436
  140.7 56.3 %copy-start.7 = (f32[256,256]{1,0:T(8,128)S(1)}, f32[256,256]{1,0:T(8,128)}, u32[]{:S(2)}) copy-start(f32[256,256]{1,0:T(8,128)} %param.27) | copy-start | bytes 786436
  140.7 56.3 %copy-start.28 = (f32[256]{0:T(256)S(1)}, f32[256]{0:T(256)}, u32[]{:S(2)}) copy-start(f32[256]{0:T(256)} %param.29) | copy-start | bytes 3076
  311.0 8.8 %collective-permute-start.6 = (bf16[4,7,64,128]{3,2,1,0:T(8,128)(2,1)}, bf16[4,7,64,128]{3,2,1,0:T(8,128)(2,1)S(1)}, u32[]{:S(2)}, u32[]{:S(2)}) collective-permute-start(bf16[4,7,64,128]{3,2,1,0:T(8,128)(2,1)} %get-tuple-element.80), channel_id=1, source_target_pairs={{0,1},{1,0},{2,3},{3,2},{4,5},{5,4},{6,7},{7,6},{8,9},{9,8},{10,11... | collective-permute-start | bytes 1376264 | tf_op jit(solution)/shard_map/ppermute | solution.py:779
  312.1 13.6 %collective-permute-start.7 = (bf16[4,7,64,128]{3,2,1,0:T(8,128)(2,1)}, bf16[4,7,64,128]{3,2,1,0:T(8,128)(2,1)S(1)}, u32[]{:S(2)}, u32[]{:S(2)}) collective-permute-start(bf16[4,7,64,128]{3,2,1,0:T(8,128)(2,1)} %get-tuple-element.81), channel_id=1, source_target_pairs={{0,2},{1,3},{2,0},{3,1},{4,6},{5,7},{6,4},{7,5},{8,10},{9,11},{10,... | collective-permute-start | bytes 1376264 | tf_op jit(solution)/shard_map/ppermute | solution.py:779
  313.1 12.6 %collective-permute-start.8 = (bf16[4,7,64,128]{3,2,1,0:T(8,128)(2,1)}, bf16[4,7,64,128]{3,2,1,0:T(8,128)(2,1)S(1)}, u32[]{:S(2)}, u32[]{:S(2)}) collective-permute-start(bf16[4,7,64,128]{3,2,1,0:T(8,128)(2,1)} %get-tuple-element.82), channel_id=1, source_target_pairs={{0,3},{1,2},{2,1},{3,0},{4,7},{5,6},{6,5},{7,4},{8,11},{9,10},{10,... | collective-permute-start | bytes 1376264 | tf_op jit(solution)/shard_map/ppermute | solution.py:779
  319.8 6.0 copy-start.37
  382.5 97.2 %collective-permute-start.9 = (bf16[4,7,64,384]{3,2,1,0:T(8,128)(2,1)}, bf16[4,7,64,384]{3,2,1,0:T(8,128)(2,1)S(1)}, u32[]{:S(2)}, u32[]{:S(2)}) collective-permute-start(bf16[4,7,64,384]{3,2,1,0:T(8,128)(2,1)} %get-tuple-element.84), channel_id=1, source_target_pairs={{0,1},{1,0},{2,3},{3,2},{4,5},{5,4},{6,7},{7,6},{8,9},{9,8},{10,11... | collective-permute-start | bytes 4128776 | tf_op jit(solution)/shard_map/ppermute | solution.py:779
  383.5 96.2 %collective-permute-start.10 = (bf16[4,7,64,384]{3,2,1,0:T(8,128)(2,1)}, bf16[4,7,64,384]{3,2,1,0:T(8,128)(2,1)S(1)}, u32[]{:S(2)}, u32[]{:S(2)}) collective-permute-start(bf16[4,7,64,384]{3,2,1,0:T(8,128)(2,1)} %get-tuple-element.85), channel_id=1, source_target_pairs={{0,2},{1,3},{2,0},{3,1},{4,6},{5,7},{6,4},{7,5},{8,10},{9,11},{10,... | collective-permute-start | bytes 4128776 | tf_op jit(solution)/shard_map/ppermute | solution.py:779
  384.5 95.2 %collective-permute-start.11 = (bf16[4,7,64,384]{3,2,1,0:T(8,128)(2,1)}, bf16[4,7,64,384]{3,2,1,0:T(8,128)(2,1)S(1)}, u32[]{:S(2)}, u32[]{:S(2)}) collective-permute-start(bf16[4,7,64,384]{3,2,1,0:T(8,128)(2,1)} %get-tuple-element.86), channel_id=1, source_target_pairs={{0,3},{1,2},{2,1},{3,0},{4,7},{5,6},{6,5},{7,4},{8,11},{9,10},{10,... | collective-permute-start | bytes 4128776 | tf_op jit(solution)/shard_map/ppermute | solution.py:779
  644.1 4.6 copy-start.1
  654.4 5.6 copy-start.13
  654.4 5.6 copy-start.18
  654.4 5.6 copy-start.19
  654.4 7.1 %copy-start.6 = (f32[64,1024]{1,0:T(8,128)S(1)}, f32[64,1024]{1,0:T(8,128)}, u32[]{:S(2)}) copy-start(f32[64,1024]{1,0:T(8,128)} %param.26) | copy-start | bytes 786436
  654.4 7.1 %copy-start.10 = (f32[64,1024]{1,0:T(8,128)S(1)}, f32[64,1024]{1,0:T(8,128)}, u32[]{:S(2)}) copy-start(f32[64,1024]{1,0:T(8,128)} %param.38) | copy-start | bytes 786436
  654.5 7.1 %copy-start.11 = (f32[64,1024]{1,0:T(8,128)S(1)}, f32[64,1024]{1,0:T(8,128)}, u32[]{:S(2)}) copy-start(f32[64,1024]{1,0:T(8,128)} %param.32) | copy-start | bytes 786436
  658.1 4.5 copy-start.22
  658.1 4.5 copy-start.26
  658.1 4.5 copy-start.27
  658.1 5.2 copy-start.29
  658.1 5.2 copy-start.30
  658.1 5.2 copy-start.31
  (21 other events, 33.3 us)
Sparse Core Ops, SparseCore 0:
  504.4 139.6 all-reduce.3

commit v2 on v1

--- a/solution.py
+++ b/solution.py
@@ -229,24 +229,61 @@
     return jnp.where(iota(values.shape, 0) == rows - 1, 0.0, pltpu.roll(values, rows - 1, 0))
 
 
+def start_sums(sums, starts):
+    @pl.when(pl.program_id(0) == 0)
+    def _():
+        for index, total in enumerate(sums):
+            if starts:
+                total[...] = starts[index][...]
+            else:
+                total[...] = jnp.zeros_like(total)
+
+
+def at_last_step(body):
+    pl.when(pl.program_id(0) == pl.num_programs(0) - 1)(body)
+
+
 def project_kernel(dims, ways, *refs):
     rows, width, wide, wide_part = dims
-    me_ref, x_ref, small_ref, weight_ref, across_ref = refs[:5]
-    down_refs = refs[5 : 5 + ways]
-    down_ref = refs[5 + ways]
+    me_ref, x_ref = refs[:2]
+    pieces = refs[2 : 2 + ways]
+    across_ref, normed_ref = refs[2 + ways : 4 + ways]
+    down_refs = refs[4 + ways : 4 + 2 * ways]
+    weight_ref, small_ref, bias_ref, spread_ref = refs[4 + 2 * ways :]
+
+    @pl.when(pl.program_id(0) == 0)
+    def _():
+        channels, hidden_width = small_ref.shape[1], bias_ref.shape[1]
+        shard = channels // ways
+        bias_shard = hidden_width // ways
+        lanes = -(-(shard + bias_shard) // 128) * 128
+        lane, column = iota((lanes, channels + hidden_width), 0), iota((lanes, channels + hidden_width), 1)
+        total = jnp.zeros((16, channels + hidden_width), F32)
+        for distance, piece in enumerate(pieces):
+            place = me_ref[0] ^ distance
+            weight_ref[pl.ds(pl.multiple_of(place * shard, shard), shard)] = piece[:shard]
+            target = jnp.where(
+                lane < shard,
+                lane + shard * place,
+                channels + lane - shard + bias_shard * place,
+            )
+            chosen = one_hot((column == target) & (lane < shard + bias_shard))
+            total = total + dot(piece[shard : shard + 16, :lanes], chosen)
+        small_ref[...] = total[:, :channels]
+        bias_ref[...] = total[0:1, channels:]
+
     gain, offset = small_ref[9:10], small_ref[10:11]
     expand = one_hot(expand_condition(wide, width))
     for row in range(rows):
         span = slice(row * width, (row + 1) * width)
         normed, _, _ = normalize(x_ref[0, span].astype(F32), gain, offset)
         normed = normed.astype(BF)
+        normed_ref[0, span] = normed
         across_ref[0, span] = dot(normed, weight_ref[:, : 3 * HALF]).astype(BF)
-        spread = dot(expand, normed).astype(BF)
-        down = dot(spread, weight_ref[:, 3 * HALF :]).astype(BF)
-        down_ref[row] = down
+        spread_ref[row] = dot(expand, normed).astype(BF)
         for distance in range(ways):
             start = pl.multiple_of((me_ref[0] ^ distance) * wide_part, wide_part)
-            down_refs[distance][0, row] = down_ref[row, pl.ds(start, wide_part)]
+            down_refs[distance][0, row] = spread_ref[row, pl.ds(start, wide_part)]
 
 
 def rank_row(mask_row, width):
@@ -360,8 +397,8 @@
             )
 
 
-def down_setup(me_ref, mask_ref, column_ref, width, wide, wide_part):
-    image = pl.program_id(0)
+def down_setup(me_ref, mask_ref, column_ref, width, wide, wide_part, first):
+    image = pl.program_id(0) + first
     mask_row = mask_ref[pl.ds(image, 1)].astype(F32)
     valid = one_hot(expand_condition(wide, width) & (mask_row > 0.0))
     column_ref[...] = dot(valid, jnp.ones((width, HALF), BF))
@@ -400,17 +437,24 @@
     return jnp.concatenate([edge, values, edge], axis=0)
 
 
-def down_kernel(dims, ways, *refs):
+def down_kernel(dims, ways, first, *refs):
     height, width, wide, wide_part, spare = dims
-    me_ref, mask_ref, small_ref = refs[:3]
-    pieces_in = refs[3 : 3 + ways]
-    joined_refs = refs[3 + ways : 3 + 2 * ways]
-    attended_ref, total_ref, mixed_ref, joined_ref, column_ref, shift_ref = refs[3 + 2 * ways :]
+    me_ref, mask_ref, small_ref, weight_ref = refs[:4]
+    pieces_in = refs[4 : 4 + ways]
+    joined_refs = refs[4 + ways : 4 + 2 * ways]
+    attended_ref, total_ref, saved_ref, normed_ref, mixed_ref, joined_ref, column_ref, shift_ref = refs[
+        4 + 2 * ways :
+    ]
     rows = height // ways
-    start = down_setup(me_ref, mask_ref, column_ref, width, wide, wide_part)
-    assemble(me_ref, pieces_in, mixed_ref, 0, rows)
+    start = down_setup(me_ref, mask_ref, column_ref, width, wide, wide_part, first)
+    assemble(me_ref, pieces_in, normed_ref, 0, rows)
     tokens = height * GROUP
     windows = wide_part // GROUP
+    normed = normed_ref[...].reshape(height * wide_part, 2 * HALF)
+    mixed_low = dot(normed, weight_ref[:, 3 * HALF :]).astype(BF)
+    mixed_low = mixed_low.reshape(height, wide_part, 3 * HALF)
+    saved_ref[0] = mixed_low
+    mixed_ref[...] = mixed_low.astype(F32)
 
     @pl.when(pl.program_id(0) == 0)
     def _():
@@ -474,24 +518,46 @@
     return jnp.where(hidden >= 0.0, 1.0 - tail, tail), decay * INV_ROOT_TAU
 
 
-def middle_kernel(dims, ways, *refs):
+def middle_kernel(dims, ways, last, *refs):
     rows, width, wide, wide_part, chunk, hidden_part = dims
-    me_ref, x_ref, cot_ref, across_ref = refs[:4]
-    pieces_in = refs[4 : 4 + ways]
-    out_ref, expand_ref, shrink_ref, small_ref, bias_ref = refs[4 + ways : 9 + ways]
-    block_ref, middle_ref, grad_across_ref = refs[9 + ways : 12 + ways]
-    grad_refs = refs[12 + ways : 12 + 2 * ways]
-    dout_ref, dexpand_ref, dshrink_ref, dbias_ref, dsmall_ref = refs[12 + 2 * ways : 17 + 2 * ways]
-    wide_ref, joined_ref, normed_ref, active_ref, hidden_ref, attended_ref, down_ref, gwide_ref = refs[
-        17 + 2 * ways :
-    ]
+    refs = list(refs)
+
+    def take(number):
+        taken = refs[:number]
+        del refs[:number]
+        return taken
+
+    me_ref, x_ref, cot_ref, across_ref = take(4)
+    pieces_in = take(ways)
+    weights_in = take(ways)
+    small_ref, bias_ref = take(2)
+    starts = take(5) if last else None
+    block_ref, middle_ref, grad_across_ref = take(3)
+    grad_refs = take(ways)
+    dbias_ref, dsmall_ref = take(2)
+    piece_refs = take(ways) if last else None
+    dout_ref, dexpand_ref, dshrink_ref = take(3)
+    out_ref, expand_ref, shrink_ref = take(3)
+    wide_ref, joined_ref, normed_ref, active_ref, hidden_ref, attended_ref, down_ref, gwide_ref = take(8)
+    turned_ref = take(1)[0] if last else None
     tokens = rows * width
     hidden_width = expand_ref.shape[1]
+    channels = 2 * HALF
+    shard = channels // ways
+    blocks = hidden_width // channels
+    start_sums((dbias_ref, dsmall_ref, dout_ref, dexpand_ref, dshrink_ref), starts)
 
     @pl.when(pl.program_id(0) == 0)
     def _():
-        for ref in (dout_ref, dexpand_ref, dshrink_ref, dbias_ref, dsmall_ref):
-            ref[...] = jnp.zeros_like(ref)
+        for distance, piece in enumerate(weights_in):
+            place = me_ref[0] ^ distance
+            span = pl.ds(pl.multiple_of(place * shard, shard), shard)
+            out_ref[span] = piece[:, :channels]
+            expand_ref[span] = piece[:, channels : channels + hidden_width]
+            for block in range(blocks):
+                begin = pl.multiple_of((place * blocks + block) * shard, shard)
+                lanes = slice(channels + hidden_width + block * channels, channels + hidden_width + (block + 1) * channels)
+                shrink_ref[pl.ds(begin, shard)] = piece[:, lanes]
 
     assemble(me_ref, pieces_in, wide_ref, 1, wide_part)
     contract = contract_matrix(width, wide)
@@ -551,32 +617,52 @@
     dout_ref[...] += dot_tn(joined_ref[...], attended_ref[...])
     dexpand_ref[...] += dot_tn(normed_ref[...], hidden_ref[...])
     dshrink_ref[...] += dot_tn(cot_ref[0], active_ref[...])
-
-
-def across_back_kernel(
-    dims,
-    across_ref,
-    grad_ref,
-    attended_ref,
-    total_ref,
-    keys_ref,
-    values_ref,
-    mask_ref,
-    small_ref,
-    mixed_ref,
-    taps_ref,
-    dkeys_ref,
-    dvalues_ref,
-    local_ref,
-):
+    if last:
+
+        @at_last_step
+        def _():
+            for block in range(blocks):
+                lanes = slice(block * channels, (block + 1) * channels)
+                turned_ref[lanes] = jnp.transpose(dshrink_ref[:, lanes])
+            for distance, piece in enumerate(piece_refs):
+                place = me_ref[0] ^ distance
+                span = pl.ds(pl.multiple_of(place * shard, shard), shard)
+                piece[:, :channels] = dout_ref[span]
+                piece[:, channels : channels + hidden_width] = dexpand_ref[span]
+                for block in range(blocks):
+                    begin = pl.multiple_of((place * blocks + block) * shard, shard)
+                    lanes = slice(channels + hidden_width + block * channels, channels + hidden_width + (block + 1) * channels)
+                    piece[:, lanes] = turned_ref[pl.ds(begin, shard)]
+
+
+def shard_pieces(me_ref, piece_refs, total_ref):
+    shard = piece_refs[0].shape[0]
+
+    @at_last_step
+    def _():
+        for distance, piece in enumerate(piece_refs):
+            begin = pl.multiple_of((me_ref[0] ^ distance) * shard, shard)
+            piece[...] = total_ref[pl.ds(begin, shard)]
+
+
+def across_back_kernel(dims, ways, first, last, *refs):
     rows, width, kept, key_rows, chunk = dims
+    refs = list(refs)
+
+    def take(number):
+        taken = refs[:number]
+        del refs[:number]
+        return taken
+
+    me_ref, across_ref, grad_ref, attended_ref, total_ref, keys_ref, values_ref, normed_ref = take(8)
+    mask_ref, small_ref = take(2)
+    starts = take(2) if last else None
+    mixed_ref, taps_ref = take(2)
+    piece_refs = take(ways) if last else None
+    dweight_ref, dkeys_ref, dvalues_ref, local_ref = take(4)
     tokens = rows * width
-    image = pl.program_id(0)
-
-    @pl.when(image == 0)
-    def _():
-        taps_ref[...] = jnp.zeros_like(taps_ref)
-
+    image = pl.program_id(0) + first
+    start_sums((taps_ref, dweight_ref), starts)
     dkeys_ref[...] = jnp.zeros_like(dkeys_ref)
     dvalues_ref[...] = jnp.zeros_like(dvalues_ref)
 
@@ -631,25 +717,36 @@
         mixed_ref[0, target, HALF : 2 * HALF] = unpacked[:, :HALF].astype(BF)
         whole = unpacked[:, HALF : 2 * HALF] + unpacked[:, 2 * HALF :] + local_ref[target]
         mixed_ref[0, target, 2 * HALF :] = whole.astype(BF)
-
-
-def down_back_kernel(dims, ways, *refs):
+    dweight_ref[...] += dot_tn(normed_ref[0], mixed_ref[0])
+    if last:
+        shard_pieces(me_ref, piece_refs, dweight_ref)
+
+
+def down_back_kernel(dims, ways, first, last, *refs):
     height, width, wide, wide_part, spare = dims
-    me_ref, mask_ref, small_ref, attended_ref, total_ref = refs[:5]
-    pieces_in = refs[5 : 5 + ways]
-    grads_in = refs[5 + ways : 5 + 2 * ways]
-    out_refs = refs[5 + 2 * ways : 5 + 3 * ways]
-    taps_ref, mixed_ref, grad_ref, out_ref, column_ref = refs[5 + 3 * ways :]
+    refs = list(refs)
+
+    def take(number):
+        taken = refs[:number]
+        del refs[:number]
+        return taken
+
+    me_ref, mask_ref, small_ref, weight_ref, attended_ref, total_ref, saved_ref = take(7)
+    normed_in = take(ways)
+    grads_in = take(ways)
+    starts = take(2) if last else None
+    out_refs = take(ways)
+    taps_ref = take(1)[0]
+    piece_refs = take(ways) if last else None
+    dweight_ref, normed_ref, mixed_ref, grad_ref, out_ref, turned_ref, column_ref = take(7)
     rows = height // ways
-    start = down_setup(me_ref, mask_ref, column_ref, width, wide, wide_part)
-    assemble(me_ref, pieces_in, mixed_ref, 0, rows)
+    start = down_setup(me_ref, mask_ref, column_ref, width, wide, wide_part, first)
+    assemble(me_ref, normed_in, normed_ref, 0, rows)
     assemble(me_ref, grads_in, grad_ref, 0, rows)
+    mixed_ref[...] = saved_ref[0].astype(F32)
     tokens = height * GROUP
     windows = wide_part // GROUP
-
-    @pl.when(pl.program_id(0) == 0)
-    def _():
-        taps_ref[...] = jnp.zeros_like(taps_ref)
+    start_sums((taps_ref, dweight_ref), starts)
 
     def one_window(window, carry):
         span = pl.ds(pl.multiple_of(window * GROUP, GROUP), GROUP)
@@ -687,42 +784,46 @@
         return carry
 
     lax.fori_loop(0, windows, one_window, 0)
+    mixed_grad = out_ref[...].reshape(height * wide_part, 3 * HALF).astype(BF)
+    grad_normed = dot_nt(mixed_grad, weight_ref[:, 3 * HALF :]).astype(BF)
+    turned_ref[...] = grad_normed.reshape(height, wide_part, 2 * HALF)
     for distance in range(ways):
         place = me_ref[0] ^ distance
-        out_refs[distance][0] = out_ref[pl.ds(place * rows, rows)].astype(BF)
-
-
-def final_kernel(dims, ways, *refs):
+        out_refs[distance][0] = turned_ref[pl.ds(place * rows, rows)]
+    normed = normed_ref[...].reshape(height * wide_part, 2 * HALF)
+    dweight_ref[...] += dot_tn(normed, mixed_grad)
+    if last:
+        shard_pieces(me_ref, piece_refs, dweight_ref)
+
+
+def final_kernel(dims, ways, last, *refs):
     rows, width, wide, wide_part, chunk = dims
-    me_ref, x_ref, middle_ref, across_ref = refs[:4]
-    pieces_in = refs[4 : 4 + ways]
-    small_ref, weight_ref, grad_ref, dweight_ref, dsmall_ref, wide_ref, mixed_ref, normed_ref = refs[
-        4 + ways :
-    ]
+    refs = list(refs)
+
+    def take(number):
+        taken = refs[:number]
+        del refs[:number]
+        return taken
+
+    me_ref, x_ref, middle_ref, across_ref = take(4)
+    pieces_in = take(ways)
+    small_ref, weight_ref = take(2)
+    starts = take(1) if last else None
+    others = take(4) if last else None
+    grad_ref, dsmall_ref = take(2)
+    whole_ref = take(1)[0] if last else None
+    wide_ref, down_ref = take(2)
     tokens = rows * width
-
-    @pl.when(pl.program_id(0) == 0)
-    def _():
-        dweight_ref[...] = jnp.zeros_like(dweight_ref)
-        dsmall_ref[...] = jnp.zeros_like(dsmall_ref)
-
+    start_sums((dsmall_ref,), starts)
     assemble(me_ref, pieces_in, wide_ref, 1, wide_part)
     contract = contract_matrix(width, wide)
     for row in range(rows):
-        span = slice(row * width, (row + 1) * width)
-        mixed_ref[span, : 3 * HALF] = across_ref[0, span]
-        mixed_ref[span, 3 * HALF :] = dot(contract, wide_ref[row]).astype(BF)
+        down_ref[row * width : (row + 1) * width] = dot(contract, wide_ref[row])
 
     def token_rows(step, carry):
         span = pl.ds(pl.multiple_of(step * chunk, 16), chunk)
-        normed, scaled, recip = normalize(
-            x_ref[0, span].astype(F32), small_ref[9:10], small_ref[10:11]
-        )
-        normed_ref[span] = normed.astype(BF)
-        mixed = mixed_ref[span]
-        grad_normed = dot_nt(mixed[:, : 3 * HALF], weight_ref[:, : 3 * HALF])
-        grad_down = dot_nt(mixed[:, 3 * HALF :], weight_ref[:, 3 * HALF :])
-        grad_normed = grad_normed + grad_down.astype(BF).astype(F32)
+        _, scaled, recip = normalize(x_ref[0, span].astype(F32), small_ref[9:10], small_ref[10:11])
+        grad_normed = dot_nt(across_ref[0, span], weight_ref[:, : 3 * HALF]) + down_ref[span]
         dsmall_ref[0:8] += fold_rows(grad_normed * scaled)
         dsmall_ref[8:16] += fold_rows(grad_normed)
         grad_ref[0, span] = middle_ref[0, span] + normalize_back(
@@ -731,11 +832,61 @@
         return carry
 
     lax.fori_loop(0, tokens // chunk, token_rows, 0)
-    dweight_ref[...] += dot_tn(normed_ref[...], mixed_ref[...])
-
-
-def image_block(*shape):
-    return pl.BlockSpec((1,) + shape, lambda image: (image,) + (0,) * len(shape))
+    if last:
+
+        @at_last_step
+        def _():
+            across_taps, down_taps, middle_sums, bias_sums = others
+            channels = 2 * HALF
+
+            def total(ref, index):
+                return jnp.sum(ref[8 * index : 8 * index + 8], axis=0, keepdims=True)
+
+            def set_taps(row, index):
+                whole_ref[row : row + 1, :HALF] = total(across_taps, index)
+                whole_ref[row : row + 1, HALF:] = total(down_taps, index)
+
+            whole_ref[...] = jnp.zeros_like(whole_ref)
+            for tap in range(9):
+                set_taps(tap, tap)
+            whole_ref[9:10] = total(dsmall_ref, 0)
+            whole_ref[10:11] = total(dsmall_ref, 1)
+            set_taps(11, 9)
+            for index in range(4):
+                whole_ref[12 + index : 13 + index] = total(middle_sums, index)
+            bias = total(bias_sums, 0)
+            for block in range(bias.shape[1] // channels):
+                whole_ref[16 + block : 17 + block] = bias[:, block * channels : (block + 1) * channels]
+
+
+def update_kernel(blocks, factor_ref, shard_ref, across_ref, down_ref, *refs):
+    old, new = refs[:12], refs[12:]
+    factor = factor_ref[0]
+    rows, channels = old[1].shape
+    hidden_width = old[2].shape[1]
+
+    def update(index, grads, rate, spans=(slice(None), slice(None))):
+        weight, first, second = (old[part * 4 + index][spans] for part in range(3))
+        results = adam_update(weight, first, second, grads * factor, rate, WEIGHT_DECAY)
+        for part in range(3):
+            new[part * 4 + index][spans] = results[part]
+
+    update(0, across_ref[...], RATE_MATRIX, (slice(None), slice(0, 3 * HALF)))
+    update(0, down_ref[...], RATE_MATRIX, (slice(None), slice(3 * HALF, 6 * HALF)))
+    update(1, shard_ref[:, :channels], RATE_OUTPUT)
+    update(2, shard_ref[:, channels : channels + hidden_width], RATE_MATRIX)
+    for block in range(blocks):
+        begin = channels + hidden_width + block * channels
+        update(
+            3,
+            shard_ref[:, begin : begin + channels],
+            RATE_MATRIX,
+            (slice(block * rows, (block + 1) * rows), slice(None)),
+        )
+
+
+def image_block(*shape, first=0):
+    return pl.BlockSpec((1,) + shape, lambda image: (image + first,) + (0,) * len(shape))
 
 
 def whole_block(*shape):
@@ -746,19 +897,30 @@
     return pl.BlockSpec(memory_space=pltpu.SMEM)
 
 
-def run_kernel(body, images, in_specs, out_specs, out_shapes, scratch, flops, operands):
+def run_kernel(body, images, inputs, outputs, scratch, micros, after=(), alias=None):
+    number = len(inputs)
+    hidden = list(after)
+    aliases = {}
+    if alias is not None:
+        aliases = {number + len(hidden): alias[1]}
+        hidden.append(alias[0])
+
+    def wrapped(*refs):
+        body(*refs[:number], *refs[number + len(hidden) :])
+
     return pl.pallas_call(
-        body,
+        wrapped,
         grid=(images,),
-        in_specs=in_specs,
-        out_specs=out_specs,
-        out_shape=out_shapes,
+        in_specs=[spec for _, spec in inputs] + [pl.BlockSpec(memory_space=pl.ANY)] * len(hidden),
+        out_specs=[spec for _, _, spec in outputs],
+        out_shape=[jax.ShapeDtypeStruct(shape, dtype) for shape, dtype, _ in outputs],
         scratch_shapes=scratch,
+        input_output_aliases=aliases,
         compiler_params=pltpu.CompilerParams(vmem_limit_bytes=VMEM_LIMIT),
         cost_estimate=pl.CostEstimate(
-            flops=int(flops), bytes_accessed=int(flops / 300), transcendentals=0
+            flops=int(micros * 1e9), bytes_accessed=int(micros * 1e6), transcendentals=0
         ),
-    )(*operands)
+    )(*[operand for operand, _ in inputs], *hidden)
 
 
 def adam_update(weight, first_old, second_old, grad_value, rate_value, decay_value):
@@ -772,12 +934,45 @@
     return (new_first, new_second, new_weight)
 
 
-def exchange(pieces, ways):
-    received = [pieces[0]]
-    for distance in range(1, ways):
-        pairs = [(place, place ^ distance) for place in range(ways)]
-        received.append(lax.ppermute(pieces[distance], "seq", pairs))
-    return received
+def swap(value, axis, distance):
+    return lax.ppermute(value, axis, [(place, place ^ distance) for place in range(lax.axis_size(axis))])
+
+
+def exchange(pieces):
+    return [pieces[0]] + [swap(pieces[d], "seq", d) for d in range(1, len(pieces))]
+
+
+def tree_sum(values):
+    while len(values) > 1:
+        values = [values[i] + values[i + 1] for i in range(0, len(values), 2)]
+    return values[0]
+
+
+def sum_chips(value):
+    return tree_sum([value] + [swap(value, "img", d) for d in range(2, lax.axis_size("img"), 2)])
+
+
+def sum_cores(value):
+    return value + swap(value, "img", 1)
+
+
+def sum_halves(value):
+    core = lax.axis_index("img") % 2
+    rows = value.shape[0] // 2
+    mine = lax.dynamic_slice_in_dim(value, core * rows, rows, 0)
+    other = lax.dynamic_slice_in_dim(value, (1 - core) * rows, rows, 0)
+    stages = [mine + swap(other, "img", 1)]
+    distance = 2
+    while distance < lax.axis_size("img"):
+        stages.append(stages[-1] + swap(stages[-1], "img", distance))
+        distance *= 2
+    return stages
+
+
+def join_halves(mine):
+    other = swap(mine, "img", 1)
+    lower = lax.axis_index("img") % 2 == 0
+    return jnp.concatenate([jnp.where(lower, mine, other), jnp.where(lower, other, mine)], axis=0)
 
 
 def on_device(
@@ -815,277 +1010,318 @@
     key_rows = -(-rows * kept // 256) * 256
     window_tokens = height * GROUP
     spare = -window_tokens % 128
+    shard = qkv_weight.shape[0]
     hidden_width = expand_weight.shape[1]
+    blocks = hidden_width // channels
     chunk = width
-
-    gathered = (
-        lax.all_gather(qkv_weight.astype(BF), "seq", axis=0, tiled=True),
-        lax.all_gather(out_weight.astype(BF), "seq", axis=0, tiled=True),
-        lax.all_gather(expand_weight.astype(BF), "seq", axis=0, tiled=True),
-        lax.all_gather(shrink_weight.astype(BF), "seq", axis=0, tiled=True),
-        lax.all_gather(small_params.astype(BF), "seq", axis=1, tiled=True),
-        lax.all_gather(expand_bias.astype(BF), "seq", axis=0, tiled=True),
-    )
-    qkv_low, out_low, expand_low, shrink_low, small_low, bias_low = gathered
-    small_full = small_low.astype(F32)
-    bias_full = bias_low.astype(F32).reshape(1, hidden_width)
+    pair = count // 2
+    halves = (0, pair)
+
+    small_pack = jnp.concatenate(
+        [small_params, jnp.pad(expand_bias[None], ((0, small_params.shape[0] - 1), (0, 0)))], axis=1
+    )
+    small_pack = jnp.pad(small_pack, ((0, 0), (0, qkv_weight.shape[1] - small_pack.shape[1])))
+    early = jnp.concatenate([qkv_weight, small_pack], axis=0).astype(BF)
+    early_pieces = exchange([early] * ways)
+    shrink_blocks = [shrink_weight[block * shard : (block + 1) * shard] for block in range(blocks)]
+    late = jnp.concatenate([out_weight, expand_weight, *shrink_blocks], axis=1).astype(BF)
+
     x = images.reshape(count, tokens, channels)
     cot = cotangent.reshape(count, tokens, channels)
-
-    def shape(dims, dtype):
-        return jax.ShapeDtypeStruct(dims, dtype)
-
-    small_spec = whole_block(*small_full.shape)
-    mask_spec = whole_block(*valid_mask.shape)
-    piece_qkv = (rows, wide_part, 3 * HALF)
+    me_in = (me, scalar_block())
+    mask_in = (valid_mask, whole_block(*valid_mask.shape))
+    piece_in = (rows, wide_part, channels)
     piece_out = (rows, wide_part, HALF)
-
-    across_mixed, *down_pieces = run_kernel(
+    qkv_shape = (channels, 6 * HALF)
+
+    def per_image(array, first=0):
+        return (array, image_block(*array.shape[1:], first=first))
+
+    def whole(array):
+        return (array, whole_block(*array.shape))
+
+    def new_image(dims, dtype, images=pair):
+        return ((images,) + dims, dtype, image_block(*dims))
+
+    def new_whole(dims, dtype):
+        return (dims, dtype, whole_block(*dims))
+
+    results = run_kernel(
         functools.partial(project_kernel, (rows, width, wide, wide_part), ways),
         count,
-        [scalar_block(), image_block(tokens, channels), small_spec, whole_block(*qkv_low.shape)],
-        [image_block(tokens, 3 * HALF)] + [image_block(*piece_qkv)] * ways,
-        [shape((count, tokens, 3 * HALF), BF)] + [shape((count,) + piece_qkv, BF)] * ways,
-        [pltpu.VMEM((rows, wide, 3 * HALF), BF)],
-        2.2 * count * tokens * channels * 6 * HALF,
-        (me, x, small_full, qkv_low),
-    )
-    down_mixed = exchange(down_pieces, ways)
+        [me_in, per_image(x)] + [whole(piece) for piece in early_pieces],
+        [new_image((tokens, 3 * HALF), BF, count), new_image((tokens, channels), BF, count)]
+        + [new_image(piece_in, BF, count)] * ways
+        + [new_whole(qkv_shape, BF), new_whole((16, channels), F32), new_whole((1, hidden_width), F32)],
+        [pltpu.VMEM((rows, wide, channels), BF)],
+        12,
+    )
+    across_mixed, normed = results[:2]
+    normed_pieces = exchange(results[2 : 2 + ways])
+    qkv_low, small_full, bias_full = results[2 + ways :]
+    late_pieces = exchange([late] * ways)
+    small_in, qkv_in = whole(small_full), whole(qkv_low)
 
     attention_dims = (rows, width, kept, key_rows, chunk)
     key_shape = (BRANCH_HEADS, key_rows, HALF)
-    joined_across, across_attended, across_total, across_keys, across_values = run_kernel(
+    joined_across, attended, log_total, keys, values = run_kernel(
         functools.partial(across_kernel, attention_dims),
         count,
-        [image_block(tokens, 3 * HALF), mask_spec, small_spec],
+        [per_image(across_mixed), mask_in, small_in],
         [
-            image_block(tokens, HALF),
-            image_block(tokens, HALF),
-            image_block(tokens, HALF),
-            image_block(*key_shape),
-            image_block(*key_shape),
-        ],
-        [
-            shape((count, tokens, HALF), BF),
-            shape((count, tokens, HALF), F32),
-            shape((count, tokens, HALF), F32),
-            shape((count,) + key_shape, BF),
-            shape((count,) + key_shape, BF),
+            new_image((tokens, HALF), BF, count),
+            new_image((tokens, HALF), F32, count),
+            new_image((tokens, HALF), F32, count),
+            new_image(key_shape, BF, count),
+            new_image(key_shape, BF, count),
         ],
         [pltpu.VMEM((tokens, HALF), F32)],
-        4.0 * count * BRANCH_HEADS * tokens * key_rows * 256,
-        (across_mixed, valid_mask, small_full),
-    )
+        60,
+    )
+    last_result = attended
 
     down_dims = (height, width, wide, wide_part, spare)
     grid_f32 = (height, wide_part, HALF)
-    down_results = run_kernel(
-        functools.partial(down_kernel, down_dims, ways),
-        count,
-        [scalar_block(), mask_spec, small_spec] + [image_block(*piece_qkv)] * ways,
-        [image_block(*piece_out)] * ways + [image_block(*grid_f32)] * 2,
-        [shape((count,) + piece_out, BF)] * ways + [shape((count,) + grid_f32, F32)] * 2,
-        [
-            pltpu.VMEM((height, wide_part, 3 * HALF), F32),
-            pltpu.VMEM(grid_f32, F32),
-            pltpu.VMEM((wide, HALF), F32),
-            pltpu.VMEM((window_tokens, HALF), F32),
-        ],
-        4.0 * count * wide_part * BRANCH_HEADS * height * (window_tokens + spare) * 256,
-        (me, valid_mask, small_full, *down_mixed),
-    )
-    down_attended, down_total = down_results[ways:]
-    joined_down = exchange(down_results[:ways], ways)
-
-    middle_results = run_kernel(
-        functools.partial(middle_kernel, (rows, width, wide, wide_part, chunk, 2 * HALF), ways),
-        count,
-        [
-            scalar_block(),
-            image_block(tokens, channels),
-            image_block(tokens, channels),
-            image_block(tokens, HALF),
-        ]
-        + [image_block(*piece_out)] * ways
-        + [
-            whole_block(*out_low.shape),
-            whole_block(*expand_low.shape),
-            whole_block(*shrink_low.shape),
-            small_spec,
-            whole_block(1, hidden_width),
-        ],
-        [
-            image_block(tokens, channels),
-            image_block(tokens, channels),
-            image_block(tokens, HALF),
-        ]
-        + [image_block(*piece_out)] * ways
-        + [
-            whole_block(channels, channels),
-            whole_block(channels, hidden_width),
-            whole_block(channels, hidden_width),
-            whole_block(8, hidden_width),
-            whole_block(32, channels),
-        ],
-        [
-            shape((count, tokens, channels), F32),
-            shape((count, tokens, channels), F32),
-            shape((count, tokens, HALF), BF),
-        ]
-        + [shape((count,) + piece_out, BF)] * ways
-        + [
-            shape((channels, channels), F32),
-            shape((channels, hidden_width), F32),
-            shape((channels, hidden_width), F32),
-            shape((8, hidden_width), F32),
-            shape((32, channels), F32),
-        ],
-        [
-            pltpu.VMEM((rows, wide, HALF), BF),
-            pltpu.VMEM((tokens, channels), BF),
-            pltpu.VMEM((tokens, channels), BF),
-            pltpu.VMEM((tokens, hidden_width), BF),
-            pltpu.VMEM((tokens, hidden_width), BF),
-            pltpu.VMEM((tokens, channels), BF),
-            pltpu.VMEM((tokens, HALF), BF),
-            pltpu.VMEM((rows, wide, HALF), BF),
-        ],
-        6.0 * count * tokens * channels * (channels + 2 * hidden_width),
-        (me, x, cot, joined_across, *joined_down, out_low, expand_low, shrink_low, small_full, bias_full),
-    )
-    block_out, grad_middle, grad_across = middle_results[:3]
-    sum_out, sum_expand, sum_shrink, bias_part, small_part = middle_results[3 + ways :]
-    grad_down = exchange(middle_results[3 : 3 + ways], ways)
-
-    across_mixed_grad, across_taps = run_kernel(
-        functools.partial(across_back_kernel, attention_dims),
-        count,
-        [
-            image_block(tokens, 3 * HALF),
-            image_block(tokens, HALF),
-            image_block(tokens, HALF),
-            image_block(tokens, HALF),
-            image_block(*key_shape),
-            image_block(*key_shape),
-            mask_spec,
-            small_spec,
-        ],
-        [image_block(tokens, 3 * HALF), whole_block(80, HALF)],
-        [shape((count, tokens, 3 * HALF), BF), shape((80, HALF), F32)],
-        [
-            pltpu.VMEM((HALF, key_rows), F32),
-            pltpu.VMEM((HALF, key_rows), F32),
-            pltpu.VMEM((tokens, HALF), F32),
-        ],
-        10.0 * count * BRANCH_HEADS * tokens * key_rows * 256,
-        (
-            across_mixed,
-            grad_across,
-            across_attended,
-            across_total,
-            across_keys,
-            across_values,
-            valid_mask,
-            small_full,
-        ),
-    )
-
-    down_back_results = run_kernel(
-        functools.partial(down_back_kernel, down_dims, ways),
-        count,
-        [scalar_block(), mask_spec, small_spec]
-        + [image_block(*grid_f32)] * 2
-        + [image_block(*piece_qkv)] * ways
-        + [image_block(*piece_out)] * ways,
-        [image_block(*piece_qkv)] * ways + [whole_block(80, HALF)],
-        [shape((count,) + piece_qkv, BF)] * ways + [shape((80, HALF), F32)],
-        [
-            pltpu.VMEM((height, wide_part, 3 * HALF), F32),
-            pltpu.VMEM(grid_f32, F32),
-            pltpu.VMEM((height, wide_part, 3 * HALF), F32),
-            pltpu.VMEM((wide, HALF), F32),
-        ],
-        10.0 * count * wide_part * BRANCH_HEADS * height * (window_tokens + spare) * 256,
-        (me, valid_mask, small_full, down_attended, down_total, *down_mixed, *grad_down),
-    )
-    down_taps = down_back_results[ways]
-    down_mixed_grad = exchange(down_back_results[:ways], ways)
-
-    input_grad, sum_qkv, norm_part = run_kernel(
-        functools.partial(final_kernel, (rows, width, wide, wide_part, chunk), ways),
-        count,
-        [
-            scalar_block(),
-            image_block(tokens, channels),
-            image_block(tokens, channels),
-            image_block(tokens, 3 * HALF),
-        ]
-        + [image_block(*piece_qkv)] * ways
-        + [small_spec, whole_block(*qkv_low.shape)],
-        [
-            image_block(tokens, channels),
-            whole_block(channels, 6 * HALF),
-            whole_block(16, channels),
-        ],
-        [
-            shape((count, tokens, channels), F32),
-            shape((channels, 6 * HALF), F32),
-            shape((16, channels), F32),
-        ],
-        [
-            pltpu.VMEM((rows, wide, 3 * HALF), BF),
-            pltpu.VMEM((tokens, 6 * HALF), BF),
-            pltpu.VMEM((tokens, channels), BF),
-        ],
-        4.0 * count * tokens * channels * 6 * HALF,
-        (me, x, grad_middle, across_mixed_grad, *down_mixed_grad, small_full, qkv_low),
-    )
-
-    taps = jnp.concatenate([across_taps, down_taps], axis=1).reshape(10, 8, channels).sum(axis=1)
-    norm_rows = norm_part.reshape(2, 8, channels).sum(axis=1)
-    mid_rows = small_part.reshape(4, 8, channels).sum(axis=1)
-    sum_small = jnp.concatenate([taps[:9], norm_rows, taps[9:], mid_rows], axis=0)
-    sum_bias = bias_part.sum(axis=0)
-
-    params = (qkv_weight, out_weight, expand_weight, shrink_weight, small_params, expand_bias)
-    shard_dims = (0, 0, 0, 1, 1, 0)
-    full_grads = lax.psum(
-        (sum_qkv, sum_out, sum_expand, sum_shrink, sum_small, sum_bias), ("img", "seq")
-    )
-    squared = jnp.float32(0.0)
-    for full_grad in full_grads:
-        squared = squared + jnp.sum(full_grad * full_grad)
-    sizes = [part.shape[dim] for part, dim in zip(params, shard_dims)]
-    sizes[3] = shrink_weight.shape[0]
-    shares = [
-        lax.dynamic_slice_in_dim(full_grad, owner * size, size, dim)
-        for full_grad, size, dim in zip(full_grads, sizes, shard_dims)
-    ]
-    shares[3] = shares[3].T
-    grad_norm = jnp.sqrt(squared)
+    mixed_grid = (height, wide_part, 3 * HALF)
+    normed_grid = (height, wide_part, channels)
+    down, joined_pieces = [], []
+    for index, first in enumerate(halves):
+        results = run_kernel(
+            functools.partial(down_kernel, down_dims, ways, first),
+            pair,
+            [me_in, mask_in, small_in, qkv_in] + [per_image(piece, first) for piece in normed_pieces],
+            [new_image(piece_out, BF)] * ways
+            + [new_image(grid_f32, F32)] * 2
+            + [new_image(mixed_grid, BF)],
+            [
+                pltpu.VMEM(normed_grid, BF),
+                pltpu.VMEM(mixed_grid, F32),
+                pltpu.VMEM(grid_f32, F32),
+                pltpu.VMEM((wide, HALF), F32),
+                pltpu.VMEM((window_tokens, HALF), F32),
+            ],
+            18,
+            after=(last_result,),
+        )
+        down.append(results[ways:])
+        joined_pieces.append(exchange(results[:ways]))
+        last_result = results[ways]
+
+    block_out = None
+    grad_middle, grad_across, grad_pieces = [], [], []
+    sums = None
+    matrix_sums = [(channels, channels), (channels, hidden_width), (channels, hidden_width)]
+    late_shape = late.shape
+    for index, first in enumerate(halves):
+        last = index == 1
+        results = run_kernel(
+            functools.partial(
+                middle_kernel, (rows, width, wide, wide_part, chunk, channels), ways, last
+            ),
+            pair,
+            [
+                me_in,
+                (x, image_block(tokens, channels, first=first)),
+                (cot, image_block(tokens, channels, first=first)),
+                per_image(joined_across, first),
+            ]
+            + [per_image(piece) for piece in joined_pieces[index]]
+            + [whole(piece) for piece in late_pieces]
+            + [small_in, whole(bias_full)]
+            + ([whole(entry) for entry in sums] if last else []),
+            [
+                (x.shape, F32, image_block(tokens, channels, first=first)),
+                new_image((tokens, channels), F32),
+                new_image((tokens, HALF), BF),
+            ]
+            + [new_image(piece_out, BF)] * ways
+            + [new_whole((8, hidden_width), F32), new_whole((32, channels), F32)]
+            + (
+                [new_whole(late_shape, F32)] * ways
+                if last
+                else [new_whole(dims, F32) for dims in matrix_sums]
+            ),
+            ([pltpu.VMEM(dims, F32) for dims in matrix_sums] if last else [])
+            + [
+                pltpu.VMEM((channels, channels), BF),
+                pltpu.VMEM((channels, hidden_width), BF),
+                pltpu.VMEM((hidden_width, channels), BF),
+                pltpu.VMEM((rows, wide, HALF), BF),
+                pltpu.VMEM((tokens, channels), BF),
+                pltpu.VMEM((tokens, channels), BF),
+                pltpu.VMEM((tokens, hidden_width), BF),
+                pltpu.VMEM((tokens, hidden_width), BF),
+                pltpu.VMEM((tokens, channels), BF),
+                pltpu.VMEM((tokens, HALF), BF),
+                pltpu.VMEM((rows, wide, HALF), BF),
+            ]
+            + ([pltpu.VMEM((hidden_width, channels), F32)] if last else []),
+            35,
+            after=(last_result,),
+            alias=(block_out, 0) if last else None,
+        )
+        block_out = results[0]
+        grad_middle.append(results[1])
+        grad_across.append(results[2])
+        grad_pieces.append(exchange(results[3 : 3 + ways]))
+        sums = results[3 + ways :]
+        last_result = results[1]
+    bias_sums, middle_sums = sums[:2]
+    late_seq = tree_sum(exchange(sums[2:]))
+    late_stages = [late_seq] + sum_halves(late_seq)
+
+    grad_normed_pieces = []
+    sums = None
+    qkv_half = (channels, 3 * HALF)
+    half_shard = (shard, 3 * HALF)
+    for index, first in enumerate(halves):
+        last = index == 1
+        results = run_kernel(
+            functools.partial(down_back_kernel, down_dims, ways, first, last),
+            pair,
+            [me_in, mask_in, small_in, qkv_in]
+            + [per_image(entry) for entry in down[index]]
+            + [per_image(piece, first) for piece in normed_pieces]
+            + [per_image(piece) for piece in grad_pieces[index]]
+            + ([whole(entry) for entry in sums] if last else []),
+            [new_image(piece_in, BF)] * ways
+            + [new_whole((80, HALF), F32)]
+            + ([new_whole(half_shard, F32)] * ways if last else [new_whole(qkv_half, F32)]),
+            ([pltpu.VMEM(qkv_half, F32)] if last else [])
+            + [
+                pltpu.VMEM(normed_grid, BF),
+                pltpu.VMEM(mixed_grid, F32),
+                pltpu.VMEM(grid_f32, F32),
+                pltpu.VMEM(mixed_grid, F32),
+                pltpu.VMEM(normed_grid, BF),
+                pltpu.VMEM((wide, HALF), F32),
+            ],
+            28,
+            after=(last_result, late_stages[0]) if last else (last_result,),
+        )
+        grad_normed_pieces.append(exchange(results[:ways]))
+        sums = results[ways:]
+        last_result = sums[0]
+    down_taps = sums[0]
+    down_seq = tree_sum(exchange(sums[1:]))
+    down_core = sum_cores(down_seq)
+
+    across_mixed_grad = []
+    sums = None
+    for index, first in enumerate(halves):
+        last = index == 1
+        results = run_kernel(
+            functools.partial(across_back_kernel, attention_dims, ways, first, last),
+            pair,
+            [
+                me_in,
+                per_image(across_mixed, first),
+                per_image(grad_across[index]),
+                per_image(attended, first),
+                per_image(log_total, first),
+                per_image(keys, first),
+                per_image(values, first),
+                per_image(normed, first),
+                mask_in,
+                small_in,
+            ]
+            + ([whole(entry) for entry in sums] if last else []),
+            [new_image((tokens, 3 * HALF), BF), new_whole((80, HALF), F32)]
+            + ([new_whole(half_shard, F32)] * ways if last else [new_whole(qkv_half, F32)]),
+            ([pltpu.VMEM(qkv_half, F32)] if last else [])
+            + [
+                pltpu.VMEM((HALF, key_rows), F32),
+                pltpu.VMEM((HALF, key_rows), F32),
+                pltpu.VMEM((tokens, HALF), F32),
+            ],
+            45,
+            after=(last_result, late_stages[2], down_seq) if last else (last_result, late_stages[1]),
+        )
+        across_mixed_grad.append(results[0])
+        sums = results[1:]
+        last_result = sums[0]
+    across_taps = sums[0]
+    across_seq = tree_sum(exchange(sums[1:]))
+    across_core = sum_cores(across_seq)
+
+    input_grad = None
+    sums = None
+    for index, first in enumerate(halves):
+        last = index == 1
+        results = run_kernel(
+            functools.partial(final_kernel, (rows, width, wide, wide_part, chunk), ways, last),
+            pair,
+            [
+                me_in,
+                (x, image_block(tokens, channels, first=first)),
+                per_image(grad_middle[index]),
+                per_image(across_mixed_grad[index]),
+            ]
+            + [per_image(piece) for piece in grad_normed_pieces[index]]
+            + [small_in, qkv_in]
+            + (
+                [whole(entry) for entry in (*sums, across_taps, down_taps, middle_sums, bias_sums)]
+                if last
+                else []
+            ),
+            [
+                (x.shape, F32, image_block(tokens, channels, first=first)),
+                new_whole((16, channels), F32),
+            ]
+            + ([new_whole((24, channels), F32)] if last else []),
+            [pltpu.VMEM((rows, wide, channels), BF), pltpu.VMEM((tokens, channels), F32)],
+            8,
+            after=(last_result, across_seq) if last else (last_result, late_stages[-1], down_core),
+            alias=(input_grad, 0) if last else None,
+        )
+        input_grad = results[0]
+        sums = results[1:]
+        last_result = sums[0]
+    small_sum = tree_sum(exchange([results[2]] * ways))
+    small_sum = sum_chips(sum_cores(small_sum))
+    shard_late = join_halves(late_stages[-1])
+    shard_down, shard_across = sum_chips(down_core), sum_chips(across_core)
+
+    squared = sum(jnp.sum(entry * entry) for entry in (shard_late, shard_down, shard_across))
+    squared = tree_sum(exchange([jnp.full((8, 128), squared)] * ways))[0, 0]
+    grad_norm = jnp.sqrt(squared + jnp.sum(small_sum * small_sum))
     factor = CLIP_NORM / jnp.maximum(grad_norm, CLIP_NORM)
-    rates = (RATE_MATRIX, RATE_OUTPUT, RATE_MATRIX, RATE_MATRIX, RATE_SMALL, RATE_MATRIX)
-    decays = (WEIGHT_DECAY, WEIGHT_DECAY, WEIGHT_DECAY, WEIGHT_DECAY, 0.0, 0.0)
-    firsts = (first_qkv, first_out, first_expand, first_shrink, first_small, first_bias)
-    seconds = (second_qkv, second_out, second_expand, second_shrink, second_small, second_bias)
-    updated = [
-        adam_update(
-            params[index],
-            firsts[index],
-            seconds[index],
-            shares[index] * factor,
-            rates[index],
-            decays[index],
-        )
-        for index in range(6)
-    ]
+    matrices = (
+        (qkv_weight, out_weight, expand_weight, shrink_weight)
+        + (first_qkv, first_out, first_expand, first_shrink)
+        + (second_qkv, second_out, second_expand, second_shrink)
+    )
+    updated = run_kernel(
+        functools.partial(update_kernel, blocks),
+        1,
+        [(factor.reshape(1), scalar_block())]
+        + [whole(entry) for entry in (shard_late, shard_across, shard_down, *matrices)],
+        [new_whole(entry.shape, F32) for entry in matrices[:4]] * 3,
+        [],
+        4,
+    )
+    small_rows = small_params.shape[0]
+    small_grad = lax.dynamic_slice_in_dim(
+        small_sum[:small_rows], owner * small_params.shape[1], small_params.shape[1], 1
+    )
+    bias_grad = lax.dynamic_slice_in_dim(
+        small_sum[small_rows : small_rows + blocks].reshape(-1),
+        owner * expand_bias.shape[0],
+        expand_bias.shape[0],
+        0,
+    )
+    small_new = adam_update(
+        small_params, first_small, second_small, small_grad * factor, RATE_SMALL, 0.0
+    )
+    bias_new = adam_update(expand_bias, first_bias, second_bias, bias_grad * factor, RATE_MATRIX, 0.0)
+    outputs = []
+    for part in range(3):
+        outputs += [*updated[4 * part : 4 * part + 4], small_new[part], bias_new[part]]
     return (
         block_out.reshape(images.shape),
         input_grad.reshape(images.shape),
         grad_norm,
-        *(entry[0] for entry in updated),
-        *(entry[1] for entry in updated),
-        *(entry[2] for entry in updated),
+        *outputs,
     )
 
 

time: 676 us -> 533 us (0.79)
  waiting for transfers between devices: 162 us -> 39.2 us
  blocking collectives: 99.6 us -> 0 us
  starting transfers between devices: 14.2 us -> 74.3 us
  Pallas kernels: 350 us -> 378 us
  between operations: 19.6 us -> 5.84 us
    psum x1 -> x0, waiting for transfers between devices: 95.5 us -> none  [on_device(): lax.psum((sum_qkv, sum_out, sum_expand, sum_shrink, sum_small, sum_bias),...]
    ppermute x12 -> x58, starting transfers between devices: 14.1 us -> 74.3 us  [swap(): lax.ppermute(value, axis, [(place, place ^ distance) for place in range(l...]
    all_gather x6 -> x0, blocking collectives: 58.3 us -> none  [the longest x1 11.4 us: on_device(): lax.all_gather(expand_weight.astype(BF), 'seq', axis=0, tiled=True)]
    psum x1 -> x0, blocking collectives: 41.3 us -> none  [on_device(): lax.psum((sum_qkv, sum_out, sum_expand, sum_shrink, sum_small, sum_bias),...]
    pallas_call x7 -> x13, Pallas kernels: 350 us -> 378 us  [run_kernel(): pl.pallas_call(wrapped, grid=(images,), in_specs=[spec for _, spec in inp...]
    ppermute x12 -> x58, waiting for transfers between devices: 66.2 us -> 39.2 us  [swap(): lax.ppermute(value, axis, [(place, place ^ distance) for place in range(l...]
    add x0 -> x11, other arithmetic: none -> 9.75 us  [the longest x5 4.81 us: tree_sum(): values = [values[i] + values[i + 1] for i in range(0, len(values), 2)]]
  transfers between devices with their start and end apart: 13 -> 58, of which waited for: 5 -> 12; matrix products, arithmetic and copies ran while one was open for 0% -> 3% of each run, Pallas kernels for 22% -> 65%
where the time goes in v2:
time: 533 us; the launch traced here: 523 us
  Pallas kernels  378 us (71%)
  starting transfers between devices  74.3 us (14%)
  waiting for transfers between devices  39.2 us (7%)
  other arithmetic  21 us (4%)
  between operations  5.84 us (1%)
    pallas_call x13, Pallas kernels, run_kernel(): pl.pallas_call(wrapped, grid=(images,), in_specs=[spec for _, spec in inp...  378 us
    ppermute x58, starting transfers between devices, swap(): lax.ppermute(value, axis, [(place, place ^ distance) for place in range(l...  74.3 us
    ppermute x58, waiting for transfers between devices, swap(): lax.ppermute(value, axis, [(place, place ^ distance) for place in range(l...  39.2 us
  transfers between devices with their start and end apart: 58, of which 12 were waited for; matrix products, arithmetic and copies ran while one was open for 3% of the time, Pallas kernels for 65%

profile of v2, /device:TPU:0, one launch (start us, length us, event | category | flops | bytes accessed | tf_op | source)
XLA Modules:
  0.0 523.5 jit_solution(7773103417841392284)
XLA Ops:
  3.1 3.0 collective-permute-start
  10.5 2.0 collective-permute-start.10
  14.0 5.6 %collective-permute-done.1.refs_4_ = bf16[80,768]{1,0:T(8,128)(2,1)S(1)} collective-permute-done((bf16[80,768]{1,0:T(8,128)(2,1)S(1)}, bf16[80,768]{1,0:T(8,128)(2,1)S(1)}, u32[]{:S(2)}, u32[]{:S(2)}) %collective-permute-start.1) | collective-permute-done | bytes 122912 | tf_op jit(solution)/shard_map/ppermute | solution.py:938
  20.3 9.4 %shard_map.364 = (bf16[4,1568,384]{2,1,0:T(8,128)(2,1)}, bf16[4,1568,256]{2,1,0:T(8,128)(2,1)}, bf16[4,7,64,256]{3,2,1,0:T(8,128)(2,1)}, bf16[4,7,64,256]{3,2,1,...) custom-call(s32[1]{0:T(128)} %bitcast.refs_0_, ...), custom_call_target="tpu_custom_call" | custom-call | flops 12000000000 | bytes 12000000 | tf_op jit(solution)/shard_map/pallas_call | solution.py:911
  29.8 2.7 collective-permute-start.4
  33.9 56.2 %shard_map.365 = (bf16[4,1568,128]{2,1,0:T(8,128)(2,1)}, f32[4,1568,128]{2,1,0:T(8,128)}, f32[4,1568,128]{2,1,0:T(8,128)}, bf16[4,4,1280,128]{3,2,1,0:T(8,128)(2,1)}, bf16[4,4,1280,128]{3,2,1,0:T(8,128)(2,1)}) custom-call(bf16[4,1568,384]{2,1,0:T(8,128)(2,1)} %get-tuple-element.114.refs_0_.refs_1_, s32[4,224]{1,0:T(4,128)} %refs_8_.4, ...), custom_call_target="tpu_custom_call" | custom-call | flops 60000002048 | bytes 60000000 | tf_op jit(solution)/shard_map/pallas_call | solution.py:911
  91.7 20.7 %shard_map.366 = (bf16[2,7,64,128]{3,2,1,0:T(8,128)(2,1)}, bf16[2,7,64,128]{3,2,1,0:T(8,128)(2,1)}, bf16[2,7,64,128]{3,2,1,0:T(8,128)(2,1)}, bf16[2,7,64,128]{3,...) custom-call(s32[1]{0:T(128)} %bitcast.refs_0_, ...), custom_call_target="tpu_custom_call" | custom-call | flops 17999998976 | bytes 18000000 | tf_op jit(solution)/shard_map/pallas_call | solution.py:911
  113.9 2.0 collective-permute-start.13
  115.9 20.9 %shard_map.367 = (bf16[2,7,64,128]{3,2,1,0:T(8,128)(2,1)}, bf16[2,7,64,128]{3,2,1,0:T(8,128)(2,1)}, bf16[2,7,64,128]{3,2,1,0:T(8,128)(2,1)}, bf16[2,7,64,128]{3,...) custom-call(s32[1]{0:T(128)} %bitcast.refs_0_, ...), custom_call_target="tpu_custom_call" | custom-call | flops 17999998976 | bytes 18000000 | tf_op jit(solution)/shard_map/pallas_call | solution.py:911
  141.1 39.3 %shard_map.368 = (f32[4,1568,256]{2,1,0:T(8,128)}, f32[2,1568,256]{2,1,0:T(8,128)}, bf16[2,1568,128]{2,1,0:T(8,128)(2,1)}, bf16[2,7,64,128]{3,2,1,0:T(8,128)(2,1...) custom-call(s32[1]{0:T(128)} %bitcast.refs_0_, ...), custom_call_target="tpu_custom_call" | custom-call | flops 35000000512 | bytes 35000000 | tf_op jit(solution)/shard_map/pallas_call | solution.py:911
  184.8 41.1 %shard_map.369 = (f32[4,1568,256]{2,1,0:T(8,128)}, f32[2,1568,256]{2,1,0:T(8,128)}, bf16[2,1568,128]{2,1,0:T(8,128)(2,1)}, bf16[2,7,64,128]{3,2,1,0:T(8,128)(2,1...) custom-call(s32[1]{0:T(128)} %bitcast.refs_0_, ...), custom_call_target="tpu_custom_call", output_to_operand_aliasing={{0}: (20, {})} | custom-call | flops 35000000512 | bytes 35000000 | tf_op jit(solution)/shard_map/pallas_call | solution.py:911
  232.9 32.7 %shard_map.370 = (bf16[2,7,64,256]{3,2,1,0:T(8,128)(2,1)}, bf16[2,7,64,256]{3,2,1,0:T(8,128)(2,1)}, bf16[2,7,64,256]{3,2,1,0:T(8,128)(2,1)}, bf16[2,7,64,256]{3,...) custom-call(s32[1]{0:T(128)} %bitcast.refs_0_, s32[4,224]{1,0:T(4,128)} %refs_8_.4, ...), custom_call_target="tpu_custom_call" | custom-call | flops 28000000000 | bytes 28000000 | tf_op jit(solution)/shard_map/pallas_call | solution.py:911
  267.0 5.6 %collective-permute-done.17.refs_14_ = bf16[2,7,64,128]{3,2,1,0:T(8,128)(2,1)S(1)} collective-permute-done((bf16[2,7,64,128]{3,2,1,0:T(8,128)(2,1)S(1)}, bf16[2,7,64,128]{3,2,1,0:T(8,128)(2,1)S(1)}, u32[]{:S(2)}, u32[]{:S(2)}) %collective-permute-start.17) | collective-permute-done | bytes 229408 | tf_op jit(solution)/shard_map/ppermute | solution.py:938
  273.3 32.6 %shard_map.371 = (bf16[2,7,64,256]{3,2,1,0:T(8,128)(2,1)}, bf16[2,7,64,256]{3,2,1,0:T(8,128)(2,1)}, bf16[2,7,64,256]{3,2,1,0:T(8,128)(2,1)}, bf16[2,7,64,256]{3,...) custom-call(s32[1]{0:T(128)} %bitcast.refs_0_, ...), custom_call_target="tpu_custom_call" | custom-call | flops 28000000000 | bytes 28000000 | tf_op jit(solution)/shard_map/pallas_call | solution.py:911
  306.9 2.6 collective-permute-start.28
  316.5 50.4 %shard_map.372 = (bf16[2,1568,384]{2,1,0:T(8,128)(2,1)}, f32[80,128]{1,0:T(8,128)}, f32[256,384]{1,0:T(8,128)}) custom-call(s32[1]{0:T(128)} %bitcast.refs_0_, bf16[4,1568,384]{2,1,0:T(8,128)(2,1)} %get-tuple-element.114.refs_0_.refs_1_, bf16[2,1568,128]{2,1,0:T(8,128)(2,1)} %get-tuple-element.148.refs_2_, ...), custom_call_target="tpu_custom_call" | custom-call | flops 44999999488 | bytes 45000000 | tf_op jit(solution)/shard_map/pallas_call | solution.py:911
  368.6 51.1 %shard_map.373 = (bf16[2,1568,384]{2,1,0:T(8,128)(2,1)}, f32[80,128]{1,0:T(8,128)}, f32[64,384]{1,0:T(8,128)}, f32[64,384]{1,0:T(8,128)}, f32[64,384]{1,0:T(8,128)}, /*index=5*/f32[64,384]{1,0:T(8,128)}) custom-call(s32[1]{0:T(128)} %bitcast.refs_0_, bf16[4,1568,384]{2,1,0:T(8,128)(2,1)} %get-tuple-element.114.refs_0_.refs_1_, ...), custom_call_target="tpu_custom_call" | custom-call | flops 44999999488 | bytes 45000000 | tf_op jit(solution)/shard_map/pallas_call | solution.py:911
  419.7 2.3 collective-permute-start.37
  423.4 2.0 collective-permute-done.37
  425.4 2.6 collective-permute-start.39
  428.0 2.6 collective-permute-start.35
  434.4 8.8 %collective-permute-done.35 = f32[32,2304]{1,0:T(8,128)S(1)} collective-permute-done((f32[32,2304]{1,0:T(8,128)S(1)}, f32[32,2304]{1,0:T(8,128)S(1)}, u32[]{:S(2)}, u32[]{:S(2)}) %collective-permute-start.35) | collective-permute-done | bytes 294944 | tf_op jit(solution)/shard_map/ppermute | solution.py:938
  446.1 9.9 %shard_map.374 = (f32[4,1568,256]{2,1,0:T(8,128)}, f32[16,256]{1,0:T(8,128)}) custom-call(s32[1]{0:T(128)} %bitcast.refs_0_, bf16[4,1568,256]{2,1,0:T(8,128)(2,1)} %bitcast.16, f32[2,1568,256]{2,1,0:T(8,128)} %get-tuple-element.139.refs_19_.refs_2_, bf16[2,1568,384]{2,1,0:T(8,128)(2,1)} %get-tuple-element.179.refs_3_, ...), custom_call_target="tpu_custom_call" | custom-call | flops 8000000000 | bytes 8000000 | tf_op jit(solution)/shard_map/pallas_call | solution.py:911
  456.1 8.8 %collective-permute-done.30.refs_6_ = bf16[2,7,64,256]{3,2,1,0:T(8,128)(2,1)} collective-permute-done((bf16[2,7,64,256]{3,2,1,0:T(8,128)(2,1)S(1)}, bf16[2,7,64,256]{3,2,1,0:T(8,128)(2,1)}, u32[]{:S(2)}, u32[]{:S(2)}) %collective-permute-start.30) | collective-permute-done | bytes 458784 | tf_op jit(solution)/shard_map/ppermute | solution.py:938
  465.7 10.1 %shard_map.375 = (f32[4,1568,256]{2,1,0:T(8,128)}, f32[16,256]{1,0:T(8,128)}, f32[24,256]{1,0:T(8,128)}) custom-call(s32[1]{0:T(128)} %bitcast.refs_0_, bf16[4,1568,256]{2,1,0:T(8,128)(2,1)} %bitcast.17, f32[2,1568,256]{2,1,0:T(8,128)} %get-tuple-element.142.refs_15_.refs_2_, ...), custom_call_target="tpu_custom_call", output_to_operand_aliasing={{0}: (17, {})} | custom-call | flops 8000000000 | bytes 8000000 | tf_op jit(solution)/shard_map/pallas_call | solution.py:911
  477.3 2.1 collective-permute-start.53
  480.2 3.4 collective-permute-start.42
  485.2 3.8 collective-permute-start.46
  490.0 2.1 collective-permute-done.42
  493.9 4.7 collective-permute-start.55
  510.9 2.2 collective-permute-start.50
  518.7 3.4 shard_map.376
  (220 shorter events, 70.6 us)
Async XLA Ops:
  10.5 105.4 %collective-permute-start.10 = (bf16[64,2304]{1,0:T(8,128)(2,1)S(1)}, bf16[64,2304]{1,0:T(8,128)(2,1)S(1)}, u32[]{:S(2)}, u32[]{:S(2)}) collective-permute-start(bf16[64,2304]{1,0:T(8,128)(2,1)S(1)} %slice_dynamic-update-slice_fusion.refs_8_), channel_id=1, source_target_pairs={{0,2},{1,3},{2,0},{3,1},{4,6},{5,7},{6,4},{7,5},{8,10},{9,11},{10,... | collective-permute-start | bytes 884744 | tf_op jit(solution)/shard_map/ppermute | solution.py:938
  12.5 124.3 %collective-permute-start.11 = (bf16[64,2304]{1,0:T(8,128)(2,1)S(1)}, bf16[64,2304]{1,0:T(8,128)(2,1)S(1)}, u32[]{:S(2)}, u32[]{:S(2)}) collective-permute-start(bf16[64,2304]{1,0:T(8,128)(2,1)S(1)} %slice_dynamic-update-slice_fusion.refs_8_), channel_id=1, source_target_pairs={{0,3},{1,2},{2,1},{3,0},{4,7},{5,6},{6,5},{7,4},{8,11},{9,10},{10,... | collective-permute-start | bytes 884744 | tf_op jit(solution)/shard_map/ppermute | solution.py:938
  29.7 60.3 %collective-permute-start.3 = (bf16[4,7,64,256]{3,2,1,0:T(8,128)(2,1)}, bf16[4,7,64,256]{3,2,1,0:T(8,128)(2,1)S(1)}, u32[]{:S(2)}, u32[]{:S(2)}) collective-permute-start(bf16[4,7,64,256]{3,2,1,0:T(8,128)(2,1)} %get-tuple-element.119), channel_id=1, source_target_pairs={{0,1},{1,0},{2,3},{3,2},{4,5},{5,4},{6,7},{7,6},{8,9},{9,8},{10,11... | collective-permute-start | bytes 2752520 | tf_op jit(solution)/shard_map/ppermute | solution.py:938
  29.8 60.9 %collective-permute-start.4 = (bf16[4,7,64,256]{3,2,1,0:T(8,128)(2,1)}, bf16[4,7,64,256]{3,2,1,0:T(8,128)(2,1)S(1)}, u32[]{:S(2)}, u32[]{:S(2)}) collective-permute-start(bf16[4,7,64,256]{3,2,1,0:T(8,128)(2,1)} %get-tuple-element.120), channel_id=1, source_target_pairs={{0,2},{1,3},{2,0},{3,1},{4,6},{5,7},{6,4},{7,5},{8,10},{9,11},{10,... | collective-permute-start | bytes 2752520 | tf_op jit(solution)/shard_map/ppermute | solution.py:938
  32.5 58.2 %collective-permute-start.5 = (bf16[4,7,64,256]{3,2,1,0:T(8,128)(2,1)}, bf16[4,7,64,256]{3,2,1,0:T(8,128)(2,1)}, u32[]{:S(2)}, u32[]{:S(2)}) collective-permute-start(bf16[4,7,64,256]{3,2,1,0:T(8,128)(2,1)} %get-tuple-element.121), channel_id=1, source_target_pairs={{0,3},{1,2},{2,1},{3,0},{4,7},{5,6},{6,5},{7,4},{8,11},{9,10},{10,... | collective-permute-start | bytes 2752520 | tf_op jit(solution)/shard_map/ppermute | solution.py:938
  90.1 48.3 %collective-permute-start.9 = (bf16[64,2304]{1,0:T(8,128)(2,1)S(1)}, bf16[64,2304]{1,0:T(8,128)(2,1)S(1)}, u32[]{:S(2)}, u32[]{:S(2)}) collective-permute-start(bf16[64,2304]{1,0:T(8,128)(2,1)S(1)} %slice_dynamic-update-slice_fusion.refs_8_), channel_id=1, source_target_pairs={{0,1},{1,0},{2,3},{3,2},{4,5},{5,4},{6,7},{7,6},{8,9},{9,8},{10,11... | collective-permute-start | bytes 884744 | tf_op jit(solution)/shard_map/ppermute | solution.py:938
  112.4 27.9 %collective-permute-start.12 = (bf16[2,7,64,128]{3,2,1,0:T(8,128)(2,1)}, bf16[2,7,64,128]{3,2,1,0:T(8,128)(2,1)S(1)}, u32[]{:S(2)}, u32[]{:S(2)}) collective-permute-start(bf16[2,7,64,128]{3,2,1,0:T(8,128)(2,1)} %get-tuple-element.130), channel_id=1, source_target_pairs={{0,1},{1,0},{2,3},{3,2},{4,5},{5,4},{6,7},{7,6},{8,9},{9,8},{10,11... | collective-permute-start | bytes 688136 | tf_op jit(solution)/shard_map/ppermute | solution.py:938
  113.9 26.5 %collective-permute-start.13 = (bf16[2,7,64,128]{3,2,1,0:T(8,128)(2,1)}, bf16[2,7,64,128]{3,2,1,0:T(8,128)(2,1)S(1)}, u32[]{:S(2)}, u32[]{:S(2)}) collective-permute-start(bf16[2,7,64,128]{3,2,1,0:T(8,128)(2,1)} %get-tuple-element.131), channel_id=1, source_target_pairs={{0,2},{1,3},{2,0},{3,1},{4,6},{5,7},{6,4},{7,5},{8,10},{9,11},{10,... | collective-permute-start | bytes 688136 | tf_op jit(solution)/shard_map/ppermute | solution.py:938
  115.9 24.5 %collective-permute-start.14 = (bf16[2,7,64,128]{3,2,1,0:T(8,128)(2,1)}, bf16[2,7,64,128]{3,2,1,0:T(8,128)(2,1)S(1)}, u32[]{:S(2)}, u32[]{:S(2)}) collective-permute-start(bf16[2,7,64,128]{3,2,1,0:T(8,128)(2,1)} %get-tuple-element.132), channel_id=1, source_target_pairs={{0,3},{1,2},{2,1},{3,0},{4,7},{5,6},{6,5},{7,4},{8,11},{9,10},{10,... | collective-permute-start | bytes 688136 | tf_op jit(solution)/shard_map/ppermute | solution.py:938
  136.8 47.1 %collective-permute-start.6 = (bf16[2,7,64,128]{3,2,1,0:T(8,128)(2,1)}, bf16[2,7,64,128]{3,2,1,0:T(8,128)(2,1)S(1)}, u32[]{:S(2)}, u32[]{:S(2)}) collective-permute-start(bf16[2,7,64,128]{3,2,1,0:T(8,128)(2,1)} %get-tuple-element.125), channel_id=1, source_target_pairs={{0,1},{1,0},{2,3},{3,2},{4,5},{5,4},{6,7},{7,6},{8,9},{9,8},{10,11... | collective-permute-start | bytes 688136 | tf_op jit(solution)/shard_map/ppermute | solution.py:938
  138.3 45.7 %collective-permute-start.7 = (bf16[2,7,64,128]{3,2,1,0:T(8,128)(2,1)}, bf16[2,7,64,128]{3,2,1,0:T(8,128)(2,1)S(1)}, u32[]{:S(2)}, u32[]{:S(2)}) collective-permute-start(bf16[2,7,64,128]{3,2,1,0:T(8,128)(2,1)} %get-tuple-element.126), channel_id=1, source_target_pairs={{0,2},{1,3},{2,0},{3,1},{4,6},{5,7},{6,4},{7,5},{8,10},{9,11},{10,... | collective-permute-start | bytes 688136 | tf_op jit(solution)/shard_map/ppermute | solution.py:938
  140.3 43.7 %collective-permute-start.8 = (bf16[2,7,64,128]{3,2,1,0:T(8,128)(2,1)}, bf16[2,7,64,128]{3,2,1,0:T(8,128)(2,1)S(1)}, u32[]{:S(2)}, u32[]{:S(2)}) collective-permute-start(bf16[2,7,64,128]{3,2,1,0:T(8,128)(2,1)} %get-tuple-element.127), channel_id=1, source_target_pairs={{0,3},{1,2},{2,1},{3,0},{4,7},{5,6},{6,5},{7,4},{8,11},{9,10},{10,... | collective-permute-start | bytes 688136 | tf_op jit(solution)/shard_map/ppermute | solution.py:938
  180.4 49.0 %collective-permute-start.18 = (bf16[2,7,64,128]{3,2,1,0:T(8,128)(2,1)}, bf16[2,7,64,128]{3,2,1,0:T(8,128)(2,1)S(1)}, u32[]{:S(2)}, u32[]{:S(2)}) collective-permute-start(bf16[2,7,64,128]{3,2,1,0:T(8,128)(2,1)} %get-tuple-element.158), channel_id=1, source_target_pairs={{0,1},{1,0},{2,3},{3,2},{4,5},{5,4},{6,7},{7,6},{8,9},{9,8},{10,11... | collective-permute-start | bytes 688136 | tf_op jit(solution)/shard_map/ppermute | solution.py:938
  182.0 47.5 %collective-permute-start.19 = (bf16[2,7,64,128]{3,2,1,0:T(8,128)(2,1)}, bf16[2,7,64,128]{3,2,1,0:T(8,128)(2,1)S(1)}, u32[]{:S(2)}, u32[]{:S(2)}) collective-permute-start(bf16[2,7,64,128]{3,2,1,0:T(8,128)(2,1)} %get-tuple-element.159), channel_id=1, source_target_pairs={{0,2},{1,3},{2,0},{3,1},{4,6},{5,7},{6,4},{7,5},{8,10},{9,11},{10,... | collective-permute-start | bytes 688136 | tf_op jit(solution)/shard_map/ppermute | solution.py:938
  183.9 47.0 %collective-permute-start.20 = (bf16[2,7,64,128]{3,2,1,0:T(8,128)(2,1)}, bf16[2,7,64,128]{3,2,1,0:T(8,128)(2,1)S(1)}, u32[]{:S(2)}, u32[]{:S(2)}) collective-permute-start(bf16[2,7,64,128]{3,2,1,0:T(8,128)(2,1)} %get-tuple-element.160), channel_id=1, source_target_pairs={{0,3},{1,2},{2,1},{3,0},{4,7},{5,6},{6,5},{7,4},{8,11},{9,10},{10,... | collective-permute-start | bytes 688136 | tf_op jit(solution)/shard_map/ppermute | solution.py:938
  225.9 39.7 %collective-permute-start.21 = (f32[64,2304]{1,0:T(8,128)}, f32[64,2304]{1,0:T(8,128)S(1)}, u32[]{:S(2)}, u32[]{:S(2)}) collective-permute-start(f32[64,2304]{1,0:T(8,128)} %get-tuple-element.164), channel_id=1, source_target_pairs={{0,1},{1,0},{2,3},{3,2},{4,5},{5,4},{6,7},{7,6},{8,9},{9,8},{10,11... | collective-permute-start | bytes 1769480 | tf_op jit(solution)/shard_map/ppermute | solution.py:938
  227.4 38.6 %collective-permute-start.22 = (f32[64,2304]{1,0:T(8,128)}, f32[64,2304]{1,0:T(8,128)S(1)}, u32[]{:S(2)}, u32[]{:S(2)}) collective-permute-start(f32[64,2304]{1,0:T(8,128)} %get-tuple-element.165), channel_id=1, source_target_pairs={{0,2},{1,3},{2,0},{3,1},{4,6},{5,7},{6,4},{7,5},{8,10},{9,11},{10,... | collective-permute-start | bytes 1769480 | tf_op jit(solution)/shard_map/ppermute | solution.py:938
  229.4 36.6 %collective-permute-start.23 = (f32[64,2304]{1,0:T(8,128)}, f32[64,2304]{1,0:T(8,128)S(1)}, u32[]{:S(2)}, u32[]{:S(2)}) collective-permute-start(f32[64,2304]{1,0:T(8,128)} %get-tuple-element.166), channel_id=1, source_target_pairs={{0,3},{1,2},{2,1},{3,0},{4,7},{5,6},{6,5},{7,4},{8,11},{9,10},{10,... | collective-permute-start | bytes 1769480 | tf_op jit(solution)/shard_map/ppermute | solution.py:938
  229.5 37.5 %collective-permute-start.15 = (bf16[2,7,64,128]{3,2,1,0:T(8,128)(2,1)}, bf16[2,7,64,128]{3,2,1,0:T(8,128)(2,1)S(1)}, u32[]{:S(2)}, u32[]{:S(2)}) collective-permute-start(bf16[2,7,64,128]{3,2,1,0:T(8,128)(2,1)} %get-tuple-element.152), channel_id=1, source_target_pairs={{0,1},{1,0},{2,3},{3,2},{4,5},{5,4},{6,7},{7,6},{8,9},{9,8},{10,11... | collective-permute-start | bytes 688136 | tf_op jit(solution)/shard_map/ppermute | solution.py:938
  230.9 36.0 %collective-permute-start.16 = (bf16[2,7,64,128]{3,2,1,0:T(8,128)(2,1)}, bf16[2,7,64,128]{3,2,1,0:T(8,128)(2,1)S(1)}, u32[]{:S(2)}, u32[]{:S(2)}) collective-permute-start(bf16[2,7,64,128]{3,2,1,0:T(8,128)(2,1)} %get-tuple-element.153), channel_id=1, source_target_pairs={{0,2},{1,3},{2,0},{3,1},{4,6},{5,7},{6,4},{7,5},{8,10},{9,11},{10,... | collective-permute-start | bytes 688136 | tf_op jit(solution)/shard_map/ppermute | solution.py:938
  309.7 135.0 %collective-permute-start.32 = (bf16[2,7,64,256]{3,2,1,0:T(8,128)(2,1)S(1)}, bf16[2,7,64,256]{3,2,1,0:T(8,128)(2,1)S(1)}, u32[]{:S(2)}, u32[]{:S(2)}) collective-permute-start(bf16[2,7,64,256]{3,2,1,0:T(8,128)(2,1)S(1)} %copy-done.18), channel_id=1, source_target_pairs={{0,1},{1,0},{2,3},{3,2},{4,5},{5,4},{6,7},{7,6},{8,9},{9,8},{10,11... | collective-permute-start | bytes 1376264 | tf_op jit(solution)/shard_map/ppermute | solution.py:938
  310.9 135.2 %collective-permute-start.33 = (bf16[2,7,64,256]{3,2,1,0:T(8,128)(2,1)S(1)}, bf16[2,7,64,256]{3,2,1,0:T(8,128)(2,1)}, u32[]{:S(2)}, u32[]{:S(2)}) collective-permute-start(bf16[2,7,64,256]{3,2,1,0:T(8,128)(2,1)S(1)} %copy-done.17), channel_id=1, source_target_pairs={{0,2},{1,3},{2,0},{3,1},{4,6},{5,7},{6,4},{7,5},{8,10},{9,11},{10,... | collective-permute-start | bytes 1376264 | tf_op jit(solution)/shard_map/ppermute | solution.py:938
  311.5 134.6 %collective-permute-start.34 = (bf16[2,7,64,256]{3,2,1,0:T(8,128)(2,1)S(1)}, bf16[2,7,64,256]{3,2,1,0:T(8,128)(2,1)}, u32[]{:S(2)}, u32[]{:S(2)}) collective-permute-start(bf16[2,7,64,256]{3,2,1,0:T(8,128)(2,1)S(1)} %copy-done.16), channel_id=1, source_target_pairs={{0,3},{1,2},{2,1},{3,0},{4,7},{5,6},{6,5},{7,4},{8,11},{9,10},{10,... | collective-permute-start | bytes 1376264 | tf_op jit(solution)/shard_map/ppermute | solution.py:938
  314.8 107.2 %collective-permute-start.36 = (f32[64,384]{1,0:T(8,128)}, f32[64,384]{1,0:T(8,128)S(1)}, u32[]{:S(2)}, u32[]{:S(2)}) collective-permute-start(f32[64,384]{1,0:T(8,128)} %add_add_fusion.4.refs_14_), channel_id=1, source_target_pairs={{0,4},{4,0},{8,12},{12,8},{16,20},{20,16},{24,28},{28,24},{1,5},{5... | collective-permute-start | bytes 294920 | tf_op jit(solution)/shard_map/ppermute | solution.py:938
  314.8 52.0 %collective-permute-start.25 = (f32[32,2304]{1,0:T(8,128)S(1)}, f32[32,2304]{1,0:T(8,128)S(1)}, u32[]{:S(2)}, u32[]{:S(2)}) collective-permute-start(f32[32,2304]{1,0:T(8,128)S(1)} %dynamic-slice_add_fusion.refs_11_), channel_id=1, source_target_pairs={{0,8},{4,12},{8,0},{12,4},{16,24},{20,28},{24,16},{28,20},{1,9},{5... | collective-permute-start | bytes 884744 | tf_op jit(solution)/shard_map/ppermute | solution.py:938
  428.0 15.3 %collective-permute-start.35 = (f32[32,2304]{1,0:T(8,128)S(1)}, f32[32,2304]{1,0:T(8,128)S(1)}, u32[]{:S(2)}, u32[]{:S(2)}) collective-permute-start(f32[32,2304]{1,0:T(8,128)S(1)} %copy-done.1), channel_id=1, source_target_pairs={{0,16},{4,20},{8,24},{12,28},{16,0},{20,4},{24,8},{28,12},{1,17},{... | collective-permute-start | bytes 884744 | tf_op jit(solution)/shard_map/ppermute | solution.py:938
  432.1 24.0 %collective-permute-start.29 = (bf16[2,7,64,256]{3,2,1,0:T(8,128)(2,1)S(1)}, bf16[2,7,64,256]{3,2,1,0:T(8,128)(2,1)}, u32[]{:S(2)}, u32[]{:S(2)}) collective-permute-start(bf16[2,7,64,256]{3,2,1,0:T(8,128)(2,1)S(1)} %copy-done.21), channel_id=1, source_target_pairs={{0,1},{1,0},{2,3},{3,2},{4,5},{5,4},{6,7},{7,6},{8,9},{9,8},{10,11... | collective-permute-start | bytes 1376264 | tf_op jit(solution)/shard_map/ppermute | solution.py:938
  443.2 21.7 %collective-permute-start.30 = (bf16[2,7,64,256]{3,2,1,0:T(8,128)(2,1)S(1)}, bf16[2,7,64,256]{3,2,1,0:T(8,128)(2,1)}, u32[]{:S(2)}, u32[]{:S(2)}) collective-permute-start(bf16[2,7,64,256]{3,2,1,0:T(8,128)(2,1)S(1)} %copy-done.20), channel_id=1, source_target_pairs={{0,2},{1,3},{2,0},{3,1},{4,6},{5,7},{6,4},{7,5},{8,10},{9,11},{10,... | collective-permute-start | bytes 1376264 | tf_op jit(solution)/shard_map/ppermute | solution.py:938
  444.6 20.3 %collective-permute-start.31 = (bf16[2,7,64,256]{3,2,1,0:T(8,128)(2,1)S(1)}, bf16[2,7,64,256]{3,2,1,0:T(8,128)(2,1)S(1)}, u32[]{:S(2)}, u32[]{:S(2)}) collective-permute-start(bf16[2,7,64,256]{3,2,1,0:T(8,128)(2,1)S(1)} %copy-done.19), channel_id=1, source_target_pairs={{0,3},{1,2},{2,1},{3,0},{4,7},{5,6},{6,5},{7,4},{8,11},{9,10},{10,... | collective-permute-start | bytes 1376264 | tf_op jit(solution)/shard_map/ppermute | solution.py:938
  446.1 34.1 %collective-permute-start.44 = (f32[64,384]{1,0:T(8,128)}, f32[64,384]{1,0:T(8,128)S(1)}, u32[]{:S(2)}, u32[]{:S(2)}) collective-permute-start(f32[64,384]{1,0:T(8,128)} %add_add_fusion.3.refs_16_), channel_id=1, source_target_pairs={{0,4},{4,0},{8,12},{12,8},{16,20},{20,16},{24,28},{28,24},{1,5},{5... | collective-permute-start | bytes 294920 | tf_op jit(solution)/shard_map/ppermute | solution.py:938
  484.8 13.8 %collective-permute-start.45 = (f32[64,384]{1,0:T(8,128)S(1)}, f32[64,384]{1,0:T(8,128)S(1)}, u32[]{:S(2)}, u32[]{:S(2)}) collective-permute-start(f32[64,384]{1,0:T(8,128)S(1)} %add.170), channel_id=1, source_target_pairs={{0,8},{4,12},{8,0},{12,4},{16,24},{20,28},{24,16},{28,20},{1,9},{5... | collective-permute-start | bytes 294920 | tf_op jit(solution)/shard_map/ppermute | solution.py:938
  485.2 14.6 %collective-permute-start.46 = (f32[64,384]{1,0:T(8,128)S(1)}, f32[64,384]{1,0:T(8,128)S(1)}, u32[]{:S(2)}, u32[]{:S(2)}) collective-permute-start(f32[64,384]{1,0:T(8,128)S(1)} %add.170), channel_id=1, source_target_pairs={{0,16},{4,20},{8,24},{12,28},{16,0},{20,4},{24,8},{28,12},{1,17},{... | collective-permute-start | bytes 294920 | tf_op jit(solution)/shard_map/ppermute | solution.py:938
  (69 other events, 1135.5 us)

commit v3 on v2

--- a/solution.py
+++ b/solution.py
@@ -33,6 +33,7 @@
 SCALE = HEAD_DIM**-0.5
 GROUP = 8
 MASKED = -1e38
+EXPONENT_SCALE = SCALE * LOG2E
 EXPONENT_BOUND = 60.0
 VMEM_LIMIT = 60 * 2**20
 
@@ -94,68 +95,51 @@
     return first, second, (rest - second).astype(BF).astype(F32)
 
 
-def lane_place(rows, head):
-    lane = iota((rows, HALF), 1)
-    return ((lane >> 5) - head) & 3
+def lane_head(rows):
+    return (iota((rows, HALF), 1) >> 5) & 3
 
 
 def lane_sub(rows):
     return iota((rows, HALF), 1) & 31
 
 
-def head_key(keys, keys_rolled, bias, head):
-    rows = keys.shape[0]
-    place, sub = lane_place(rows, head), lane_sub(rows)
+def piece_lanes(values, fourth):
+    one, two, three = pieces_of(values)
+    sub = lane_sub(values.shape[0])
+    return jnp.where(
+        sub == 0, one, jnp.where(sub == 1, two, jnp.where(sub == 2, three, jnp.where(sub == 3, fourth, 0.0)))
+    )
+
+
+def wide_keys(keys, bias):
+    sub = lane_sub(keys.shape[0])
     extra = jnp.where(sub < 3, 1.0, jnp.where(sub == 3, bias, 0.0))
-    return jnp.where(
-        place == 0, keys, jnp.where(place == 1, keys_rolled, jnp.where(place == 2, extra, 0.0))
-    ).astype(BF)
-
-
-def head_value(values, head):
-    place = lane_place(values.shape[0], head)
-    return jnp.where(place == 0, values, jnp.where(place == 1, 1.0, 0.0)).astype(BF)
-
-
-def query_parts(queries, shift):
-    rows = queries.shape[0]
-    scaled = queries * (SCALE * LOG2E)
-    high = scaled.astype(BF).astype(F32)
-    low = pltpu.roll(scaled - high, HEAD_DIM, 1)
-    one, two, three = pieces_of(-pltpu.roll(shift, 2 * HEAD_DIM, 1))
-    sub = lane_sub(rows)
-    extra = jnp.where(
-        sub == 0,
-        one,
-        jnp.where(sub == 1, two, jnp.where(sub == 2, three, jnp.where(sub == 3, 1.0, 0.0))),
-    )
-    return high, low, extra
-
-
-def head_query(parts, head):
-    high, low, extra = parts
-    place = lane_place(high.shape[0], head)
-    return jnp.where(
-        place == 0, high, jnp.where(place == 1, low, jnp.where(place == 2, extra, 0.0))
-    ).astype(BF)
-
-
-def grad_parts(grad, attended):
-    rows = grad.shape[0]
-    product = grad * attended
-    block = one_hot((iota((HALF, HALF), 0) >> 5) == (iota((HALF, HALF), 1) >> 5))
-    first, second, third = pieces_of(product)
-    inner = dot(first.astype(BF), block) + dot(second.astype(BF), block) + dot(third.astype(BF), block)
-    one, two, three = pieces_of(-pltpu.roll(inner, HEAD_DIM, 1))
-    sub = lane_sub(rows)
-    extra = jnp.where(sub == 0, one, jnp.where(sub == 1, two, jnp.where(sub == 2, three, 0.0)))
-    return grad, extra
-
-
-def head_grad(parts, head):
-    grad, extra = parts
-    place = lane_place(grad.shape[0], head)
-    return jnp.where(place == 0, grad, jnp.where(place == 1, extra, 0.0)).astype(BF)
+    return jnp.concatenate([keys.astype(BF), extra.astype(BF)], axis=1)
+
+
+def wide_values(values):
+    return jnp.concatenate([values.astype(BF), jnp.ones(values.shape, BF)], axis=1)
+
+
+def stack_heads(left, right):
+    head_of = lane_head(left.shape[0])
+    parts = []
+    for head in range(BRANCH_HEADS):
+        mine = head_of == head
+        parts.append(
+            jnp.concatenate(
+                [jnp.where(mine, left, 0.0).astype(BF), jnp.where(mine, right, 0.0).astype(BF)], axis=1
+            )
+        )
+    return jnp.concatenate(parts, axis=0)
+
+
+def pick_heads(stacked, rows):
+    head_of = lane_head(rows)
+    picked = stacked[:rows]
+    for head in range(1, BRANCH_HEADS):
+        picked = jnp.where(head_of == head, stacked[head * rows : (head + 1) * rows], picked)
+    return picked
 
 
 def head_norms(values):
@@ -169,54 +153,45 @@
     return jnp.logical_not(bound <= EXPONENT_BOUND * EXPONENT_BOUND)
 
 
-def attend_heads(query_rows, shift, keys_of, values_of):
-    rows = query_rows.shape[0]
-    parts = query_parts(query_rows, shift)
-    attended = jnp.zeros((rows, HALF), F32)
-    log_total = jnp.zeros((rows, HALF), F32)
-    for head in range(BRANCH_HEADS):
-        scores = dot_nt(head_query(parts, head), keys_of(head))
-        weights = jnp.exp2(scores).astype(BF)
-        result = dot(weights, values_of(head))
-        totals = pltpu.roll(result, HALF - HEAD_DIM, 1)
-        mine = lane_place(rows, head) == 0
-        attended = jnp.where(mine, result / totals, attended)
-        log_total = jnp.where(mine, jnp.log(totals) * LOG2E + shift, log_total)
-    return attended, log_total
-
-
-def highest_scores(query_rows, keys_of):
-    rows = query_rows.shape[0]
-    parts = query_parts(query_rows, jnp.zeros((rows, HALF), F32))
-    shift = jnp.zeros((rows, HALF), F32)
-    for head in range(BRANCH_HEADS):
-        scores = dot_nt(head_query(parts, head), keys_of(head))
-        highest = jnp.max(scores, axis=-1, keepdims=True)
-        shift = jnp.where(lane_place(rows, head) == 0, highest, shift)
-    return shift
-
-
-def attend_heads_back(query_rows, grad_rows, attended, log_total, keys_of, values_of):
-    rows = query_rows.shape[0]
+def stack_queries(queries, shift):
+    return stack_heads(queries, piece_lanes(shift * (-1.0 / EXPONENT_SCALE), 1.0))
+
+
+def attend_heads(queries, shift, keys, values):
+    rows = queries.shape[0]
+    scores = dot_nt(stack_queries(queries, shift), keys)
+    weights = jnp.exp2(scores * EXPONENT_SCALE).astype(BF)
+    result = dot(weights, values)
+    totals = pick_heads(result[:, HALF:], rows)
+    return pick_heads(result[:, :HALF], rows) / totals, jnp.log(totals) * LOG2E + shift
+
+
+def highest_scores(queries, keys):
+    rows = queries.shape[0]
+    scores = dot_nt(stack_queries(queries, jnp.zeros((rows, HALF), F32)), keys)
+    highest = jnp.max(scores, axis=-1, keepdims=True) * EXPONENT_SCALE
+    return pick_heads(jnp.broadcast_to(highest, (BRANCH_HEADS * rows, HALF)), rows)
+
+
+def attend_heads_back(queries, grad, attended, log_total, keys, values):
+    rows = queries.shape[0]
     eye = one_hot(iota((HALF, HALF), 0) == iota((HALF, HALF), 1))
-    query_turned = dot_nt(eye, query_rows.astype(BF)).astype(BF)
-    grad_turned = dot_nt(eye, grad_rows.astype(BF)).astype(BF)
-    parts = query_parts(query_rows, log_total)
-    back_parts = grad_parts(grad_rows, attended)
-    grad_queries = jnp.zeros((rows, HALF), F32)
+    query_turned = dot_nt(eye, queries.astype(BF)).astype(BF)
+    grad_turned = dot_nt(eye, grad.astype(BF)).astype(BF)
+    block = one_hot((iota((HALF, HALF), 0) >> 5) == (iota((HALF, HALF), 1) >> 5))
+    inner = sum(dot(piece.astype(BF), block) for piece in pieces_of(grad * attended))
+    weights = jnp.exp2(dot_nt(stack_queries(queries, log_total), keys) * EXPONENT_SCALE)
+    weights_low = weights.astype(BF)
+    grad_weights = dot_nt(stack_heads(grad, piece_lanes(-inner, 0.0)), values)
+    grad_scores = (weights * grad_weights).astype(BF)
+    grad_queries = pick_heads(dot(grad_scores, keys[:, :HALF]), rows) * SCALE
     grad_keys, grad_values = [], []
     for head in range(BRANCH_HEADS):
-        keys, values = keys_of(head), values_of(head)
-        weights = jnp.exp2(dot_nt(head_query(parts, head), keys))
-        weights_low = weights.astype(BF)
-        grad_weights = dot_nt(head_grad(back_parts, head), values)
-        grad_scores = (weights * grad_weights).astype(BF)
         lanes = slice(head * HEAD_DIM, (head + 1) * HEAD_DIM)
-        grad_values.append(dot(grad_turned[lanes], weights_low))
-        grad_keys.append(dot(query_turned[lanes], grad_scores))
-        mine = lane_place(rows, head) == 0
-        grad_queries = jnp.where(mine, dot(grad_scores, keys), grad_queries)
-    return grad_queries * SCALE, grad_keys, grad_values
+        span = slice(head * rows, (head + 1) * rows)
+        grad_values.append(dot(grad_turned[lanes], weights_low[span]))
+        grad_keys.append(dot(query_turned[lanes], grad_scores[span]))
+    return grad_queries, grad_keys, grad_values
 
 
 def shift_down(values):
@@ -313,21 +288,15 @@
     key_norms = jnp.zeros((1, HALF), F32)
     for row in range(rows):
         picked = dot(select, across_ref[0, row * width : (row + 1) * width, HALF:])
-        keys, values = picked[:, :HALF], picked[:, HALF:]
-        rolled = pltpu.roll(keys, HEAD_DIM, 1)
-        key_norms = jnp.maximum(key_norms, head_norms(keys))
+        key_norms = jnp.maximum(key_norms, head_norms(picked[:, :HALF]))
         span = slice(row * kept, (row + 1) * kept)
-        for head in range(BRANCH_HEADS):
-            keys_ref[0, head, span] = head_key(keys, rolled, bias, head)
-            values_ref[0, head, span] = head_value(values, head)
+        keys_ref[0, span] = wide_keys(picked[:, :HALF], bias)
+        values_ref[0, span] = wide_values(picked[:, HALF:])
     spare = key_rows - rows * kept
     if spare:
         nothing = jnp.zeros((spare, HALF), F32)
-        for head in range(BRANCH_HEADS):
-            keys_ref[0, head, rows * kept :] = head_key(
-                nothing, nothing, jnp.full((spare, HALF), MASKED, F32), head
-            )
-            values_ref[0, head, rows * kept :] = nothing.astype(BF)
+        keys_ref[0, rows * kept :] = wide_keys(nothing, nothing + MASKED)
+        values_ref[0, rows * kept :] = wide_values(nothing)
 
     query_norms = head_norms(across_ref[0, :, :HALF].astype(F32) * (SCALE * LOG2E))
     large = exceeds(query_norms, key_norms)
@@ -338,18 +307,12 @@
 
     def rows_of(step):
         return pl.ds(pl.multiple_of(step * chunk, 16), chunk)
-
-    def keys_of(head):
-        return keys_ref[0, head]
-
-    def values_of(head):
-        return values_ref[0, head]
 
     @pl.when(large)
     def _():
         def highest(step, carry):
             span = rows_of(step)
-            shift_ref[span] = highest_scores(across_ref[0, span, :HALF].astype(F32), keys_of)
+            shift_ref[span] = highest_scores(across_ref[0, span, :HALF].astype(F32), keys_ref[0])
             return carry
 
         lax.fori_loop(0, tokens // chunk, highest, 0)
@@ -357,13 +320,13 @@
     def attend(step, carry):
         span = rows_of(step)
         attended, log_total = attend_heads(
-            across_ref[0, span, :HALF].astype(F32), shift_ref[span], keys_of, values_of
+            across_ref[0, span, :HALF].astype(F32), shift_ref[span], keys_ref[0], values_ref[0]
         )
         attended_ref[0, span] = attended
         total_ref[0, span] = log_total
         return carry
 
-    lax.fori_loop(0, tokens // chunk, attend, 0)
+    lax.fori_loop(0, tokens // chunk, attend, 0, unroll=True)
 
     @pl.when(large)
     def _():
@@ -418,14 +381,10 @@
 
 
 def window_operands(keys, values, bias, spare):
-    rolled = pltpu.roll(keys, HEAD_DIM, 1)
-    keys_in = pad_keys(keys, spare, 0.0)
-    rolled_in = pad_keys(rolled, spare, 0.0)
-    bias_in = pad_keys(bias, spare, MASKED)
-    values_in = pad_keys(values, spare, 0.0)
-    key_list = [head_key(keys_in, rolled_in, bias_in, head) for head in range(BRANCH_HEADS)]
-    value_list = [head_value(values_in, head) for head in range(BRANCH_HEADS)]
-    return key_list, value_list
+    return (
+        wide_keys(pad_keys(keys, spare, 0.0), pad_keys(bias, spare, MASKED)),
+        wide_values(pad_keys(values, spare, 0.0)),
+    )
 
 
 def grid_shift(values, amount):
@@ -471,15 +430,13 @@
         flat = grid.reshape(tokens, 3 * HALF)
         queries, keys, values = (flat[:, part * HALF : (part + 1) * HALF] for part in range(3))
         bias = window_bias(column_ref, start, window, height)
-        key_list, value_list = window_operands(keys, values, bias, spare)
+        keys_in, values_in = window_operands(keys, values, bias, spare)
 
         @pl.when(large)
         def _():
-            shift_ref[...] = highest_scores(queries, lambda head: key_list[head])
-
-        attended, log_total = attend_heads(
-            queries, shift_ref[...], lambda head: key_list[head], lambda head: value_list[head]
-        )
+            shift_ref[...] = highest_scores(queries, keys_in)
+
+        attended, log_total = attend_heads(queries, shift_ref[...], keys_in, values_in)
         attended_ref[0, :, span] = attended.reshape(height, GROUP, HALF)
         total_ref[0, :, span] = log_total.reshape(height, GROUP, HALF)
         stacked = grid_stack(values.reshape(height, GROUP, HALF))
@@ -495,7 +452,7 @@
         joined_ref[:, span] = attended.reshape(height, GROUP, HALF) + local
         return carry
 
-    lax.fori_loop(0, windows, one_window, 0)
+    lax.fori_loop(0, windows, one_window, 0, unroll=min(windows, 4))
 
     @pl.when(large)
     def _():
@@ -507,15 +464,8 @@
 
 
 def gelu_parts(hidden):
-    size = jnp.abs(hidden) * INV_ROOT_TWO
-    ratio = 1.0 / (1.0 + 0.3275911 * size)
-    poly = ratio * (
-        0.127414796
-        + ratio * (-0.142248368 + ratio * (0.7107068705 + ratio * (-0.7265760135 + ratio * 0.5307027145)))
-    )
-    decay = jnp.exp2(hidden * hidden * (-0.5 * LOG2E))
-    tail = poly * decay
-    return jnp.where(hidden >= 0.0, 1.0 - tail, tail), decay * INV_ROOT_TAU
+    upper = 0.5 + 0.5 * lax.erf(hidden * INV_ROOT_TWO)
+    return upper, jnp.exp2(hidden * hidden * (-0.5 * LOG2E)) * INV_ROOT_TAU
 
 
 def middle_kernel(dims, ways, last, *refs):
@@ -605,7 +555,7 @@
         dsmall_ref[24:32] += fold_rows(back_wide)
         return carry
 
-    lax.fori_loop(0, tokens // chunk, token_rows, 0)
+    lax.fori_loop(0, tokens // chunk, token_rows, 0, unroll=True)
     expand = one_hot(expand_condition(wide, width))
     for row in range(rows):
         gwide_ref[row] = dot(expand, down_ref[row * width : (row + 1) * width]).astype(BF)
@@ -673,8 +623,8 @@
             grad_ref[0, span].astype(F32),
             attended_ref[0, span],
             total_ref[0, span],
-            lambda head: keys_ref[0, head],
-            lambda head: values_ref[0, head],
+            keys_ref[0],
+            values_ref[0],
         )
         mixed_ref[0, span, :HALF] = grad_queries.astype(BF)
         for head in range(BRANCH_HEADS):
@@ -683,7 +633,7 @@
             dvalues_ref[lanes] += grad_values[head]
         return carry
 
-    lax.fori_loop(0, tokens // chunk, attend, 0)
+    lax.fori_loop(0, tokens // chunk, attend, 0, unroll=True)
 
     local_ref[...] = jnp.zeros_like(local_ref)
     for row in range(rows):
@@ -755,14 +705,14 @@
         grad_grid = grad_ref[:, span]
         grad = grad_grid.reshape(tokens, HALF)
         bias = window_bias(column_ref, start, window, height)
-        key_list, value_list = window_operands(keys, values, bias, spare)
+        keys_in, values_in = window_operands(keys, values, bias, spare)
         grad_queries, grad_keys, grad_values = attend_heads_back(
             queries,
             grad,
             attended_ref[0, :, span].reshape(tokens, HALF),
             total_ref[0, :, span].reshape(tokens, HALF),
-            lambda head: key_list[head],
-            lambda head: value_list[head],
+            keys_in,
+            values_in,
         )
         grad_keys = jnp.transpose(jnp.concatenate(grad_keys, axis=0))[:tokens] * SCALE
         grad_values = jnp.transpose(jnp.concatenate(grad_values, axis=0))[:tokens]
@@ -783,7 +733,7 @@
         out_ref[:, span, 2 * HALF :] = grad_values.reshape(shape) + local
         return carry
 
-    lax.fori_loop(0, windows, one_window, 0)
+    lax.fori_loop(0, windows, one_window, 0, unroll=min(windows, 4))
     mixed_grad = out_ref[...].reshape(height * wide_part, 3 * HALF).astype(BF)
     grad_normed = dot_nt(mixed_grad, weight_ref[:, 3 * HALF :]).astype(BF)
     turned_ref[...] = grad_normed.reshape(height, wide_part, 2 * HALF)
@@ -1063,7 +1013,7 @@
     small_in, qkv_in = whole(small_full), whole(qkv_low)
 
     attention_dims = (rows, width, kept, key_rows, chunk)
-    key_shape = (BRANCH_HEADS, key_rows, HALF)
+    key_shape = (key_rows, 2 * HALF)
     joined_across, attended, log_total, keys, values = run_kernel(
         functools.partial(across_kernel, attention_dims),
         count,
@@ -1116,7 +1066,7 @@
         last = index == 1
         results = run_kernel(
             functools.partial(
-                middle_kernel, (rows, width, wide, wide_part, chunk, channels), ways, last
+                middle_kernel, (rows, width, wide, wide_part, tokens // 2, channels), ways, last
             ),
             pair,
             [
@@ -1249,7 +1199,7 @@
     for index, first in enumerate(halves):
         last = index == 1
         results = run_kernel(
-            functools.partial(final_kernel, (rows, width, wide, wide_part, chunk), ways, last),
+            functools.partial(final_kernel, (rows, width, wide, wide_part, tokens), ways, last),
             pair,
             [
                 me_in,

time: 533 us -> 448 us (0.84); the launches traced: 523 us -> 446 us
  Pallas kernels: 378 us -> 295 us
    pallas_call x13, Pallas kernels: 378 us -> 295 us  [run_kernel(): pl.pallas_call(wrapped, grid=(images,), in_specs=[spec for _, spec in inp...]
  transfers between devices with their start and end apart: 58 -> 58, of which waited for: 12 -> 15; matrix products, arithmetic and copies ran while one was open for 3% -> 4% of each run, Pallas kernels for 65% -> 61%
where the time goes in v3:
time: 448 us; the launch traced here: 446 us
  Pallas kernels  295 us (66%)
  starting transfers between devices  77.5 us (17%)
  waiting for transfers between devices  41.5 us (9%)
  other arithmetic  21 us (5%)
  between operations  5.84 us (1%)
  local copies, waits for them, and re-layouts  5.24 us (1%)
    pallas_call x13, Pallas kernels, run_kernel(): pl.pallas_call(wrapped, grid=(images,), in_specs=[spec for _, spec in inp...  295 us
    ppermute x58, starting transfers between devices, swap(): lax.ppermute(value, axis, [(place, place ^ distance) for place in range(l...  77.5 us
    ppermute x58, waiting for transfers between devices, swap(): lax.ppermute(value, axis, [(place, place ^ distance) for place in range(l...  41.5 us
  transfers between devices with their start and end apart: 58, of which 15 were waited for; matrix products, arithmetic and copies ran while one was open for 4% of the time, Pallas kernels for 61%

profile of v3, /device:TPU:0, one launch (start us, length us, event | category | flops | bytes accessed | tf_op | source)
XLA Modules:
  0.0 446.4 jit_solution(3238281551761995843)
XLA Ops:
  3.1 3.0 collective-permute-start
  10.5 2.0 collective-permute-start.10
  14.0 5.6 %collective-permute-done.1.refs_4_ = bf16[80,768]{1,0:T(8,128)(2,1)S(1)} collective-permute-done((bf16[80,768]{1,0:T(8,128)(2,1)S(1)}, bf16[80,768]{1,0:T(8,128)(2,1)S(1)}, u32[]{:S(2)}, u32[]{:S(2)}) %collective-permute-start.1) | collective-permute-done | bytes 122912 | tf_op jit(solution)/shard_map/ppermute | solution.py:888
  20.3 9.4 %shard_map.364 = (bf16[4,1568,384]{2,1,0:T(8,128)(2,1)}, bf16[4,1568,256]{2,1,0:T(8,128)(2,1)}, bf16[4,7,64,256]{3,2,1,0:T(8,128)(2,1)}, bf16[4,7,64,256]{3,2,1,...) custom-call(s32[1]{0:T(128)} %bitcast.refs_0_, ...), custom_call_target="tpu_custom_call" | custom-call | flops 12000000000 | bytes 12000000 | tf_op jit(solution)/shard_map/pallas_call | solution.py:861
  29.8 2.7 collective-permute-start.4
  33.8 43.9 %shard_map.365 = (bf16[4,1568,128]{2,1,0:T(8,128)(2,1)}, f32[4,1568,128]{2,1,0:T(8,128)}, f32[4,1568,128]{2,1,0:T(8,128)}, bf16[4,1280,256]{2,1,0:T(8,128)(2,1)}, bf16[4,1280,256]{2,1,0:T(8,128)(2,1)}) custom-call(bf16[4,1568,384]{2,1,0:T(8,128)(2,1)} %get-tuple-element.114.refs_0_.refs_1_, s32[4,224]{1,0:T(4,128)} %refs_8_.4, ...), custom_call_target="tpu_custom_call" | custom-call | flops 60000002048 | bytes 60000000 | tf_op jit(solution)/shard_map/pallas_call | solution.py:861
  79.3 15.4 %shard_map.366 = (bf16[2,7,64,128]{3,2,1,0:T(8,128)(2,1)}, bf16[2,7,64,128]{3,2,1,0:T(8,128)(2,1)}, bf16[2,7,64,128]{3,2,1,0:T(8,128)(2,1)}, bf16[2,7,64,128]{3,...) custom-call(s32[1]{0:T(128)} %bitcast.refs_0_, ...), custom_call_target="tpu_custom_call" | custom-call | flops 17999998976 | bytes 18000000 | tf_op jit(solution)/shard_map/pallas_call | solution.py:861
  96.3 2.0 collective-permute-start.13
  98.3 15.3 %shard_map.367 = (bf16[2,7,64,128]{3,2,1,0:T(8,128)(2,1)}, bf16[2,7,64,128]{3,2,1,0:T(8,128)(2,1)}, bf16[2,7,64,128]{3,2,1,0:T(8,128)(2,1)}, bf16[2,7,64,128]{3,...) custom-call(s32[1]{0:T(128)} %bitcast.refs_0_, ...), custom_call_target="tpu_custom_call" | custom-call | flops 17999998976 | bytes 18000000 | tf_op jit(solution)/shard_map/pallas_call | solution.py:861
  118.0 23.4 %shard_map.368 = (f32[4,1568,256]{2,1,0:T(8,128)}, f32[2,1568,256]{2,1,0:T(8,128)}, bf16[2,1568,128]{2,1,0:T(8,128)(2,1)}, bf16[2,7,64,128]{3,2,1,0:T(8,128)(2,1...) custom-call(s32[1]{0:T(128)} %bitcast.refs_0_, ...), custom_call_target="tpu_custom_call" | custom-call | flops 35000000512 | bytes 35000000 | tf_op jit(solution)/shard_map/pallas_call | solution.py:861
  145.7 25.5 %shard_map.369 = (f32[4,1568,256]{2,1,0:T(8,128)}, f32[2,1568,256]{2,1,0:T(8,128)}, bf16[2,1568,128]{2,1,0:T(8,128)(2,1)}, bf16[2,7,64,128]{3,2,1,0:T(8,128)(2,1...) custom-call(s32[1]{0:T(128)} %bitcast.refs_0_, ...), custom_call_target="tpu_custom_call", output_to_operand_aliasing={{0}: (20, {})} | custom-call | flops 35000000512 | bytes 35000000 | tf_op jit(solution)/shard_map/pallas_call | solution.py:861
  178.3 20.9 %shard_map.370 = (bf16[2,7,64,256]{3,2,1,0:T(8,128)(2,1)}, bf16[2,7,64,256]{3,2,1,0:T(8,128)(2,1)}, bf16[2,7,64,256]{3,2,1,0:T(8,128)(2,1)}, bf16[2,7,64,256]{3,...) custom-call(s32[1]{0:T(128)} %bitcast.refs_0_, s32[4,224]{1,0:T(4,128)} %refs_8_.4, ...), custom_call_target="tpu_custom_call" | custom-call | flops 28000000000 | bytes 28000000 | tf_op jit(solution)/shard_map/pallas_call | solution.py:861
  202.4 3.8 collective-permute-done.17.refs_14_
  206.9 20.9 %shard_map.371 = (bf16[2,7,64,256]{3,2,1,0:T(8,128)(2,1)}, bf16[2,7,64,256]{3,2,1,0:T(8,128)(2,1)}, bf16[2,7,64,256]{3,2,1,0:T(8,128)(2,1)}, bf16[2,7,64,256]{3,...) custom-call(s32[1]{0:T(128)} %bitcast.refs_0_, ...), custom_call_target="tpu_custom_call" | custom-call | flops 28000000000 | bytes 28000000 | tf_op jit(solution)/shard_map/pallas_call | solution.py:861
  228.7 2.6 collective-permute-start.28
  236.6 4.8 %collective-permute-start.25 = (f32[32,2304]{1,0:T(8,128)S(1)}, f32[32,2304]{1,0:T(8,128)S(1)}, u32[]{:S(2)}, u32[]{:S(2)}) collective-permute-start(f32[32,2304]{1,0:T(8,128)S(1)} %dynamic-slice_add_fusion.refs_11_), channel_id=1, source_target_pairs={{0,8},{4,12},{8,0},{12,4},{16,24},{20,28},{24,16},{28,20},{1,9},{5... | collective-permute-start | bytes 884744 | tf_op jit(solution)/shard_map/ppermute | solution.py:888
  241.4 44.1 %shard_map.372 = (bf16[2,1568,384]{2,1,0:T(8,128)(2,1)}, f32[80,128]{1,0:T(8,128)}, f32[256,384]{1,0:T(8,128)}) custom-call(s32[1]{0:T(128)} %bitcast.refs_0_, bf16[4,1568,384]{2,1,0:T(8,128)(2,1)} %get-tuple-element.114.refs_0_.refs_1_, bf16[2,1568,128]{2,1,0:T(8,128)(2,1)} %get-tuple-element.148.refs_2_, ...), custom_call_target="tpu_custom_call" | custom-call | flops 44999999488 | bytes 45000000 | tf_op jit(solution)/shard_map/pallas_call | solution.py:861
  287.3 58.5 %shard_map.373 = (bf16[2,1568,384]{2,1,0:T(8,128)(2,1)}, f32[80,128]{1,0:T(8,128)}, f32[64,384]{1,0:T(8,128)}, f32[64,384]{1,0:T(8,128)}, f32[64,384]{1,0:T(8,128)}, /*index=5*/f32[64,384]{1,0:T(8,128)}) custom-call(s32[1]{0:T(128)} %bitcast.refs_0_, bf16[4,1568,384]{2,1,0:T(8,128)(2,1)} %get-tuple-element.114.refs_0_.refs_1_, ...), custom_call_target="tpu_custom_call" | custom-call | flops 44999999488 | bytes 45000000 | tf_op jit(solution)/shard_map/pallas_call | solution.py:861
  345.8 2.3 collective-permute-start.37
  351.5 2.5 collective-permute-start.39
  354.1 2.6 collective-permute-start.35
  360.5 8.8 %collective-permute-done.35 = f32[32,2304]{1,0:T(8,128)S(1)} collective-permute-done((f32[32,2304]{1,0:T(8,128)S(1)}, f32[32,2304]{1,0:T(8,128)S(1)}, u32[]{:S(2)}, u32[]{:S(2)}) %collective-permute-start.35) | collective-permute-done | bytes 294944 | tf_op jit(solution)/shard_map/ppermute | solution.py:888
  372.2 7.3 %shard_map.374 = (f32[4,1568,256]{2,1,0:T(8,128)}, f32[16,256]{1,0:T(8,128)}) custom-call(s32[1]{0:T(128)} %bitcast.refs_0_, bf16[4,1568,256]{2,1,0:T(8,128)(2,1)} %bitcast.16, f32[2,1568,256]{2,1,0:T(8,128)} %get-tuple-element.139.refs_19_.refs_2_, bf16[2,1568,384]{2,1,0:T(8,128)(2,1)} %get-tuple-element.179.refs_3_, ...), custom_call_target="tpu_custom_call" | custom-call | flops 8000000000 | bytes 8000000 | tf_op jit(solution)/shard_map/pallas_call | solution.py:861
  379.5 11.5 %collective-permute-done.30.refs_6_ = bf16[2,7,64,256]{3,2,1,0:T(8,128)(2,1)} collective-permute-done((bf16[2,7,64,256]{3,2,1,0:T(8,128)(2,1)S(1)}, bf16[2,7,64,256]{3,2,1,0:T(8,128)(2,1)}, u32[]{:S(2)}, u32[]{:S(2)}) %collective-permute-start.30) | collective-permute-done | bytes 458784 | tf_op jit(solution)/shard_map/ppermute | solution.py:888
  391.8 7.3 %shard_map.375 = (f32[4,1568,256]{2,1,0:T(8,128)}, f32[16,256]{1,0:T(8,128)}, f32[24,256]{1,0:T(8,128)}) custom-call(s32[1]{0:T(128)} %bitcast.refs_0_, bf16[4,1568,256]{2,1,0:T(8,128)(2,1)} %bitcast.17, f32[2,1568,256]{2,1,0:T(8,128)} %get-tuple-element.142.refs_15_.refs_2_, ...), custom_call_target="tpu_custom_call", output_to_operand_aliasing={{0}: (17, {})} | custom-call | flops 8000000000 | bytes 8000000 | tf_op jit(solution)/shard_map/pallas_call | solution.py:861
  400.6 2.1 collective-permute-start.53
  403.5 3.4 collective-permute-start.42
  408.4 3.8 collective-permute-start.46
  413.3 2.0 collective-permute-done.42
  417.1 4.7 %collective-permute-start.55 = (f32[24,256]{1,0:T(8,128)S(1)}, f32[24,256]{1,0:T(8,128)S(1)}, u32[]{:S(2)}, u32[]{:S(2)}) collective-permute-start(f32[24,256]{1,0:T(8,128)S(1)} %add.181), channel_id=1, source_target_pairs={{0,8},{4,12},{8,0},{12,4},{16,24},{20,28},{24,16},{28,20},{1,9},{5... | collective-permute-start | bytes 73736 | tf_op jit(solution)/shard_map/ppermute | solution.py:888
  433.8 2.5 collective-permute-start.50
  441.6 3.4 shard_map.376
  (220 shorter events, 72.3 us)
Async XLA Ops:
  10.5 87.8 %collective-permute-start.10 = (bf16[64,2304]{1,0:T(8,128)(2,1)S(1)}, bf16[64,2304]{1,0:T(8,128)(2,1)S(1)}, u32[]{:S(2)}, u32[]{:S(2)}) collective-permute-start(bf16[64,2304]{1,0:T(8,128)(2,1)S(1)} %slice_dynamic-update-slice_fusion.refs_8_), channel_id=1, source_target_pairs={{0,2},{1,3},{2,0},{3,1},{4,6},{5,7},{6,4},{7,5},{8,10},{9,11},{10,... | collective-permute-start | bytes 884744 | tf_op jit(solution)/shard_map/ppermute | solution.py:888
  12.5 101.1 %collective-permute-start.11 = (bf16[64,2304]{1,0:T(8,128)(2,1)S(1)}, bf16[64,2304]{1,0:T(8,128)(2,1)S(1)}, u32[]{:S(2)}, u32[]{:S(2)}) collective-permute-start(bf16[64,2304]{1,0:T(8,128)(2,1)S(1)} %slice_dynamic-update-slice_fusion.refs_8_), channel_id=1, source_target_pairs={{0,3},{1,2},{2,1},{3,0},{4,7},{5,6},{6,5},{7,4},{8,11},{9,10},{10,... | collective-permute-start | bytes 884744 | tf_op jit(solution)/shard_map/ppermute | solution.py:888
  29.7 48.0 %collective-permute-start.3 = (bf16[4,7,64,256]{3,2,1,0:T(8,128)(2,1)}, bf16[4,7,64,256]{3,2,1,0:T(8,128)(2,1)S(1)}, u32[]{:S(2)}, u32[]{:S(2)}) collective-permute-start(bf16[4,7,64,256]{3,2,1,0:T(8,128)(2,1)} %get-tuple-element.119), channel_id=1, source_target_pairs={{0,1},{1,0},{2,3},{3,2},{4,5},{5,4},{6,7},{7,6},{8,9},{9,8},{10,11... | collective-permute-start | bytes 2752520 | tf_op jit(solution)/shard_map/ppermute | solution.py:888
  29.8 48.6 %collective-permute-start.4 = (bf16[4,7,64,256]{3,2,1,0:T(8,128)(2,1)}, bf16[4,7,64,256]{3,2,1,0:T(8,128)(2,1)S(1)}, u32[]{:S(2)}, u32[]{:S(2)}) collective-permute-start(bf16[4,7,64,256]{3,2,1,0:T(8,128)(2,1)} %get-tuple-element.120), channel_id=1, source_target_pairs={{0,2},{1,3},{2,0},{3,1},{4,6},{5,7},{6,4},{7,5},{8,10},{9,11},{10,... | collective-permute-start | bytes 2752520 | tf_op jit(solution)/shard_map/ppermute | solution.py:888
  32.5 45.9 %collective-permute-start.5 = (bf16[4,7,64,256]{3,2,1,0:T(8,128)(2,1)}, bf16[4,7,64,256]{3,2,1,0:T(8,128)(2,1)}, u32[]{:S(2)}, u32[]{:S(2)}) collective-permute-start(bf16[4,7,64,256]{3,2,1,0:T(8,128)(2,1)} %get-tuple-element.121), channel_id=1, source_target_pairs={{0,3},{1,2},{2,1},{3,0},{4,7},{5,6},{6,5},{7,4},{8,11},{9,10},{10,... | collective-permute-start | bytes 2752520 | tf_op jit(solution)/shard_map/ppermute | solution.py:888
  77.7 37.4 %collective-permute-start.9 = (bf16[64,2304]{1,0:T(8,128)(2,1)S(1)}, bf16[64,2304]{1,0:T(8,128)(2,1)S(1)}, u32[]{:S(2)}, u32[]{:S(2)}) collective-permute-start(bf16[64,2304]{1,0:T(8,128)(2,1)S(1)} %slice_dynamic-update-slice_fusion.refs_8_), channel_id=1, source_target_pairs={{0,1},{1,0},{2,3},{3,2},{4,5},{5,4},{6,7},{7,6},{8,9},{9,8},{10,11... | collective-permute-start | bytes 884744 | tf_op jit(solution)/shard_map/ppermute | solution.py:888
  94.8 22.3 %collective-permute-start.12 = (bf16[2,7,64,128]{3,2,1,0:T(8,128)(2,1)}, bf16[2,7,64,128]{3,2,1,0:T(8,128)(2,1)S(1)}, u32[]{:S(2)}, u32[]{:S(2)}) collective-permute-start(bf16[2,7,64,128]{3,2,1,0:T(8,128)(2,1)} %get-tuple-element.130), channel_id=1, source_target_pairs={{0,1},{1,0},{2,3},{3,2},{4,5},{5,4},{6,7},{7,6},{8,9},{9,8},{10,11... | collective-permute-start | bytes 688136 | tf_op jit(solution)/shard_map/ppermute | solution.py:888
  96.3 20.9 %collective-permute-start.13 = (bf16[2,7,64,128]{3,2,1,0:T(8,128)(2,1)}, bf16[2,7,64,128]{3,2,1,0:T(8,128)(2,1)S(1)}, u32[]{:S(2)}, u32[]{:S(2)}) collective-permute-start(bf16[2,7,64,128]{3,2,1,0:T(8,128)(2,1)} %get-tuple-element.131), channel_id=1, source_target_pairs={{0,2},{1,3},{2,0},{3,1},{4,6},{5,7},{6,4},{7,5},{8,10},{9,11},{10,... | collective-permute-start | bytes 688136 | tf_op jit(solution)/shard_map/ppermute | solution.py:888
  98.3 18.9 %collective-permute-start.14 = (bf16[2,7,64,128]{3,2,1,0:T(8,128)(2,1)}, bf16[2,7,64,128]{3,2,1,0:T(8,128)(2,1)S(1)}, u32[]{:S(2)}, u32[]{:S(2)}) collective-permute-start(bf16[2,7,64,128]{3,2,1,0:T(8,128)(2,1)} %get-tuple-element.132), channel_id=1, source_target_pairs={{0,3},{1,2},{2,1},{3,0},{4,7},{5,6},{6,5},{7,4},{8,11},{9,10},{10,... | collective-permute-start | bytes 688136 | tf_op jit(solution)/shard_map/ppermute | solution.py:888
  113.6 31.3 %collective-permute-start.6 = (bf16[2,7,64,128]{3,2,1,0:T(8,128)(2,1)}, bf16[2,7,64,128]{3,2,1,0:T(8,128)(2,1)S(1)}, u32[]{:S(2)}, u32[]{:S(2)}) collective-permute-start(bf16[2,7,64,128]{3,2,1,0:T(8,128)(2,1)} %get-tuple-element.125), channel_id=1, source_target_pairs={{0,1},{1,0},{2,3},{3,2},{4,5},{5,4},{6,7},{7,6},{8,9},{9,8},{10,11... | collective-permute-start | bytes 688136 | tf_op jit(solution)/shard_map/ppermute | solution.py:888
  115.1 29.8 %collective-permute-start.7 = (bf16[2,7,64,128]{3,2,1,0:T(8,128)(2,1)}, bf16[2,7,64,128]{3,2,1,0:T(8,128)(2,1)S(1)}, u32[]{:S(2)}, u32[]{:S(2)}) collective-permute-start(bf16[2,7,64,128]{3,2,1,0:T(8,128)(2,1)} %get-tuple-element.126), channel_id=1, source_target_pairs={{0,2},{1,3},{2,0},{3,1},{4,6},{5,7},{6,4},{7,5},{8,10},{9,11},{10,... | collective-permute-start | bytes 688136 | tf_op jit(solution)/shard_map/ppermute | solution.py:888
  117.1 27.9 %collective-permute-start.8 = (bf16[2,7,64,128]{3,2,1,0:T(8,128)(2,1)}, bf16[2,7,64,128]{3,2,1,0:T(8,128)(2,1)S(1)}, u32[]{:S(2)}, u32[]{:S(2)}) collective-permute-start(bf16[2,7,64,128]{3,2,1,0:T(8,128)(2,1)} %get-tuple-element.127), channel_id=1, source_target_pairs={{0,3},{1,2},{2,1},{3,0},{4,7},{5,6},{6,5},{7,4},{8,11},{9,10},{10,... | collective-permute-start | bytes 688136 | tf_op jit(solution)/shard_map/ppermute | solution.py:888
  141.4 33.3 %collective-permute-start.18 = (bf16[2,7,64,128]{3,2,1,0:T(8,128)(2,1)}, bf16[2,7,64,128]{3,2,1,0:T(8,128)(2,1)S(1)}, u32[]{:S(2)}, u32[]{:S(2)}) collective-permute-start(bf16[2,7,64,128]{3,2,1,0:T(8,128)(2,1)} %get-tuple-element.158), channel_id=1, source_target_pairs={{0,1},{1,0},{2,3},{3,2},{4,5},{5,4},{6,7},{7,6},{8,9},{9,8},{10,11... | collective-permute-start | bytes 688136 | tf_op jit(solution)/shard_map/ppermute | solution.py:888
  142.9 31.9 %collective-permute-start.19 = (bf16[2,7,64,128]{3,2,1,0:T(8,128)(2,1)}, bf16[2,7,64,128]{3,2,1,0:T(8,128)(2,1)S(1)}, u32[]{:S(2)}, u32[]{:S(2)}) collective-permute-start(bf16[2,7,64,128]{3,2,1,0:T(8,128)(2,1)} %get-tuple-element.159), channel_id=1, source_target_pairs={{0,2},{1,3},{2,0},{3,1},{4,6},{5,7},{6,4},{7,5},{8,10},{9,11},{10,... | collective-permute-start | bytes 688136 | tf_op jit(solution)/shard_map/ppermute | solution.py:888
  144.9 31.4 %collective-permute-start.20 = (bf16[2,7,64,128]{3,2,1,0:T(8,128)(2,1)}, bf16[2,7,64,128]{3,2,1,0:T(8,128)(2,1)S(1)}, u32[]{:S(2)}, u32[]{:S(2)}) collective-permute-start(bf16[2,7,64,128]{3,2,1,0:T(8,128)(2,1)} %get-tuple-element.160), channel_id=1, source_target_pairs={{0,3},{1,2},{2,1},{3,0},{4,7},{5,6},{6,5},{7,4},{8,11},{9,10},{10,... | collective-permute-start | bytes 688136 | tf_op jit(solution)/shard_map/ppermute | solution.py:888
  171.3 27.9 %collective-permute-start.21 = (f32[64,2304]{1,0:T(8,128)}, f32[64,2304]{1,0:T(8,128)S(1)}, u32[]{:S(2)}, u32[]{:S(2)}) collective-permute-start(f32[64,2304]{1,0:T(8,128)} %get-tuple-element.164), channel_id=1, source_target_pairs={{0,1},{1,0},{2,3},{3,2},{4,5},{5,4},{6,7},{7,6},{8,9},{9,8},{10,11... | collective-permute-start | bytes 1769480 | tf_op jit(solution)/shard_map/ppermute | solution.py:888
  172.8 27.1 %collective-permute-start.22 = (f32[64,2304]{1,0:T(8,128)}, f32[64,2304]{1,0:T(8,128)S(1)}, u32[]{:S(2)}, u32[]{:S(2)}) collective-permute-start(f32[64,2304]{1,0:T(8,128)} %get-tuple-element.165), channel_id=1, source_target_pairs={{0,2},{1,3},{2,0},{3,1},{4,6},{5,7},{6,4},{7,5},{8,10},{9,11},{10,... | collective-permute-start | bytes 1769480 | tf_op jit(solution)/shard_map/ppermute | solution.py:888
  174.7 25.2 %collective-permute-start.23 = (f32[64,2304]{1,0:T(8,128)}, f32[64,2304]{1,0:T(8,128)S(1)}, u32[]{:S(2)}, u32[]{:S(2)}) collective-permute-start(f32[64,2304]{1,0:T(8,128)} %get-tuple-element.166), channel_id=1, source_target_pairs={{0,3},{1,2},{2,1},{3,0},{4,7},{5,6},{6,5},{7,4},{8,11},{9,10},{10,... | collective-permute-start | bytes 1769480 | tf_op jit(solution)/shard_map/ppermute | solution.py:888
  174.8 27.4 %collective-permute-start.15 = (bf16[2,7,64,128]{3,2,1,0:T(8,128)(2,1)}, bf16[2,7,64,128]{3,2,1,0:T(8,128)(2,1)S(1)}, u32[]{:S(2)}, u32[]{:S(2)}) collective-permute-start(bf16[2,7,64,128]{3,2,1,0:T(8,128)(2,1)} %get-tuple-element.152), channel_id=1, source_target_pairs={{0,1},{1,0},{2,3},{3,2},{4,5},{5,4},{6,7},{7,6},{8,9},{9,8},{10,11... | collective-permute-start | bytes 688136 | tf_op jit(solution)/shard_map/ppermute | solution.py:888
  176.3 26.1 %collective-permute-start.16 = (bf16[2,7,64,128]{3,2,1,0:T(8,128)(2,1)}, bf16[2,7,64,128]{3,2,1,0:T(8,128)(2,1)S(1)}, u32[]{:S(2)}, u32[]{:S(2)}) collective-permute-start(bf16[2,7,64,128]{3,2,1,0:T(8,128)(2,1)} %get-tuple-element.153), channel_id=1, source_target_pairs={{0,2},{1,3},{2,0},{3,1},{4,6},{5,7},{6,4},{7,5},{8,10},{9,11},{10,... | collective-permute-start | bytes 688136 | tf_op jit(solution)/shard_map/ppermute | solution.py:888
  231.5 139.3 %collective-permute-start.32 = (bf16[2,7,64,256]{3,2,1,0:T(8,128)(2,1)S(1)}, bf16[2,7,64,256]{3,2,1,0:T(8,128)(2,1)S(1)}, u32[]{:S(2)}, u32[]{:S(2)}) collective-permute-start(bf16[2,7,64,256]{3,2,1,0:T(8,128)(2,1)S(1)} %copy-done.18), channel_id=1, source_target_pairs={{0,1},{1,0},{2,3},{3,2},{4,5},{5,4},{6,7},{7,6},{8,9},{9,8},{10,11... | collective-permute-start | bytes 1376264 | tf_op jit(solution)/shard_map/ppermute | solution.py:888
  232.7 139.5 %collective-permute-start.33 = (bf16[2,7,64,256]{3,2,1,0:T(8,128)(2,1)S(1)}, bf16[2,7,64,256]{3,2,1,0:T(8,128)(2,1)}, u32[]{:S(2)}, u32[]{:S(2)}) collective-permute-start(bf16[2,7,64,256]{3,2,1,0:T(8,128)(2,1)S(1)} %copy-done.17), channel_id=1, source_target_pairs={{0,2},{1,3},{2,0},{3,1},{4,6},{5,7},{6,4},{7,5},{8,10},{9,11},{10,... | collective-permute-start | bytes 1376264 | tf_op jit(solution)/shard_map/ppermute | solution.py:888
  233.3 138.9 %collective-permute-start.34 = (bf16[2,7,64,256]{3,2,1,0:T(8,128)(2,1)S(1)}, bf16[2,7,64,256]{3,2,1,0:T(8,128)(2,1)}, u32[]{:S(2)}, u32[]{:S(2)}) collective-permute-start(bf16[2,7,64,256]{3,2,1,0:T(8,128)(2,1)S(1)} %copy-done.16), channel_id=1, source_target_pairs={{0,3},{1,2},{2,1},{3,0},{4,7},{5,6},{6,5},{7,4},{8,11},{9,10},{10,... | collective-permute-start | bytes 1376264 | tf_op jit(solution)/shard_map/ppermute | solution.py:888
  236.6 111.5 %collective-permute-start.36 = (f32[64,384]{1,0:T(8,128)}, f32[64,384]{1,0:T(8,128)S(1)}, u32[]{:S(2)}, u32[]{:S(2)}) collective-permute-start(f32[64,384]{1,0:T(8,128)} %add_add_fusion.4.refs_14_), channel_id=1, source_target_pairs={{0,4},{4,0},{8,12},{12,8},{16,20},{20,16},{24,28},{28,24},{1,5},{5... | collective-permute-start | bytes 294920 | tf_op jit(solution)/shard_map/ppermute | solution.py:888
  236.6 48.9 %collective-permute-start.25 = (f32[32,2304]{1,0:T(8,128)S(1)}, f32[32,2304]{1,0:T(8,128)S(1)}, u32[]{:S(2)}, u32[]{:S(2)}) collective-permute-start(f32[32,2304]{1,0:T(8,128)S(1)} %dynamic-slice_add_fusion.refs_11_), channel_id=1, source_target_pairs={{0,8},{4,12},{8,0},{12,4},{16,24},{20,28},{24,16},{28,20},{1,9},{5... | collective-permute-start | bytes 884744 | tf_op jit(solution)/shard_map/ppermute | solution.py:888
  354.1 15.3 %collective-permute-start.35 = (f32[32,2304]{1,0:T(8,128)S(1)}, f32[32,2304]{1,0:T(8,128)S(1)}, u32[]{:S(2)}, u32[]{:S(2)}) collective-permute-start(f32[32,2304]{1,0:T(8,128)S(1)} %copy-done.1), channel_id=1, source_target_pairs={{0,16},{4,20},{8,24},{12,28},{16,0},{20,4},{24,8},{28,12},{1,17},{... | collective-permute-start | bytes 884744 | tf_op jit(solution)/shard_map/ppermute | solution.py:888
  358.2 21.3 %collective-permute-start.29 = (bf16[2,7,64,256]{3,2,1,0:T(8,128)(2,1)S(1)}, bf16[2,7,64,256]{3,2,1,0:T(8,128)(2,1)}, u32[]{:S(2)}, u32[]{:S(2)}) collective-permute-start(bf16[2,7,64,256]{3,2,1,0:T(8,128)(2,1)S(1)} %copy-done.21), channel_id=1, source_target_pairs={{0,1},{1,0},{2,3},{3,2},{4,5},{5,4},{6,7},{7,6},{8,9},{9,8},{10,11... | collective-permute-start | bytes 1376264 | tf_op jit(solution)/shard_map/ppermute | solution.py:888
  369.3 21.7 %collective-permute-start.30 = (bf16[2,7,64,256]{3,2,1,0:T(8,128)(2,1)S(1)}, bf16[2,7,64,256]{3,2,1,0:T(8,128)(2,1)}, u32[]{:S(2)}, u32[]{:S(2)}) collective-permute-start(bf16[2,7,64,256]{3,2,1,0:T(8,128)(2,1)S(1)} %copy-done.20), channel_id=1, source_target_pairs={{0,2},{1,3},{2,0},{3,1},{4,6},{5,7},{6,4},{7,5},{8,10},{9,11},{10,... | collective-permute-start | bytes 1376264 | tf_op jit(solution)/shard_map/ppermute | solution.py:888
  370.8 20.3 %collective-permute-start.31 = (bf16[2,7,64,256]{3,2,1,0:T(8,128)(2,1)S(1)}, bf16[2,7,64,256]{3,2,1,0:T(8,128)(2,1)S(1)}, u32[]{:S(2)}, u32[]{:S(2)}) collective-permute-start(bf16[2,7,64,256]{3,2,1,0:T(8,128)(2,1)S(1)} %copy-done.19), channel_id=1, source_target_pairs={{0,3},{1,2},{2,1},{3,0},{4,7},{5,6},{6,5},{7,4},{8,11},{9,10},{10,... | collective-permute-start | bytes 1376264 | tf_op jit(solution)/shard_map/ppermute | solution.py:888
  372.2 31.3 %collective-permute-start.44 = (f32[64,384]{1,0:T(8,128)}, f32[64,384]{1,0:T(8,128)S(1)}, u32[]{:S(2)}, u32[]{:S(2)}) collective-permute-start(f32[64,384]{1,0:T(8,128)} %add_add_fusion.3.refs_16_), channel_id=1, source_target_pairs={{0,4},{4,0},{8,12},{12,8},{16,20},{20,16},{24,28},{28,24},{1,5},{5... | collective-permute-start | bytes 294920 | tf_op jit(solution)/shard_map/ppermute | solution.py:888
  408.1 13.7 %collective-permute-start.45 = (f32[64,384]{1,0:T(8,128)S(1)}, f32[64,384]{1,0:T(8,128)S(1)}, u32[]{:S(2)}, u32[]{:S(2)}) collective-permute-start(f32[64,384]{1,0:T(8,128)S(1)} %add.170), channel_id=1, source_target_pairs={{0,8},{4,12},{8,0},{12,4},{16,24},{20,28},{24,16},{28,20},{1,9},{5... | collective-permute-start | bytes 294920 | tf_op jit(solution)/shard_map/ppermute | solution.py:888
  408.4 14.6 %collective-permute-start.46 = (f32[64,384]{1,0:T(8,128)S(1)}, f32[64,384]{1,0:T(8,128)S(1)}, u32[]{:S(2)}, u32[]{:S(2)}) collective-permute-start(f32[64,384]{1,0:T(8,128)S(1)} %add.170), channel_id=1, source_target_pairs={{0,16},{4,20},{8,24},{12,28},{16,0},{20,4},{24,8},{28,12},{1,17},{... | collective-permute-start | bytes 294920 | tf_op jit(solution)/shard_map/ppermute | solution.py:888
  (69 other events, 1068.6 us)

commit v4 on v3

--- a/solution.py
+++ b/solution.py
@@ -218,35 +218,61 @@
     pl.when(pl.program_id(0) == pl.num_programs(0) - 1)(body)
 
 
-def project_kernel(dims, ways, *refs):
+def pack_early_kernel(qkv_ref, small_ref, bias_ref, early_ref):
+    shard, small_lanes = qkv_ref.shape[0], small_ref.shape[1]
+    bias_lanes = bias_ref.shape[1]
+    early_ref[:shard] = qkv_ref[...].astype(BF)
+    spare = early_ref.shape[1] - small_lanes - bias_lanes
+    bias = jnp.concatenate([bias_ref[...], jnp.zeros((small_ref.shape[0] - 1, bias_lanes), F32)], axis=0)
+    early_ref[shard:] = jnp.concatenate(
+        [small_ref[...], bias, jnp.zeros((small_ref.shape[0], spare), F32)], axis=1
+    ).astype(BF)
+
+
+def pack_late_kernel(out_ref, expand_ref, shrink_ref, late_ref):
+    shard, channels = out_ref.shape
+    begin = channels + expand_ref.shape[1]
+    late_ref[:, :channels] = out_ref[...].astype(BF)
+    late_ref[:, channels:begin] = expand_ref[...].astype(BF)
+    for block in range(shrink_ref.shape[0] // shard):
+        lanes = slice(begin + block * channels, begin + (block + 1) * channels)
+        late_ref[:, lanes] = shrink_ref[block * shard : (block + 1) * shard].astype(BF)
+
+
+def project_kernel(dims, ways, assembles, *refs):
     rows, width, wide, wide_part = dims
     me_ref, x_ref = refs[:2]
-    pieces = refs[2 : 2 + ways]
-    across_ref, normed_ref = refs[2 + ways : 4 + ways]
-    down_refs = refs[4 + ways : 4 + 2 * ways]
-    weight_ref, small_ref, bias_ref, spread_ref = refs[4 + 2 * ways :]
-
-    @pl.when(pl.program_id(0) == 0)
-    def _():
-        channels, hidden_width = small_ref.shape[1], bias_ref.shape[1]
-        shard = channels // ways
-        bias_shard = hidden_width // ways
-        lanes = -(-(shard + bias_shard) // 128) * 128
-        lane, column = iota((lanes, channels + hidden_width), 0), iota((lanes, channels + hidden_width), 1)
-        total = jnp.zeros((16, channels + hidden_width), F32)
-        for distance, piece in enumerate(pieces):
-            place = me_ref[0] ^ distance
-            weight_ref[pl.ds(pl.multiple_of(place * shard, shard), shard)] = piece[:shard]
-            target = jnp.where(
-                lane < shard,
-                lane + shard * place,
-                channels + lane - shard + bias_shard * place,
-            )
-            chosen = one_hot((column == target) & (lane < shard + bias_shard))
-            total = total + dot(piece[shard : shard + 16, :lanes], chosen)
-        small_ref[...] = total[:, :channels]
-        bias_ref[...] = total[0:1, channels:]
-
+    if assembles:
+        pieces = refs[2 : 2 + ways]
+        across_ref, normed_ref = refs[2 + ways : 4 + ways]
+        down_refs = refs[4 + ways : 4 + 2 * ways]
+        weight_ref, small_ref, bias_ref, spread_ref = refs[4 + 2 * ways :]
+
+        @pl.when(pl.program_id(0) == 0)
+        def _():
+            channels, hidden_width = small_ref.shape[1], bias_ref.shape[1]
+            shard = channels // ways
+            bias_shard = hidden_width // ways
+            lanes = -(-(shard + bias_shard) // 128) * 128
+            lane, column = iota((lanes, channels + hidden_width), 0), iota((lanes, channels + hidden_width), 1)
+            total = jnp.zeros((16, channels + hidden_width), F32)
+            for distance, piece in enumerate(pieces):
+                place = me_ref[0] ^ distance
+                weight_ref[pl.ds(pl.multiple_of(place * shard, shard), shard)] = piece[:shard]
+                target = jnp.where(
+                    lane < shard,
+                    lane + shard * place,
+                    channels + lane - shard + bias_shard * place,
+                )
+                chosen = one_hot((column == target) & (lane < shard + bias_shard))
+                total = total + dot(piece[shard : shard + 16, :lanes], chosen)
+            small_ref[...] = total[:, :channels]
+            bias_ref[...] = total[0:1, channels:]
+
+    else:
+        weight_ref, small_ref, across_ref, normed_ref = refs[2:6]
+        down_refs = refs[6 : 6 + ways]
+        spread_ref = refs[6 + ways]
     gain, offset = small_ref[9:10], small_ref[10:11]
     expand = one_hot(expand_condition(wide, width))
     for row in range(rows):
@@ -269,6 +295,7 @@
 
 def across_kernel(
     dims,
+    first,
     across_ref,
     mask_ref,
     small_ref,
@@ -282,7 +309,7 @@
     rows, width, kept, key_rows, chunk = dims
     tokens = rows * width
     image = pl.program_id(0)
-    ranks = rank_row(mask_ref[pl.ds(image, 1)].astype(F32), width)
+    ranks = rank_row(mask_ref[pl.ds(image + first, 1)].astype(F32), width)
     select = one_hot(iota((kept, width), 0).astype(F32) == ranks)
     bias = jnp.where(iota((kept, HALF), 0) >= VALID, MASKED, 0.0)
     key_norms = jnp.zeros((1, HALF), F32)
@@ -401,9 +428,10 @@
     me_ref, mask_ref, small_ref, weight_ref = refs[:4]
     pieces_in = refs[4 : 4 + ways]
     joined_refs = refs[4 + ways : 4 + 2 * ways]
-    attended_ref, total_ref, saved_ref, normed_ref, mixed_ref, joined_ref, column_ref, shift_ref = refs[
+    attended_ref, total_ref, saved_ref, normed_out, mixed_ref, joined_ref, column_ref, shift_ref = refs[
         4 + 2 * ways :
     ]
+    normed_ref = normed_out.at[0]
     rows = height // ways
     start = down_setup(me_ref, mask_ref, column_ref, width, wide, wide_part, first)
     assemble(me_ref, pieces_in, normed_ref, 0, rows)
@@ -468,7 +496,7 @@
     return upper, jnp.exp2(hidden * hidden * (-0.5 * LOG2E)) * INV_ROOT_TAU
 
 
-def middle_kernel(dims, ways, last, *refs):
+def middle_kernel(dims, ways, *refs):
     rows, width, wide, wide_part, chunk, hidden_part = dims
     refs = list(refs)
 
@@ -478,24 +506,23 @@
         return taken
 
     me_ref, x_ref, cot_ref, across_ref = take(4)
-    pieces_in = take(ways)
+    pieces_in = [take(ways), take(ways)]
     weights_in = take(ways)
     small_ref, bias_ref = take(2)
-    starts = take(5) if last else None
     block_ref, middle_ref, grad_across_ref = take(3)
     grad_refs = take(ways)
     dbias_ref, dsmall_ref = take(2)
-    piece_refs = take(ways) if last else None
+    piece_refs = take(ways)
     dout_ref, dexpand_ref, dshrink_ref = take(3)
     out_ref, expand_ref, shrink_ref = take(3)
     wide_ref, joined_ref, normed_ref, active_ref, hidden_ref, attended_ref, down_ref, gwide_ref = take(8)
-    turned_ref = take(1)[0] if last else None
+    turned_ref = take(1)[0]
     tokens = rows * width
     hidden_width = expand_ref.shape[1]
     channels = 2 * HALF
     shard = channels // ways
     blocks = hidden_width // channels
-    start_sums((dbias_ref, dsmall_ref, dout_ref, dexpand_ref, dshrink_ref), starts)
+    start_sums((dbias_ref, dsmall_ref, dout_ref, dexpand_ref, dshrink_ref), None)
 
     @pl.when(pl.program_id(0) == 0)
     def _():
@@ -509,7 +536,16 @@
                 lanes = slice(channels + hidden_width + block * channels, channels + hidden_width + (block + 1) * channels)
                 shrink_ref[pl.ds(begin, shard)] = piece[:, lanes]
 
-    assemble(me_ref, pieces_in, wide_ref, 1, wide_part)
+    image, pair = pl.program_id(0), pl.num_programs(0) // 2
+
+    @pl.when(image < pair)
+    def _():
+        assemble(me_ref, pieces_in[0], wide_ref, 1, wide_part)
+
+    @pl.when(image >= pair)
+    def _():
+        assemble(me_ref, pieces_in[1], wide_ref, 1, wide_part)
+
     contract = contract_matrix(width, wide)
     for row in range(rows):
         span = slice(row * width, (row + 1) * width)
@@ -567,22 +603,21 @@
     dout_ref[...] += dot_tn(joined_ref[...], attended_ref[...])
     dexpand_ref[...] += dot_tn(normed_ref[...], hidden_ref[...])
     dshrink_ref[...] += dot_tn(cot_ref[0], active_ref[...])
-    if last:
-
-        @at_last_step
-        def _():
+
+    @at_last_step
+    def _():
+        for block in range(blocks):
+            lanes = slice(block * channels, (block + 1) * channels)
+            turned_ref[lanes] = jnp.transpose(dshrink_ref[:, lanes])
+        for distance, piece in enumerate(piece_refs):
+            place = me_ref[0] ^ distance
+            span = pl.ds(pl.multiple_of(place * shard, shard), shard)
+            piece[:, :channels] = dout_ref[span]
+            piece[:, channels : channels + hidden_width] = dexpand_ref[span]
             for block in range(blocks):
-                lanes = slice(block * channels, (block + 1) * channels)
-                turned_ref[lanes] = jnp.transpose(dshrink_ref[:, lanes])
-            for distance, piece in enumerate(piece_refs):
-                place = me_ref[0] ^ distance
-                span = pl.ds(pl.multiple_of(place * shard, shard), shard)
-                piece[:, :channels] = dout_ref[span]
-                piece[:, channels : channels + hidden_width] = dexpand_ref[span]
-                for block in range(blocks):
-                    begin = pl.multiple_of((place * blocks + block) * shard, shard)
-                    lanes = slice(channels + hidden_width + block * channels, channels + hidden_width + (block + 1) * channels)
-                    piece[:, lanes] = turned_ref[pl.ds(begin, shard)]
+                begin = pl.multiple_of((place * blocks + block) * shard, shard)
+                lanes = slice(channels + hidden_width + block * channels, channels + hidden_width + (block + 1) * channels)
+                piece[:, lanes] = turned_ref[pl.ds(begin, shard)]
 
 
 def shard_pieces(me_ref, piece_refs, total_ref):
@@ -595,7 +630,7 @@
             piece[...] = total_ref[pl.ds(begin, shard)]
 
 
-def across_back_kernel(dims, ways, first, last, *refs):
+def across_back_kernel(dims, first, last, *refs):
     rows, width, kept, key_rows, chunk = dims
     refs = list(refs)
 
@@ -604,12 +639,10 @@
         del refs[:number]
         return taken
 
-    me_ref, across_ref, grad_ref, attended_ref, total_ref, keys_ref, values_ref, normed_ref = take(8)
+    across_ref, grad_ref, attended_ref, total_ref, keys_ref, values_ref, normed_ref = take(7)
     mask_ref, small_ref = take(2)
     starts = take(2) if last else None
-    mixed_ref, taps_ref = take(2)
-    piece_refs = take(ways) if last else None
-    dweight_ref, dkeys_ref, dvalues_ref, local_ref = take(4)
+    mixed_ref, taps_ref, dweight_ref, dkeys_ref, dvalues_ref, local_ref = take(6)
     tokens = rows * width
     image = pl.program_id(0) + first
     start_sums((taps_ref, dweight_ref), starts)
@@ -633,7 +666,7 @@
             dvalues_ref[lanes] += grad_values[head]
         return carry
 
-    lax.fori_loop(0, tokens // chunk, attend, 0, unroll=True)
+    lax.fori_loop(0, tokens // chunk, attend, 0)
 
     local_ref[...] = jnp.zeros_like(local_ref)
     for row in range(rows):
@@ -668,11 +701,9 @@
         whole = unpacked[:, HALF : 2 * HALF] + unpacked[:, 2 * HALF :] + local_ref[target]
         mixed_ref[0, target, 2 * HALF :] = whole.astype(BF)
     dweight_ref[...] += dot_tn(normed_ref[0], mixed_ref[0])
-    if last:
-        shard_pieces(me_ref, piece_refs, dweight_ref)
-
-
-def down_back_kernel(dims, ways, first, last, *refs):
+
+
+def down_back_kernel(dims, ways, *refs):
     height, width, wide, wide_part, spare = dims
     refs = list(refs)
 
@@ -681,22 +712,19 @@
         del refs[:number]
         return taken
 
-    me_ref, mask_ref, small_ref, weight_ref, attended_ref, total_ref, saved_ref = take(7)
-    normed_in = take(ways)
+    me_ref, mask_ref, small_ref, weight_ref, attended_ref, total_ref, saved_ref, normed_ref = take(8)
     grads_in = take(ways)
-    starts = take(2) if last else None
     out_refs = take(ways)
     taps_ref = take(1)[0]
-    piece_refs = take(ways) if last else None
-    dweight_ref, normed_ref, mixed_ref, grad_ref, out_ref, turned_ref, column_ref = take(7)
+    piece_refs = take(ways)
+    dweight_ref, mixed_ref, grad_ref, out_ref, turned_ref, column_ref = take(6)
     rows = height // ways
-    start = down_setup(me_ref, mask_ref, column_ref, width, wide, wide_part, first)
-    assemble(me_ref, normed_in, normed_ref, 0, rows)
+    start = down_setup(me_ref, mask_ref, column_ref, width, wide, wide_part, 0)
     assemble(me_ref, grads_in, grad_ref, 0, rows)
     mixed_ref[...] = saved_ref[0].astype(F32)
     tokens = height * GROUP
     windows = wide_part // GROUP
-    start_sums((taps_ref, dweight_ref), starts)
+    start_sums((taps_ref, dweight_ref), None)
 
     def one_window(window, carry):
         span = pl.ds(pl.multiple_of(window * GROUP, GROUP), GROUP)
@@ -740,10 +768,9 @@
     for distance in range(ways):
         place = me_ref[0] ^ distance
         out_refs[distance][0] = turned_ref[pl.ds(place * rows, rows)]
-    normed = normed_ref[...].reshape(height * wide_part, 2 * HALF)
+    normed = normed_ref[0].reshape(height * wide_part, 2 * HALF)
     dweight_ref[...] += dot_tn(normed, mixed_grad)
-    if last:
-        shard_pieces(me_ref, piece_refs, dweight_ref)
+    shard_pieces(me_ref, piece_refs, dweight_ref)
 
 
 def final_kernel(dims, ways, last, *refs):
@@ -759,10 +786,11 @@
     pieces_in = take(ways)
     small_ref, weight_ref = take(2)
     starts = take(1) if last else None
-    others = take(4) if last else None
+    others = take(5) if last else None
     grad_ref, dsmall_ref = take(2)
+    piece_refs = take(ways) if last else None
+    wide_ref, down_ref = take(2)
     whole_ref = take(1)[0] if last else None
-    wide_ref, down_ref = take(2)
     tokens = rows * width
     start_sums((dsmall_ref,), starts)
     assemble(me_ref, pieces_in, wide_ref, 1, wide_part)
@@ -786,7 +814,7 @@
 
         @at_last_step
         def _():
-            across_taps, down_taps, middle_sums, bias_sums = others
+            across_taps, down_taps, middle_sums, bias_sums, dweight = others
             channels = 2 * HALF
 
             def total(ref, index):
@@ -807,32 +835,71 @@
             bias = total(bias_sums, 0)
             for block in range(bias.shape[1] // channels):
                 whole_ref[16 + block : 17 + block] = bias[:, block * channels : (block + 1) * channels]
-
-
-def update_kernel(blocks, factor_ref, shard_ref, across_ref, down_ref, *refs):
-    old, new = refs[:12], refs[12:]
-    factor = factor_ref[0]
+            shard = dweight.shape[0] // ways
+            for distance, piece in enumerate(piece_refs):
+                begin = pl.multiple_of((me_ref[0] ^ distance) * shard, shard)
+                piece[:shard] = dweight[pl.ds(begin, shard)].astype(BF)
+                piece[shard:, :channels] = whole_ref[...].astype(BF)
+                piece[shard:, channels:] = jnp.zeros(
+                    (whole_ref.shape[0], dweight.shape[1] - channels), BF
+                )
+
+
+def update_kernel(ways, place_ref, mine_ref, other_ref, tail_ref, *refs):
+    squares, old, new = refs[:ways], refs[ways : ways + 18], refs[ways + 19 : ways + 37]
+    norm_ref, joined_ref = refs[ways + 18], refs[ways + 37]
+    me, core = place_ref[0], place_ref[1]
+    half = mine_ref.shape[0]
+    joined_ref[pl.ds(pl.multiple_of(core * half, half), half)] = mine_ref[...]
+    joined_ref[pl.ds(pl.multiple_of((1 - core) * half, half), half)] = other_ref[...]
+    shard = 2 * half
     rows, channels = old[1].shape
     hidden_width = old[2].shape[1]
-
-    def update(index, grads, rate, spans=(slice(None), slice(None))):
-        weight, first, second = (old[part * 4 + index][spans] for part in range(3))
-        results = adam_update(weight, first, second, grads * factor, rate, WEIGHT_DECAY)
+    blocks = hidden_width // channels
+    small = tail_ref[shard:, :channels]
+    small_rows, small_lanes = old[4].shape
+    bias_lanes = old[5].shape[1]
+    total = tree_sum([entry[...] for entry in squares]) + jnp.sum(small * small)
+    norm = jnp.sqrt(total)
+    norm_ref[0, 0] = jnp.max(norm)
+    factor = (CLIP_NORM / jnp.maximum(norm, CLIP_NORM))[0:1, 0:1]
+
+    def update(index, grads, rate, decay, spans=(slice(None), slice(None))):
+        weight, first, second = (old[part * 6 + index][spans] for part in range(3))
+        results = adam_update(weight, first, second, grads * factor, rate, decay)
         for part in range(3):
-            new[part * 4 + index][spans] = results[part]
-
-    update(0, across_ref[...], RATE_MATRIX, (slice(None), slice(0, 3 * HALF)))
-    update(0, down_ref[...], RATE_MATRIX, (slice(None), slice(3 * HALF, 6 * HALF)))
-    update(1, shard_ref[:, :channels], RATE_OUTPUT)
-    update(2, shard_ref[:, channels : channels + hidden_width], RATE_MATRIX)
+            new[part * 6 + index][spans] = results[part]
+
+    update(0, tail_ref[:shard], RATE_MATRIX, WEIGHT_DECAY, (slice(None), slice(0, 3 * HALF)))
+    begin = channels + 2 * hidden_width
+    update(
+        0,
+        joined_ref[:, begin : begin + 3 * HALF],
+        RATE_MATRIX,
+        WEIGHT_DECAY,
+        (slice(None), slice(3 * HALF, 6 * HALF)),
+    )
+    update(1, joined_ref[:, :channels], RATE_OUTPUT, WEIGHT_DECAY)
+    update(2, joined_ref[:, channels : channels + hidden_width], RATE_MATRIX, WEIGHT_DECAY)
     for block in range(blocks):
         begin = channels + hidden_width + block * channels
         update(
             3,
-            shard_ref[:, begin : begin + channels],
+            joined_ref[:, begin : begin + channels],
             RATE_MATRIX,
+            WEIGHT_DECAY,
             (slice(block * rows, (block + 1) * rows), slice(None)),
         )
+    small_grad = jnp.zeros((small_rows, small_lanes), F32)
+    bias_grad = jnp.zeros((1, bias_lanes), F32)
+    for place in range(ways):
+        lanes = slice(place * small_lanes, (place + 1) * small_lanes)
+        small_grad = jnp.where(me == place, small[:small_rows, lanes], small_grad)
+        row, lane = divmod(place * bias_lanes, channels)
+        row = small_rows + row
+        bias_grad = jnp.where(me == place, small[row : row + 1, lane : lane + bias_lanes], bias_grad)
+    update(4, small_grad, RATE_SMALL, 0.0)
+    update(5, bias_grad, RATE_MATRIX, 0.0)
 
 
 def image_block(*shape, first=0):
@@ -847,18 +914,21 @@
     return pl.BlockSpec(memory_space=pltpu.SMEM)
 
 
-def run_kernel(body, images, inputs, outputs, scratch, micros, after=(), alias=None):
-    number = len(inputs)
+def run_kernel(body, images, inputs, outputs, scratch, micros, after=(), alias=()):
+    number, made = len(inputs), len(outputs)
     hidden = list(after)
     aliases = {}
-    if alias is not None:
-        aliases = {number + len(hidden): alias[1]}
-        hidden.append(alias[0])
+    for operand, output in alias:
+        aliases[number + len(hidden)] = output
+        hidden.append(operand)
+    skipped = number + len(hidden)
 
     def wrapped(*refs):
-        body(*refs[:number], *refs[number + len(hidden) :])
-
-    return pl.pallas_call(
+        refs[skipped + made][...] = jnp.zeros((8, 128), F32)
+        body(*refs[:number], *refs[skipped : skipped + made], *refs[skipped + made + 1 :])
+
+    outputs = list(outputs) + [((8, 128), F32, whole_block(8, 128))]
+    *results, token = pl.pallas_call(
         wrapped,
         grid=(images,),
         in_specs=[spec for _, spec in inputs] + [pl.BlockSpec(memory_space=pl.ANY)] * len(hidden),
@@ -871,6 +941,7 @@
             flops=int(micros * 1e9), bytes_accessed=int(micros * 1e6), transcendentals=0
         ),
     )(*[operand for operand, _ in inputs], *hidden)
+    return results, token
 
 
 def adam_update(weight, first_old, second_old, grad_value, rate_value, decay_value):
@@ -898,31 +969,10 @@
     return values[0]
 
 
-def sum_chips(value):
-    return tree_sum([value] + [swap(value, "img", d) for d in range(2, lax.axis_size("img"), 2)])
-
-
-def sum_cores(value):
-    return value + swap(value, "img", 1)
-
-
-def sum_halves(value):
-    core = lax.axis_index("img") % 2
-    rows = value.shape[0] // 2
-    mine = lax.dynamic_slice_in_dim(value, core * rows, rows, 0)
-    other = lax.dynamic_slice_in_dim(value, (1 - core) * rows, rows, 0)
-    stages = [mine + swap(other, "img", 1)]
-    distance = 2
-    while distance < lax.axis_size("img"):
-        stages.append(stages[-1] + swap(stages[-1], "img", distance))
-        distance *= 2
-    return stages
-
-
-def join_halves(mine):
-    other = swap(mine, "img", 1)
-    lower = lax.axis_index("img") % 2 == 0
-    return jnp.concatenate([jnp.where(lower, mine, other), jnp.where(lower, other, mine)], axis=0)
+def share_low(value, distances):
+    rounded = lax.reduce_precision(value, 8, 7)
+    sent = rounded.astype(BF)
+    return [rounded] + [swap(sent, "img", distance).astype(F32) for distance in distances]
 
 
 def on_device(
@@ -965,16 +1015,7 @@
     blocks = hidden_width // channels
     chunk = width
     pair = count // 2
-    halves = (0, pair)
-
-    small_pack = jnp.concatenate(
-        [small_params, jnp.pad(expand_bias[None], ((0, small_params.shape[0] - 1), (0, 0)))], axis=1
-    )
-    small_pack = jnp.pad(small_pack, ((0, 0), (0, qkv_weight.shape[1] - small_pack.shape[1])))
-    early = jnp.concatenate([qkv_weight, small_pack], axis=0).astype(BF)
-    early_pieces = exchange([early] * ways)
-    shrink_blocks = [shrink_weight[block * shard : (block + 1) * shard] for block in range(blocks)]
-    late = jnp.concatenate([out_weight, expand_weight, *shrink_blocks], axis=1).astype(BF)
+    chip_steps = [2 << bit for bit in range((lax.axis_size("img") // 2).bit_length() - 1)][::-1]
 
     x = images.reshape(count, tokens, channels)
     cot = cotangent.reshape(count, tokens, channels)
@@ -990,183 +1031,176 @@
     def whole(array):
         return (array, whole_block(*array.shape))
 
-    def new_image(dims, dtype, images=pair):
+    def half_images(array, first):
+        last = array.shape[0] - 1
+        dims = (1,) + array.shape[1:]
+        return (
+            array,
+            pl.BlockSpec(
+                dims, lambda image: (jnp.clip(image - first, 0, last),) + (0,) * (len(dims) - 1)
+            ),
+        )
+
+    def new_image(dims, dtype, images):
         return ((images,) + dims, dtype, image_block(*dims))
+
+    def part_image(dims, dtype, first):
+        return ((count,) + dims, dtype, image_block(*dims, first=first))
 
     def new_whole(dims, dtype):
         return (dims, dtype, whole_block(*dims))
 
-    results = run_kernel(
-        functools.partial(project_kernel, (rows, width, wide, wide_part), ways),
-        count,
-        [me_in, per_image(x)] + [whole(piece) for piece in early_pieces],
-        [new_image((tokens, 3 * HALF), BF, count), new_image((tokens, channels), BF, count)]
-        + [new_image(piece_in, BF, count)] * ways
-        + [new_whole(qkv_shape, BF), new_whole((16, channels), F32), new_whole((1, hidden_width), F32)],
-        [pltpu.VMEM((rows, wide, channels), BF)],
-        12,
-    )
-    across_mixed, normed = results[:2]
-    normed_pieces = exchange(results[2 : 2 + ways])
-    qkv_low, small_full, bias_full = results[2 + ways :]
+    (early,), _ = run_kernel(
+        pack_early_kernel,
+        1,
+        [whole(qkv_weight), whole(small_params), whole(expand_bias.reshape(1, -1))],
+        [new_whole((shard + 16, qkv_weight.shape[1]), BF)],
+        [],
+        2,
+    )
+    weights_in = exchange([early] * ways)
+
+    whole_images, normed_pieces, parameters = [], [], None
+    for first in (0, pair):
+        assembles = first == 0
+        results, token = run_kernel(
+            functools.partial(project_kernel, (rows, width, wide, wide_part), ways, assembles),
+            pair,
+            [me_in, per_image(x, first)] + [whole(entry) for entry in weights_in],
+            [part_image((tokens, 3 * HALF), BF, first), part_image((tokens, channels), BF, first)]
+            + [new_image(piece_in, BF, pair)] * ways
+            + (
+                [new_whole(qkv_shape, BF), new_whole((16, channels), F32), new_whole((1, hidden_width), F32)]
+                if assembles
+                else []
+            ),
+            [pltpu.VMEM((rows, wide, channels), BF)],
+            6,
+            alias=[(entry, place) for place, entry in enumerate(whole_images)],
+        )
+        whole_images = results[:2]
+        normed_pieces.append(exchange(results[2 : 2 + ways]))
+        if assembles:
+            qkv_low, small_full, bias_full = results[2 + ways :]
+            weights_in = (qkv_low, small_full)
+    across_mixed, normed = whole_images
+    small_in, qkv_in = whole(small_full), whole(qkv_low)
+
+    attention_dims = (rows, width, kept, key_rows, chunk)
+    key_shape = (key_rows, channels)
+    across = []
+
+    def run_across(first, images_in, after):
+        return run_kernel(
+            functools.partial(across_kernel, attention_dims, first),
+            images_in,
+            [per_image(across_mixed, first), mask_in, small_in],
+            [
+                part_image((tokens, HALF), BF, first),
+                part_image((tokens, HALF), F32, first),
+                part_image((tokens, HALF), F32, first),
+                part_image(key_shape, BF, first),
+                part_image(key_shape, BF, first),
+            ],
+            [pltpu.VMEM((tokens, HALF), F32)],
+            11 * images_in,
+            after=after,
+            alias=[(entry, place) for place, entry in enumerate(across)],
+        )
+
+    across, token = run_across(0, count - 1, (token,))
+    (late,), token = run_kernel(
+        pack_late_kernel,
+        1,
+        [whole(out_weight), whole(expand_weight), whole(shrink_weight)],
+        [new_whole((shard, channels + 2 * hidden_width), BF)],
+        [],
+        2,
+        after=(token,),
+    )
     late_pieces = exchange([late] * ways)
-    small_in, qkv_in = whole(small_full), whole(qkv_low)
-
-    attention_dims = (rows, width, kept, key_rows, chunk)
-    key_shape = (key_rows, 2 * HALF)
-    joined_across, attended, log_total, keys, values = run_kernel(
-        functools.partial(across_kernel, attention_dims),
-        count,
-        [per_image(across_mixed), mask_in, small_in],
-        [
-            new_image((tokens, HALF), BF, count),
-            new_image((tokens, HALF), F32, count),
-            new_image((tokens, HALF), F32, count),
-            new_image(key_shape, BF, count),
-            new_image(key_shape, BF, count),
-        ],
-        [pltpu.VMEM((tokens, HALF), F32)],
-        60,
-    )
-    last_result = attended
+    normed_pieces, token = lax.optimization_barrier((normed_pieces, token))
 
     down_dims = (height, width, wide, wide_part, spare)
     grid_f32 = (height, wide_part, HALF)
     mixed_grid = (height, wide_part, 3 * HALF)
     normed_grid = (height, wide_part, channels)
     down, joined_pieces = [], []
-    for index, first in enumerate(halves):
-        results = run_kernel(
+    for index, first in enumerate((0, pair)):
+        results, token = run_kernel(
             functools.partial(down_kernel, down_dims, ways, first),
             pair,
-            [me_in, mask_in, small_in, qkv_in] + [per_image(piece, first) for piece in normed_pieces],
-            [new_image(piece_out, BF)] * ways
-            + [new_image(grid_f32, F32)] * 2
-            + [new_image(mixed_grid, BF)],
+            [me_in, mask_in, small_in, qkv_in] + [per_image(piece) for piece in normed_pieces[index]],
+            [new_image(piece_out, BF, pair)] * ways
+            + [part_image(grid_f32, F32, first)] * 2
+            + [part_image(mixed_grid, BF, first), part_image(normed_grid, BF, first)],
             [
-                pltpu.VMEM(normed_grid, BF),
                 pltpu.VMEM(mixed_grid, F32),
                 pltpu.VMEM(grid_f32, F32),
                 pltpu.VMEM((wide, HALF), F32),
                 pltpu.VMEM((window_tokens, HALF), F32),
             ],
-            18,
-            after=(last_result,),
+            15,
+            after=(token,),
+            alias=[(entry, ways + place) for place, entry in enumerate(down)],
         )
-        down.append(results[ways:])
+        down = results[ways:]
         joined_pieces.append(exchange(results[:ways]))
-        last_result = results[ways]
-
-    block_out = None
-    grad_middle, grad_across, grad_pieces = [], [], []
-    sums = None
+    across, token = run_across(count - 1, 1, (token,))
+    joined_across, attended, log_total, keys, values = across
+
     matrix_sums = [(channels, channels), (channels, hidden_width), (channels, hidden_width)]
-    late_shape = late.shape
-    for index, first in enumerate(halves):
-        last = index == 1
-        results = run_kernel(
-            functools.partial(
-                middle_kernel, (rows, width, wide, wide_part, tokens // 2, channels), ways, last
-            ),
-            pair,
-            [
-                me_in,
-                (x, image_block(tokens, channels, first=first)),
-                (cot, image_block(tokens, channels, first=first)),
-                per_image(joined_across, first),
-            ]
-            + [per_image(piece) for piece in joined_pieces[index]]
-            + [whole(piece) for piece in late_pieces]
-            + [small_in, whole(bias_full)]
-            + ([whole(entry) for entry in sums] if last else []),
-            [
-                (x.shape, F32, image_block(tokens, channels, first=first)),
-                new_image((tokens, channels), F32),
-                new_image((tokens, HALF), BF),
-            ]
-            + [new_image(piece_out, BF)] * ways
-            + [new_whole((8, hidden_width), F32), new_whole((32, channels), F32)]
-            + (
-                [new_whole(late_shape, F32)] * ways
-                if last
-                else [new_whole(dims, F32) for dims in matrix_sums]
-            ),
-            ([pltpu.VMEM(dims, F32) for dims in matrix_sums] if last else [])
-            + [
-                pltpu.VMEM((channels, channels), BF),
-                pltpu.VMEM((channels, hidden_width), BF),
-                pltpu.VMEM((hidden_width, channels), BF),
-                pltpu.VMEM((rows, wide, HALF), BF),
-                pltpu.VMEM((tokens, channels), BF),
-                pltpu.VMEM((tokens, channels), BF),
-                pltpu.VMEM((tokens, hidden_width), BF),
-                pltpu.VMEM((tokens, hidden_width), BF),
-                pltpu.VMEM((tokens, channels), BF),
-                pltpu.VMEM((tokens, HALF), BF),
-                pltpu.VMEM((rows, wide, HALF), BF),
-            ]
-            + ([pltpu.VMEM((hidden_width, channels), F32)] if last else []),
-            35,
-            after=(last_result,),
-            alias=(block_out, 0) if last else None,
-        )
-        block_out = results[0]
-        grad_middle.append(results[1])
-        grad_across.append(results[2])
-        grad_pieces.append(exchange(results[3 : 3 + ways]))
-        sums = results[3 + ways :]
-        last_result = results[1]
-    bias_sums, middle_sums = sums[:2]
-    late_seq = tree_sum(exchange(sums[2:]))
-    late_stages = [late_seq] + sum_halves(late_seq)
-
-    grad_normed_pieces = []
-    sums = None
+    results, token = run_kernel(
+        functools.partial(middle_kernel, (rows, width, wide, wide_part, tokens // 2, channels), ways),
+        count,
+        [me_in, per_image(x), per_image(cot), per_image(joined_across)]
+        + [half_images(piece, 0) for piece in joined_pieces[0]]
+        + [half_images(piece, pair) for piece in joined_pieces[1]]
+        + [whole(piece) for piece in late_pieces]
+        + [small_in, whole(bias_full)],
+        [
+            new_image((tokens, channels), F32, count),
+            new_image((tokens, channels), F32, count),
+            new_image((tokens, HALF), BF, count),
+        ]
+        + [new_image(piece_out, BF, count)] * ways
+        + [new_whole((8, hidden_width), F32), new_whole((32, channels), F32)]
+        + [new_whole(late.shape, F32)] * ways,
+        [pltpu.VMEM(dims, F32) for dims in matrix_sums]
+        + [
+            pltpu.VMEM((channels, channels), BF),
+            pltpu.VMEM((channels, hidden_width), BF),
+            pltpu.VMEM((hidden_width, channels), BF),
+            pltpu.VMEM((rows, wide, HALF), BF),
+            pltpu.VMEM((tokens, channels), BF),
+            pltpu.VMEM((tokens, channels), BF),
+            pltpu.VMEM((tokens, hidden_width), BF),
+            pltpu.VMEM((tokens, hidden_width), BF),
+            pltpu.VMEM((tokens, channels), BF),
+            pltpu.VMEM((tokens, HALF), BF),
+            pltpu.VMEM((rows, wide, HALF), BF),
+            pltpu.VMEM((hidden_width, channels), F32),
+        ],
+        45,
+        after=(token,),
+    )
+    block_out, grad_middle, grad_across = results[:3]
+    grad_pieces = exchange(results[3 : 3 + ways])
+    bias_sums, middle_sums, *late_sums = results[3 + ways :]
+
     qkv_half = (channels, 3 * HALF)
     half_shard = (shard, 3 * HALF)
-    for index, first in enumerate(halves):
-        last = index == 1
-        results = run_kernel(
-            functools.partial(down_back_kernel, down_dims, ways, first, last),
-            pair,
-            [me_in, mask_in, small_in, qkv_in]
-            + [per_image(entry) for entry in down[index]]
-            + [per_image(piece, first) for piece in normed_pieces]
-            + [per_image(piece) for piece in grad_pieces[index]]
-            + ([whole(entry) for entry in sums] if last else []),
-            [new_image(piece_in, BF)] * ways
-            + [new_whole((80, HALF), F32)]
-            + ([new_whole(half_shard, F32)] * ways if last else [new_whole(qkv_half, F32)]),
-            ([pltpu.VMEM(qkv_half, F32)] if last else [])
-            + [
-                pltpu.VMEM(normed_grid, BF),
-                pltpu.VMEM(mixed_grid, F32),
-                pltpu.VMEM(grid_f32, F32),
-                pltpu.VMEM(mixed_grid, F32),
-                pltpu.VMEM(normed_grid, BF),
-                pltpu.VMEM((wide, HALF), F32),
-            ],
-            28,
-            after=(last_result, late_stages[0]) if last else (last_result,),
-        )
-        grad_normed_pieces.append(exchange(results[:ways]))
-        sums = results[ways:]
-        last_result = sums[0]
-    down_taps = sums[0]
-    down_seq = tree_sum(exchange(sums[1:]))
-    down_core = sum_cores(down_seq)
-
-    across_mixed_grad = []
-    sums = None
-    for index, first in enumerate(halves):
-        last = index == 1
-        results = run_kernel(
-            functools.partial(across_back_kernel, attention_dims, ways, first, last),
-            pair,
+    back_sums, norm_sums, input_grad = None, None, None
+
+    def run_across_back(first, images_in, sums, after):
+        results, token = run_kernel(
+            functools.partial(
+                across_back_kernel, (rows, width, kept, key_rows, tokens // 2), first, sums is not None
+            ),
+            images_in,
             [
-                me_in,
                 per_image(across_mixed, first),
-                per_image(grad_across[index]),
+                per_image(grad_across, first),
                 per_image(attended, first),
                 per_image(log_total, first),
                 per_image(keys, first),
@@ -1175,103 +1209,134 @@
                 mask_in,
                 small_in,
             ]
-            + ([whole(entry) for entry in sums] if last else []),
-            [new_image((tokens, 3 * HALF), BF), new_whole((80, HALF), F32)]
-            + ([new_whole(half_shard, F32)] * ways if last else [new_whole(qkv_half, F32)]),
-            ([pltpu.VMEM(qkv_half, F32)] if last else [])
-            + [
+            + ([whole(entry) for entry in sums[1:]] if sums else []),
+            [
+                part_image((tokens, 3 * HALF), BF, first),
+                new_whole((80, HALF), F32),
+                new_whole(qkv_half, F32),
+            ],
+            [
                 pltpu.VMEM((HALF, key_rows), F32),
                 pltpu.VMEM((HALF, key_rows), F32),
                 pltpu.VMEM((tokens, HALF), F32),
             ],
-            45,
-            after=(last_result, late_stages[2], down_seq) if last else (last_result, late_stages[1]),
+            23 * images_in,
+            after=after,
+            alias=[(sums[0], 0)] if sums else [],
         )
-        across_mixed_grad.append(results[0])
-        sums = results[1:]
-        last_result = sums[0]
-    across_taps = sums[0]
-    across_seq = tree_sum(exchange(sums[1:]))
-    across_core = sum_cores(across_seq)
-
-    input_grad = None
-    sums = None
-    for index, first in enumerate(halves):
-        last = index == 1
-        results = run_kernel(
+        return results, token
+
+    def run_final(first, images_in, starts, others, after):
+        last = others is not None
+        return run_kernel(
             functools.partial(final_kernel, (rows, width, wide, wide_part, tokens), ways, last),
-            pair,
-            [
-                me_in,
-                (x, image_block(tokens, channels, first=first)),
-                per_image(grad_middle[index]),
-                per_image(across_mixed_grad[index]),
-            ]
-            + [per_image(piece) for piece in grad_normed_pieces[index]]
+            images_in,
+            [me_in, per_image(x, first), per_image(grad_middle, first), per_image(back_sums[0], first)]
+            + [per_image(piece, first) for piece in grad_normed_pieces]
             + [small_in, qkv_in]
-            + (
-                [whole(entry) for entry in (*sums, across_taps, down_taps, middle_sums, bias_sums)]
-                if last
-                else []
-            ),
-            [
-                (x.shape, F32, image_block(tokens, channels, first=first)),
-                new_whole((16, channels), F32),
-            ]
-            + ([new_whole((24, channels), F32)] if last else []),
-            [pltpu.VMEM((rows, wide, channels), BF), pltpu.VMEM((tokens, channels), F32)],
-            8,
-            after=(last_result, across_seq) if last else (last_result, late_stages[-1], down_core),
-            alias=(input_grad, 0) if last else None,
+            + ([whole(entry) for entry in (starts[1], *others)] if last else []),
+            [part_image((tokens, channels), F32, first), new_whole((16, channels), F32)]
+            + ([new_whole((shard + 32, 3 * HALF), BF)] * ways if last else []),
+            [pltpu.VMEM((rows, wide, channels), BF), pltpu.VMEM((tokens, channels), F32)]
+            + ([pltpu.VMEM((32, channels), F32)] if last else []),
+            4 * images_in,
+            after=after,
+            alias=[(starts[0], 0)] if last else [],
         )
-        input_grad = results[0]
-        sums = results[1:]
-        last_result = sums[0]
-    small_sum = tree_sum(exchange([results[2]] * ways))
-    small_sum = sum_chips(sum_cores(small_sum))
-    shard_late = join_halves(late_stages[-1])
-    shard_down, shard_across = sum_chips(down_core), sum_chips(across_core)
-
-    squared = sum(jnp.sum(entry * entry) for entry in (shard_late, shard_down, shard_across))
-    squared = tree_sum(exchange([jnp.full((8, 128), squared)] * ways))[0, 0]
-    grad_norm = jnp.sqrt(squared + jnp.sum(small_sum * small_sum))
-    factor = CLIP_NORM / jnp.maximum(grad_norm, CLIP_NORM)
-    matrices = (
-        (qkv_weight, out_weight, expand_weight, shrink_weight)
-        + (first_qkv, first_out, first_expand, first_shrink)
-        + (second_qkv, second_out, second_expand, second_shrink)
-    )
-    updated = run_kernel(
-        functools.partial(update_kernel, blocks),
+
+    back_sums, token = run_across_back(0, 1, None, (token,))
+    *late_sums, token = lax.optimization_barrier((*late_sums, token))
+    late_parts = exchange(late_sums)
+    results, token = run_kernel(
+        functools.partial(down_back_kernel, down_dims, ways),
+        count,
+        [me_in, mask_in, small_in, qkv_in]
+        + [per_image(entry) for entry in down]
+        + [per_image(piece) for piece in grad_pieces],
+        [new_image(piece_in, BF, count)] * ways
+        + [new_whole((80, HALF), F32)]
+        + [new_whole(half_shard, F32)] * ways,
+        [
+            pltpu.VMEM(qkv_half, F32),
+            pltpu.VMEM(mixed_grid, F32),
+            pltpu.VMEM(grid_f32, F32),
+            pltpu.VMEM(mixed_grid, F32),
+            pltpu.VMEM(normed_grid, BF),
+            pltpu.VMEM((wide, HALF), F32),
+        ],
+        38,
+        after=(token,),
+    )
+    grad_normed_pieces = exchange(results[:ways])
+    down_taps, *down_sums = results[ways:]
+    late_parts, token = lax.optimization_barrier((late_parts, token))
+    late_seq = tree_sum(late_parts)
+    core_place = lax.axis_index("img") % 2
+    half = shard // 2
+    down_parts = exchange(down_sums)
+    back_sums, token = run_across_back(1, count - 2, back_sums, (token, late_seq))
+    down_parts, late_seq, token = lax.optimization_barrier((down_parts, late_seq, token))
+    seq_sum = jnp.concatenate([late_seq, tree_sum(down_parts)], axis=1)
+    kept_half = lax.dynamic_slice_in_dim(seq_sum, core_place * half, half, 0)
+    core_half = swap(lax.dynamic_slice_in_dim(seq_sum, (1 - core_place) * half, half, 0), "img", 1)
+    (input_grad, norm_sums), token = run_final(0, count - 1, None, None, (token,))
+    kept_half, core_half, token = lax.optimization_barrier((kept_half, core_half, token))
+    halves_sum = kept_half + core_half
+    chip_half = swap(halves_sum, "img", chip_steps[0])
+    back_sums, token = run_across_back(count - 1, 1, back_sums, (token,))
+    chip_half, halves_sum, token = lax.optimization_barrier((chip_half, halves_sum, token))
+    halves_sum = halves_sum + chip_half
+    chip_half = [swap(halves_sum, "img", distance) for distance in chip_steps[1:2]]
+    (input_grad, _, *tail_sums), token = run_final(
+        count - 1,
         1,
-        [(factor.reshape(1), scalar_block())]
-        + [whole(entry) for entry in (shard_late, shard_across, shard_down, *matrices)],
-        [new_whole(entry.shape, F32) for entry in matrices[:4]] * 3,
-        [],
+        (input_grad, norm_sums),
+        (back_sums[1], down_taps, middle_sums, bias_sums, back_sums[2]),
+        (token,),
+    )
+    tail_parts, halves_sum, chip_half = lax.optimization_barrier(
+        (exchange(tail_sums), halves_sum, chip_half)
+    )
+    halves_sum = tree_sum([halves_sum, *chip_half])
+    for distance in chip_steps[2:]:
+        halves_sum = halves_sum + swap(halves_sum, "img", distance)
+    other_half = swap(halves_sum, "img", 1)
+    tail = tree_sum([part.astype(F32) for part in tail_parts])
+    tail = tree_sum(share_low(tail, [1]))
+    tail = tree_sum(share_low(tail, range(2, lax.axis_size("img"), 2)))
+
+    squared = (
+        jnp.sum(halves_sum * halves_sum)
+        + jnp.sum(other_half * other_half)
+        + jnp.sum(tail[:shard] * tail[:shard])
+    )
+    squares = exchange([jnp.full((8, 128), squared)] * ways)
+
+    def as_rows(entries):
+        return [entry.reshape(1, -1) if entry.ndim == 1 else entry for entry in entries]
+
+    state = as_rows(
+        (qkv_weight, out_weight, expand_weight, shrink_weight, small_params, expand_bias)
+        + (first_qkv, first_out, first_expand, first_shrink, first_small, first_bias)
+        + (second_qkv, second_out, second_expand, second_shrink, second_small, second_bias)
+    )
+    place_in = jnp.stack([owner, core_place]).astype(jnp.int32)
+    (norm, *updated), _ = run_kernel(
+        functools.partial(update_kernel, ways),
+        1,
+        [(place_in, scalar_block())]
+        + [whole(entry) for entry in (halves_sum, other_half, tail, *squares, *state)],
+        [((1, 1), F32, scalar_block())] + [new_whole(entry.shape, F32) for entry in state[:6]] * 3,
+        [pltpu.VMEM((shard, halves_sum.shape[1]), F32)],
         4,
     )
-    small_rows = small_params.shape[0]
-    small_grad = lax.dynamic_slice_in_dim(
-        small_sum[:small_rows], owner * small_params.shape[1], small_params.shape[1], 1
-    )
-    bias_grad = lax.dynamic_slice_in_dim(
-        small_sum[small_rows : small_rows + blocks].reshape(-1),
-        owner * expand_bias.shape[0],
-        expand_bias.shape[0],
-        0,
-    )
-    small_new = adam_update(
-        small_params, first_small, second_small, small_grad * factor, RATE_SMALL, 0.0
-    )
-    bias_new = adam_update(expand_bias, first_bias, second_bias, bias_grad * factor, RATE_MATRIX, 0.0)
-    outputs = []
-    for part in range(3):
-        outputs += [*updated[4 * part : 4 * part + 4], small_new[part], bias_new[part]]
+    for index in (5, 11, 17):
+        updated[index] = updated[index].reshape(-1)
     return (
         block_out.reshape(images.shape),
         input_grad.reshape(images.shape),
-        grad_norm,
-        *outputs,
+        norm.reshape(()),
+        *updated,
     )
 
 

time: 448 us -> 384 us (0.86)
  starting transfers between devices: 77.5 us -> 52 us
  waiting for transfers between devices: 41.5 us -> 20.6 us
  other arithmetic: 21 us -> 9.34 us
  Pallas kernels: 295 us -> 290 us
    ppermute x58 -> x44, starting transfers between devices: 77.5 us -> 52 us  [swap(): lax.ppermute(value, axis, [(place, place ^ distance) for place in range(l...]
    ppermute x58 -> x44, waiting for transfers between devices: 41.5 us -> 20.6 us  [swap(): lax.ppermute(value, axis, [(place, place ^ distance) for place in range(l...]
    pallas_call x13 -> x16, Pallas kernels: 295 us -> 290 us  [run_kernel(): pl.pallas_call(wrapped, grid=(images,), in_specs=[spec for _, spec in inp...]
    add x6 -> x2, other arithmetic: 4.94 us -> 0.08 us  [the longest x1 0.04 us: on_device(): halves_sum = kept_half + core_half]
  transfers between devices with their start and end apart: 58 -> 44, of which waited for: 15 -> 11; matrix products, arithmetic and copies ran while one was open for 4% -> 2% of each run, Pallas kernels for 61% -> 62%
where the time goes in v4:
time: 384 us; the launch traced here: 381 us
  Pallas kernels  290 us (76%)
  starting transfers between devices  52 us (14%)
  waiting for transfers between devices  20.6 us (5%)
  other arithmetic  9.34 us (2%)
  local copies, waits for them, and re-layouts  5.44 us (1%)
    pallas_call x16, Pallas kernels, run_kernel(): pl.pallas_call(wrapped, grid=(images,), in_specs=[spec for _, spec in inp...  290 us
    ppermute x44, starting transfers between devices, swap(): lax.ppermute(value, axis, [(place, place ^ distance) for place in range(l...  52 us
    ppermute x44, waiting for transfers between devices, swap(): lax.ppermute(value, axis, [(place, place ^ distance) for place in range(l...  20.6 us
  transfers between devices with their start and end apart: 44, of which 11 were waited for; matrix products, arithmetic and copies ran while one was open for 2% of the time, Pallas kernels for 62%

profile of v4, /device:TPU:0, one launch (start us, length us, event | category | flops | bytes accessed | tf_op | source)
XLA Modules:
  0.0 380.6 jit_solution(16376337843238847053)
XLA Ops:
  0.7 1.7 shard_map.364
  2.3 2.9 collective-permute-start
  6.8 2.5 collective-permute-done.refs_3_
  9.3 3.7 collective-permute-done.1.refs_4_
  13.7 6.2 %shard_map.365 = (bf16[4,1568,384]{2,1,0:T(8,128)(2,1)}, bf16[4,1568,256]{2,1,0:T(8,128)(2,1)}, bf16[2,7,64,256]{3,2,1,0:T(8,128)(2,1)}, bf16[2,7,64,256]{3,2,1,...) custom-call(s32[1]{0:T(128)} %bitcast.refs_0_, ...), custom_call_target="tpu_custom_call" | custom-call | flops 6000000000 | bytes 6000000 | tf_op jit(solution)/shard_map/pallas_call | solution.py:931
  23.5 5.4 %shard_map.366 = (bf16[4,1568,384]{2,1,0:T(8,128)(2,1)}, bf16[4,1568,256]{2,1,0:T(8,128)(2,1)}, bf16[2,7,64,256]{3,2,1,0:T(8,128)(2,1)}, bf16[2,7,64,256]{3,2,1,...) custom-call(s32[1]{0:T(128)} %bitcast.refs_0_, ...), custom_call_target="tpu_custom_call", output_to_operand_aliasing={{0}: (4, {}), {1}: (5, {})} | custom-call | flops 6000000000 | bytes 6000000 | tf_op jit(solution)/shard_map/pallas_call | solution.py:931
  30.9 2.8 collective-permute-done.3.refs_5_
  35.0 33.5 %shard_map.367 = (bf16[4,1568,128]{2,1,0:T(8,128)(2,1)}, f32[4,1568,128]{2,1,0:T(8,128)}, f32[4,1568,128]{2,1,0:T(8,128)}, bf16[4,1280,256]{2,1,0:T(8,128)(2,1)}...) custom-call(bf16[4,1568,384]{2,1,0:T(8,128)(2,1)} %get-tuple-element.175.refs_0_, s32[4,224]{1,0:T(4,128)} %refs_7_.5, ...), custom_call_target="tpu_custom_call" | custom-call | flops 32999999488 | bytes 33000000 | tf_op jit(solution)/shard_map/pallas_call | solution.py:931
  68.6 1.8 shard_map.368
  74.0 15.8 %shard_map.369 = (bf16[2,7,64,128]{3,2,1,0:T(8,128)(2,1)}, bf16[2,7,64,128]{3,2,1,0:T(8,128)(2,1)}, bf16[2,7,64,128]{3,2,1,0:T(8,128)(2,1)}, bf16[2,7,64,128]{3,...) custom-call(s32[1]{0:T(128)} %bitcast.refs_0_, ...), custom_call_target="tpu_custom_call" | custom-call | flops 15000000512 | bytes 15000000 | tf_op jit(solution)/shard_map/pallas_call | solution.py:931
  89.8 1.6 collective-permute-start.9
  92.0 15.5 %shard_map.370 = (bf16[2,7,64,128]{3,2,1,0:T(8,128)(2,1)}, bf16[2,7,64,128]{3,2,1,0:T(8,128)(2,1)}, bf16[2,7,64,128]{3,2,1,0:T(8,128)(2,1)}, bf16[2,7,64,128]{3,...) custom-call(s32[1]{0:T(128)} %bitcast.refs_0_, ...), custom_call_target="tpu_custom_call", output_to_operand_aliasing={{4}: (9, {}), {5}: (10, {}), {6}: (11, {}), {7}: (12, {})} | custom-call | flops 15000000512 | bytes 15000000 | tf_op jit(solution)/shard_map/pallas_call | solution.py:931
  112.5 13.3 %shard_map.371 = (bf16[4,1568,128]{2,1,0:T(8,128)(2,1)}, f32[4,1568,128]{2,1,0:T(8,128)}, f32[4,1568,128]{2,1,0:T(8,128)}, bf16[4,1280,256]{2,1,0:T(8,128)(2,1)}...) custom-call(bf16[4,1568,384]{2,1,0:T(8,128)(2,1)} %get-tuple-element, ...), custom_call_target="tpu_custom_call", output_to_operand_aliasing={{0}: (4, {}), {1}: (5, {}), {2}: (6, {}), {3}: (7, {}), {4}... | custom-call | flops 11000000512 | bytes 11000000 | tf_op jit(solution)/shard_map/pallas_call | solution.py:931
  126.9 43.9 %shard_map.372 = (f32[4,1568,256]{2,1,0:T(8,128)}, f32[4,1568,256]{2,1,0:T(8,128)}, bf16[4,1568,128]{2,1,0:T(8,128)(2,1)}, bf16[4,7,64,128]{3,2,1,0:T(8,128)(2,1...) custom-call(s32[1]{0:T(128)} %bitcast.refs_0_, ...), custom_call_target="tpu_custom_call" | custom-call | flops 44999999488 | bytes 45000000 | tf_op jit(solution)/shard_map/pallas_call | solution.py:931
  170.8 1.6 collective-permute-start.21
  174.3 24.7 %shard_map.373 = (bf16[4,1568,384]{2,1,0:T(8,128)(2,1)}, f32[80,128]{1,0:T(8,128)}, f32[256,384]{1,0:T(8,128)}, f32[8,128]{1,0:T(8,128)}) custom-call(bf16[4,1568,384]{2,1,0:T(8,128)(2,1)} %get-tuple-element.175.refs_0_, bf16[4,1568,128]{2,1,0:T(8,128)(2,1)} %get-tuple-element.221.refs_1_, f32[4,1568,128]{2,1,0:T(8,128)} %get-tuple-element.222.refs_2_, ...), custom_call_target="tpu_custom_call" | custom-call | flops 23000000512 | bytes 23000000 | tf_op jit(solution)/shard_map/pallas_call | solution.py:931
  203.5 37.2 %shard_map.374 = (bf16[4,7,64,256]{3,2,1,0:T(8,128)(2,1)}, bf16[4,7,64,256]{3,2,1,0:T(8,128)(2,1)}, bf16[4,7,64,256]{3,2,1,0:T(8,128)(2,1)}, bf16[4,7,64,256]{3,...) custom-call(s32[1]{0:T(128)} %bitcast.refs_0_, ...), custom_call_target="tpu_custom_call" | custom-call | flops 38000001024 | bytes 38000000 | tf_op jit(solution)/shard_map/pallas_call | solution.py:931
  240.7 1.6 collective-permute-start.24
  247.2 2.0 add_add_fusion.refs_12_
  250.6 46.0 %shard_map.375 = (bf16[4,1568,384]{2,1,0:T(8,128)(2,1)}, f32[80,128]{1,0:T(8,128)}, f32[256,384]{1,0:T(8,128)}, f32[8,128]{1,0:T(8,128)}) custom-call(bf16[4,1568,384]{2,1,0:T(8,128)(2,1)} %get-tuple-element.175.refs_0_, bf16[4,1568,128]{2,1,0:T(8,128)(2,1)} %get-tuple-element.221.refs_1_, ...), custom_call_target="tpu_custom_call", output_to_operand_aliasing={{0}: (13, {})} | custom-call | flops 46000001024 | bytes 46000000 | tf_op jit(solution)/shard_map/pallas_call | solution.py:931
  299.9 10.9 %shard_map.376 = (f32[4,1568,256]{2,1,0:T(8,128)}, f32[16,256]{1,0:T(8,128)}, f32[8,128]{1,0:T(8,128)}) custom-call(s32[1]{0:T(128)} %bitcast.refs_0_, bf16[4,1568,256]{2,1,0:T(8,128)(2,1)} %bitcast.17, f32[4,1568,256]{2,1,0:T(8,128)} %get-tuple-element.220.refs_2_, bf16[4,1568,384]{2,1,0:T(8,128)(2,1)} %get-tuple-element.267.refs_3_.refs_12_, ...), custom_call_target="tpu_custom_call" | custom-call | flops 12000000000 | bytes 12000000 | tf_op jit(solution)/shard_map/pallas_call | solution.py:931
  310.9 2.7 collective-permute-start.31
  313.5 24.6 %shard_map.377 = (bf16[4,1568,384]{2,1,0:T(8,128)(2,1)}, f32[80,128]{1,0:T(8,128)}, f32[256,384]{1,0:T(8,128)}, f32[8,128]{1,0:T(8,128)}) custom-call(bf16[4,1568,384]{2,1,0:T(8,128)(2,1)} %get-tuple-element.175.refs_0_, bf16[4,1568,128]{2,1,0:T(8,128)(2,1)} %get-tuple-element.221.refs_1_, ...), custom_call_target="tpu_custom_call", output_to_operand_aliasing={{0}: (12, {})} | custom-call | flops 23000000512 | bytes 23000000 | tf_op jit(solution)/shard_map/pallas_call | solution.py:931
  338.2 1.6 collective-permute-start.35
  339.8 5.4 %shard_map.378 = (f32[4,1568,256]{2,1,0:T(8,128)}, f32[16,256]{1,0:T(8,128)}, bf16[96,384]{1,0:T(8,128)(2,1)}, bf16[96,384]{1,0:T(8,128)(2,1)}, bf16[96,384]{1,0...) custom-call(s32[1]{0:T(128)} %bitcast.refs_0_, ...), custom_call_target="tpu_custom_call", output_to_operand_aliasing={{0}: (17, {})} | custom-call | flops 4000000000 | bytes 4000000 | tf_op jit(solution)/shard_map/pallas_call | solution.py:931
  349.8 2.2 collective-permute-done.33
  356.3 1.7 collective-permute-start.39
  358.0 2.5 collective-permute-start.38
  361.1 1.9 collective-permute-done.40
  363.1 2.0 collective-permute-done.39
  374.1 1.8 collective-permute-done.43.refs_7_
  376.4 3.9 %shard_map.379 = (f32[1,1]{1,0:T(1,128)}, f32[64,768]{1,0:T(8,128)}, f32[64,256]{1,0:T(8,128)}, f32[64,1024]{1,0:T(8,128)}, f32[256,256]{1,0:T(8,128)}, /*index=...) custom-call(s32[2]{0:T(128)} %pad_add_fusion.refs_0_, ...), custom_call_target="tpu_custom_call" | custom-call | flops 4000000000 | bytes 4000000 | tf_op jit(solution)/shard_map/pallas_call | solution.py:931
  (157 shorter events, 52.5 us)
Async XLA Ops:
  5.3 7.7 %collective-permute-start.1 = (bf16[80,768]{1,0:T(8,128)(2,1)}, bf16[80,768]{1,0:T(8,128)(2,1)S(1)}, u32[]{:S(2)}, u32[]{:S(2)}) collective-permute-start(bf16[80,768]{1,0:T(8,128)(2,1)} %get-tuple-element.170.refs_2_), channel_id=1, source_target_pairs={{0,2},{1,3},{2,0},{3,1},{4,6},{5,7},{6,4},{7,5},{8,10},{9,11},{10,... | collective-permute-start | bytes 368648 | tf_op jit(solution)/shard_map/ppermute | solution.py:959
  19.9 13.7 %collective-permute-start.3 = (bf16[2,7,64,256]{3,2,1,0:T(8,128)(2,1)}, bf16[2,7,64,256]{3,2,1,0:T(8,128)(2,1)S(1)}, u32[]{:S(2)}, u32[]{:S(2)}) collective-permute-start(bf16[2,7,64,256]{3,2,1,0:T(8,128)(2,1)} %get-tuple-element.177), channel_id=1, source_target_pairs={{0,1},{1,0},{2,3},{3,2},{4,5},{5,4},{6,7},{7,6},{8,9},{9,8},{10,11... | collective-permute-start | bytes 1376264 | tf_op jit(solution)/shard_map/ppermute | solution.py:959
  21.1 49.3 %collective-permute-start.4 = (bf16[2,7,64,256]{3,2,1,0:T(8,128)(2,1)}, bf16[2,7,64,256]{3,2,1,0:T(8,128)(2,1)S(1)}, u32[]{:S(2)}, u32[]{:S(2)}) collective-permute-start(bf16[2,7,64,256]{3,2,1,0:T(8,128)(2,1)} %get-tuple-element.178), channel_id=1, source_target_pairs={{0,2},{1,3},{2,0},{3,1},{4,6},{5,7},{6,4},{7,5},{8,10},{9,11},{10,... | collective-permute-start | bytes 1376264 | tf_op jit(solution)/shard_map/ppermute | solution.py:959
  21.9 50.0 %collective-permute-start.5 = (bf16[2,7,64,256]{3,2,1,0:T(8,128)(2,1)}, bf16[2,7,64,256]{3,2,1,0:T(8,128)(2,1)S(1)}, u32[]{:S(2)}, u32[]{:S(2)}) collective-permute-start(bf16[2,7,64,256]{3,2,1,0:T(8,128)(2,1)} %get-tuple-element.179), channel_id=1, source_target_pairs={{0,3},{1,2},{2,1},{3,0},{4,7},{5,6},{6,5},{7,4},{8,11},{9,10},{10,... | collective-permute-start | bytes 1376264 | tf_op jit(solution)/shard_map/ppermute | solution.py:959
  28.9 43.6 %collective-permute-start.6 = (bf16[2,7,64,256]{3,2,1,0:T(8,128)(2,1)}, bf16[2,7,64,256]{3,2,1,0:T(8,128)(2,1)S(1)}, u32[]{:S(2)}, u32[]{:S(2)}) collective-permute-start(bf16[2,7,64,256]{3,2,1,0:T(8,128)(2,1)} %get-tuple-element.181), channel_id=1, source_target_pairs={{0,1},{1,0},{2,3},{3,2},{4,5},{5,4},{6,7},{7,6},{8,9},{9,8},{10,11... | collective-permute-start | bytes 1376264 | tf_op jit(solution)/shard_map/ppermute | solution.py:959
  30.0 43.9 %collective-permute-start.7 = (bf16[2,7,64,256]{3,2,1,0:T(8,128)(2,1)}, bf16[2,7,64,256]{3,2,1,0:T(8,128)(2,1)S(1)}, u32[]{:S(2)}, u32[]{:S(2)}) collective-permute-start(bf16[2,7,64,256]{3,2,1,0:T(8,128)(2,1)} %get-tuple-element.182), channel_id=1, source_target_pairs={{0,2},{1,3},{2,0},{3,1},{4,6},{5,7},{6,4},{7,5},{8,10},{9,11},{10,... | collective-permute-start | bytes 1376264 | tf_op jit(solution)/shard_map/ppermute | solution.py:959
  33.7 40.3 %collective-permute-start.8 = (bf16[2,7,64,256]{3,2,1,0:T(8,128)(2,1)}, bf16[2,7,64,256]{3,2,1,0:T(8,128)(2,1)S(1)}, u32[]{:S(2)}, u32[]{:S(2)}) collective-permute-start(bf16[2,7,64,256]{3,2,1,0:T(8,128)(2,1)} %get-tuple-element.183), channel_id=1, source_target_pairs={{0,3},{1,2},{2,1},{3,0},{4,7},{5,6},{6,5},{7,4},{8,11},{9,10},{10,... | collective-permute-start | bytes 1376264 | tf_op jit(solution)/shard_map/ppermute | solution.py:959
  70.4 37.2 %collective-permute-start.15 = (bf16[64,2304]{1,0:T(8,128)(2,1)}, bf16[64,2304]{1,0:T(8,128)(2,1)S(1)}, u32[]{:S(2)}, u32[]{:S(2)}) collective-permute-start(bf16[64,2304]{1,0:T(8,128)(2,1)} %get-tuple-element.216.refs_12_), channel_id=1, source_target_pairs={{0,1},{1,0},{2,3},{3,2},{4,5},{5,4},{6,7},{7,6},{8,9},{9,8},{10,11... | collective-permute-start | bytes 884744 | tf_op jit(solution)/shard_map/ppermute | solution.py:959
  71.9 37.1 %collective-permute-start.16 = (bf16[64,2304]{1,0:T(8,128)(2,1)}, bf16[64,2304]{1,0:T(8,128)(2,1)S(1)}, u32[]{:S(2)}, u32[]{:S(2)}) collective-permute-start(bf16[64,2304]{1,0:T(8,128)(2,1)} %get-tuple-element.216.refs_12_), channel_id=1, source_target_pairs={{0,2},{1,3},{2,0},{3,1},{4,6},{5,7},{6,4},{7,5},{8,10},{9,11},{10,... | collective-permute-start | bytes 884744 | tf_op jit(solution)/shard_map/ppermute | solution.py:959
  72.5 38.0 %collective-permute-start.17 = (bf16[64,2304]{1,0:T(8,128)(2,1)}, bf16[64,2304]{1,0:T(8,128)(2,1)S(1)}, u32[]{:S(2)}, u32[]{:S(2)}) collective-permute-start(bf16[64,2304]{1,0:T(8,128)(2,1)} %get-tuple-element.216.refs_12_), channel_id=1, source_target_pairs={{0,3},{1,2},{2,1},{3,0},{4,7},{5,6},{6,5},{7,4},{8,11},{9,10},{10,... | collective-permute-start | bytes 884744 | tf_op jit(solution)/shard_map/ppermute | solution.py:959
  89.8 21.3 %collective-permute-start.9 = (bf16[2,7,64,128]{3,2,1,0:T(8,128)(2,1)}, bf16[2,7,64,128]{3,2,1,0:T(8,128)(2,1)S(1)}, u32[]{:S(2)}, u32[]{:S(2)}) collective-permute-start(bf16[2,7,64,128]{3,2,1,0:T(8,128)(2,1)} %get-tuple-element.209), channel_id=1, source_target_pairs={{0,1},{1,0},{2,3},{3,2},{4,5},{5,4},{6,7},{7,6},{8,9},{9,8},{10,11... | collective-permute-start | bytes 688136 | tf_op jit(solution)/shard_map/ppermute | solution.py:959
  91.4 34.5 %collective-permute-start.10 = (bf16[2,7,64,128]{3,2,1,0:T(8,128)(2,1)}, bf16[2,7,64,128]{3,2,1,0:T(8,128)(2,1)S(1)}, u32[]{:S(2)}, u32[]{:S(2)}) collective-permute-start(bf16[2,7,64,128]{3,2,1,0:T(8,128)(2,1)} %get-tuple-element.210), channel_id=1, source_target_pairs={{0,2},{1,3},{2,0},{3,1},{4,6},{5,7},{6,4},{7,5},{8,10},{9,11},{10,... | collective-permute-start | bytes 688136 | tf_op jit(solution)/shard_map/ppermute | solution.py:959
  107.6 18.4 %collective-permute-start.11 = (bf16[2,7,64,128]{3,2,1,0:T(8,128)(2,1)S(1)}, bf16[2,7,64,128]{3,2,1,0:T(8,128)(2,1)S(1)}, u32[]{:S(2)}, u32[]{:S(2)}) collective-permute-start(bf16[2,7,64,128]{3,2,1,0:T(8,128)(2,1)S(1)} %copy-done.26), channel_id=1, source_target_pairs={{0,3},{1,2},{2,1},{3,0},{4,7},{5,6},{6,5},{7,4},{8,11},{9,10},{10,... | collective-permute-start | bytes 688136 | tf_op jit(solution)/shard_map/ppermute | solution.py:959
  109.0 16.9 %collective-permute-start.12 = (bf16[2,7,64,128]{3,2,1,0:T(8,128)(2,1)}, bf16[2,7,64,128]{3,2,1,0:T(8,128)(2,1)S(1)}, u32[]{:S(2)}, u32[]{:S(2)}) collective-permute-start(bf16[2,7,64,128]{3,2,1,0:T(8,128)(2,1)} %get-tuple-element.213), channel_id=1, source_target_pairs={{0,1},{1,0},{2,3},{3,2},{4,5},{5,4},{6,7},{7,6},{8,9},{9,8},{10,11... | collective-permute-start | bytes 688136 | tf_op jit(solution)/shard_map/ppermute | solution.py:959
  110.5 15.4 %collective-permute-start.13 = (bf16[2,7,64,128]{3,2,1,0:T(8,128)(2,1)}, bf16[2,7,64,128]{3,2,1,0:T(8,128)(2,1)S(1)}, u32[]{:S(2)}, u32[]{:S(2)}) collective-permute-start(bf16[2,7,64,128]{3,2,1,0:T(8,128)(2,1)} %get-tuple-element.214), channel_id=1, source_target_pairs={{0,2},{1,3},{2,0},{3,1},{4,6},{5,7},{6,4},{7,5},{8,10},{9,11},{10,... | collective-permute-start | bytes 688136 | tf_op jit(solution)/shard_map/ppermute | solution.py:959
  111.1 14.9 %collective-permute-start.14 = (bf16[2,7,64,128]{3,2,1,0:T(8,128)(2,1)}, bf16[2,7,64,128]{3,2,1,0:T(8,128)(2,1)S(1)}, u32[]{:S(2)}, u32[]{:S(2)}) collective-permute-start(bf16[2,7,64,128]{3,2,1,0:T(8,128)(2,1)} %get-tuple-element.215), channel_id=1, source_target_pairs={{0,3},{1,2},{2,1},{3,0},{4,7},{5,6},{6,5},{7,4},{8,11},{9,10},{10,... | collective-permute-start | bytes 688136 | tf_op jit(solution)/shard_map/ppermute | solution.py:959
  170.8 30.4 %collective-permute-start.21 = (bf16[4,7,64,128]{3,2,1,0:T(8,128)(2,1)}, bf16[4,7,64,128]{3,2,1,0:T(8,128)(2,1)}, u32[]{:S(2)}, u32[]{:S(2)}) collective-permute-start(bf16[4,7,64,128]{3,2,1,0:T(8,128)(2,1)} %get-tuple-element.244), channel_id=1, source_target_pairs={{0,1},{1,0},{2,3},{3,2},{4,5},{5,4},{6,7},{7,6},{8,9},{9,8},{10,11... | collective-permute-start | bytes 1376264 | tf_op jit(solution)/shard_map/ppermute | solution.py:959
  172.3 30.2 %collective-permute-start.22 = (bf16[4,7,64,128]{3,2,1,0:T(8,128)(2,1)}, bf16[4,7,64,128]{3,2,1,0:T(8,128)(2,1)S(1)}, u32[]{:S(2)}, u32[]{:S(2)}) collective-permute-start(bf16[4,7,64,128]{3,2,1,0:T(8,128)(2,1)} %get-tuple-element.245), channel_id=1, source_target_pairs={{0,2},{1,3},{2,0},{3,1},{4,6},{5,7},{6,4},{7,5},{8,10},{9,11},{10,... | collective-permute-start | bytes 1376264 | tf_op jit(solution)/shard_map/ppermute | solution.py:959
  172.9 29.6 %collective-permute-start.23 = (bf16[4,7,64,128]{3,2,1,0:T(8,128)(2,1)}, bf16[4,7,64,128]{3,2,1,0:T(8,128)(2,1)S(1)}, u32[]{:S(2)}, u32[]{:S(2)}) collective-permute-start(bf16[4,7,64,128]{3,2,1,0:T(8,128)(2,1)} %get-tuple-element.246), channel_id=1, source_target_pairs={{0,3},{1,2},{2,1},{3,0},{4,7},{5,6},{6,5},{7,4},{8,11},{9,10},{10,... | collective-permute-start | bytes 1376264 | tf_op jit(solution)/shard_map/ppermute | solution.py:959
  199.1 43.8 %collective-permute-start.18 = (f32[64,2304]{1,0:T(8,128)}, f32[64,2304]{1,0:T(8,128)S(1)}, u32[]{:S(2)}, u32[]{:S(2)}) collective-permute-start(f32[64,2304]{1,0:T(8,128)} %get-tuple-element.236), channel_id=1, source_target_pairs={{0,1},{1,0},{2,3},{3,2},{4,5},{5,4},{6,7},{7,6},{8,9},{9,8},{10,11... | collective-permute-start | bytes 1769480 | tf_op jit(solution)/shard_map/ppermute | solution.py:959
  200.6 43.7 %collective-permute-start.19 = (f32[64,2304]{1,0:T(8,128)S(1)}, f32[64,2304]{1,0:T(8,128)S(1)}, u32[]{:S(2)}, u32[]{:S(2)}) collective-permute-start(f32[64,2304]{1,0:T(8,128)S(1)} %copy-done.11), channel_id=1, source_target_pairs={{0,2},{1,3},{2,0},{3,1},{4,6},{5,7},{6,4},{7,5},{8,10},{9,11},{10,... | collective-permute-start | bytes 1769480 | tf_op jit(solution)/shard_map/ppermute | solution.py:959
  201.2 44.6 %collective-permute-start.20 = (f32[64,2304]{1,0:T(8,128)}, f32[64,2304]{1,0:T(8,128)S(1)}, u32[]{:S(2)}, u32[]{:S(2)}) collective-permute-start(f32[64,2304]{1,0:T(8,128)} %get-tuple-element.238), channel_id=1, source_target_pairs={{0,3},{1,2},{2,1},{3,0},{4,7},{5,6},{6,5},{7,4},{8,11},{9,10},{10,... | collective-permute-start | bytes 1769480 | tf_op jit(solution)/shard_map/ppermute | solution.py:959
  240.7 8.5 %collective-permute-start.24 = (f32[64,384]{1,0:T(8,128)}, f32[64,384]{1,0:T(8,128)S(1)}, u32[]{:S(2)}, u32[]{:S(2)}) collective-permute-start(f32[64,384]{1,0:T(8,128)} %get-tuple-element.258), channel_id=1, source_target_pairs={{0,1},{1,0},{2,3},{3,2},{4,5},{5,4},{6,7},{7,6},{8,9},{9,8},{10,11... | collective-permute-start | bytes 294920 | tf_op jit(solution)/shard_map/ppermute | solution.py:959
  242.3 54.3 %collective-permute-start.25 = (f32[64,384]{1,0:T(8,128)}, f32[64,384]{1,0:T(8,128)}, u32[]{:S(2)}, u32[]{:S(2)}) collective-permute-start(f32[64,384]{1,0:T(8,128)} %get-tuple-element.259), channel_id=1, source_target_pairs={{0,2},{1,3},{2,0},{3,1},{4,6},{5,7},{6,4},{7,5},{8,10},{9,11},{10,... | collective-permute-start | bytes 294920 | tf_op jit(solution)/shard_map/ppermute | solution.py:959
  242.9 53.7 %collective-permute-start.26 = (f32[64,384]{1,0:T(8,128)}, f32[64,384]{1,0:T(8,128)}, u32[]{:S(2)}, u32[]{:S(2)}) collective-permute-start(f32[64,384]{1,0:T(8,128)} %get-tuple-element.260), channel_id=1, source_target_pairs={{0,3},{1,2},{2,1},{3,0},{4,7},{5,6},{6,5},{7,4},{8,11},{9,10},{10,... | collective-permute-start | bytes 294920 | tf_op jit(solution)/shard_map/ppermute | solution.py:959
  244.3 54.1 %collective-permute-start.28 = (bf16[4,7,64,256]{3,2,1,0:T(8,128)(2,1)}, bf16[4,7,64,256]{3,2,1,0:T(8,128)(2,1)S(1)}, u32[]{:S(2)}, u32[]{:S(2)}) collective-permute-start(bf16[4,7,64,256]{3,2,1,0:T(8,128)(2,1)} %get-tuple-element.269), channel_id=1, source_target_pairs={{0,1},{1,0},{2,3},{3,2},{4,5},{5,4},{6,7},{7,6},{8,9},{9,8},{10,11... | collective-permute-start | bytes 2752520 | tf_op jit(solution)/shard_map/ppermute | solution.py:959
  246.6 51.8 %collective-permute-start.29 = (bf16[4,7,64,256]{3,2,1,0:T(8,128)(2,1)}, bf16[4,7,64,256]{3,2,1,0:T(8,128)(2,1)S(1)}, u32[]{:S(2)}, u32[]{:S(2)}) collective-permute-start(bf16[4,7,64,256]{3,2,1,0:T(8,128)(2,1)} %get-tuple-element.270), channel_id=1, source_target_pairs={{0,2},{1,3},{2,0},{3,1},{4,6},{5,7},{6,4},{7,5},{8,10},{9,11},{10,... | collective-permute-start | bytes 2752520 | tf_op jit(solution)/shard_map/ppermute | solution.py:959
  249.2 49.3 %collective-permute-start.30 = (bf16[4,7,64,256]{3,2,1,0:T(8,128)(2,1)}, bf16[4,7,64,256]{3,2,1,0:T(8,128)(2,1)S(1)}, u32[]{:S(2)}, u32[]{:S(2)}) collective-permute-start(bf16[4,7,64,256]{3,2,1,0:T(8,128)(2,1)} %get-tuple-element.271), channel_id=1, source_target_pairs={{0,3},{1,2},{2,1},{3,0},{4,7},{5,6},{6,5},{7,4},{8,11},{9,10},{10,... | collective-permute-start | bytes 2752520 | tf_op jit(solution)/shard_map/ppermute | solution.py:959
  298.4 12.4 %collective-permute-start.27 = (f32[32,2688]{1,0:T(8,128)}, f32[32,2688]{1,0:T(8,128)S(1)}, u32[]{:S(2)}, u32[]{:S(2)}) collective-permute-start(f32[32,2688]{1,0:T(8,128)} %get-tuple-element.321), channel_id=1, source_target_pairs={{0,4},{4,0},{8,12},{12,8},{16,20},{20,16},{24,28},{28,24},{1,5},{5... | collective-permute-start | bytes 1032200 | tf_op jit(solution)/shard_map/ppermute | solution.py:959
  310.9 27.2 %collective-permute-start.31 = (f32[32,2688]{1,0:T(8,128)S(1)}, f32[32,2688]{1,0:T(8,128)S(1)}, u32[]{:S(2)}, u32[]{:S(2)}) collective-permute-start(f32[32,2688]{1,0:T(8,128)S(1)} %add.73), channel_id=1, source_target_pairs={{0,16},{4,20},{8,24},{12,28},{16,0},{20,4},{24,8},{28,12},{1,17},{... | collective-permute-start | bytes 1032200 | tf_op jit(solution)/shard_map/ppermute | solution.py:959
  338.2 14.6 %collective-permute-start.35 = (f32[32,2688]{1,0:T(8,128)S(1)}, f32[32,2688]{1,0:T(8,128)S(1)}, u32[]{:S(2)}, u32[]{:S(2)}) collective-permute-start(f32[32,2688]{1,0:T(8,128)S(1)} %add.74), channel_id=1, source_target_pairs={{0,8},{4,12},{8,0},{12,4},{16,24},{20,28},{24,16},{28,20},{1,9},{5... | collective-permute-start | bytes 1032200 | tf_op jit(solution)/shard_map/ppermute | solution.py:959
  356.3 8.7 %collective-permute-start.39 = (bf16[96,384]{1,0:T(8,128)(2,1)S(1)}, bf16[96,384]{1,0:T(8,128)(2,1)S(1)}, u32[]{:S(2)}, u32[]{:S(2)}) collective-permute-start(bf16[96,384]{1,0:T(8,128)(2,1)S(1)} %fusion.3), channel_id=1, source_target_pairs={{0,16},{4,20},{8,24},{12,28},{16,0},{20,4},{24,8},{28,12},{1,17},{... | collective-permute-start | bytes 221192 | tf_op jit(solution)/shard_map/ppermute | solution.py:959
  (48 other events, 455.4 us)

commit v5 on v4

--- a/solution.py
+++ b/solution.py
@@ -154,6 +154,8 @@
 
 
 def stack_queries(queries, shift):
+    if shift is None:
+        return stack_heads(queries, jnp.where(lane_sub(queries.shape[0]) == 3, 1.0, 0.0))
     return stack_heads(queries, piece_lanes(shift * (-1.0 / EXPONENT_SCALE), 1.0))
 
 
@@ -163,23 +165,25 @@
     weights = jnp.exp2(scores * EXPONENT_SCALE).astype(BF)
     result = dot(weights, values)
     totals = pick_heads(result[:, HALF:], rows)
-    return pick_heads(result[:, :HALF], rows) / totals, jnp.log(totals) * LOG2E + shift
+    log_total = jnp.log(totals) * LOG2E
+    if shift is not None:
+        log_total = log_total + shift
+    return pick_heads(result[:, :HALF], rows) / totals, log_total
 
 
 def highest_scores(queries, keys):
     rows = queries.shape[0]
-    scores = dot_nt(stack_queries(queries, jnp.zeros((rows, HALF), F32)), keys)
+    scores = dot_nt(stack_queries(queries, None), keys)
     highest = jnp.max(scores, axis=-1, keepdims=True) * EXPONENT_SCALE
     return pick_heads(jnp.broadcast_to(highest, (BRANCH_HEADS * rows, HALF)), rows)
 
 
 def attend_heads_back(queries, grad, attended, log_total, keys, values):
     rows = queries.shape[0]
-    eye = one_hot(iota((HALF, HALF), 0) == iota((HALF, HALF), 1))
-    query_turned = dot_nt(eye, queries.astype(BF)).astype(BF)
-    grad_turned = dot_nt(eye, grad.astype(BF)).astype(BF)
+    query_turned = jnp.transpose(queries).astype(BF)
+    grad_turned = jnp.transpose(grad).astype(BF)
     block = one_hot((iota((HALF, HALF), 0) >> 5) == (iota((HALF, HALF), 1) >> 5))
-    inner = sum(dot(piece.astype(BF), block) for piece in pieces_of(grad * attended))
+    inner = sum(dot(piece.astype(BF), block) for piece in pieces_of(grad * attended)[:2])
     weights = jnp.exp2(dot_nt(stack_queries(queries, log_total), keys) * EXPONENT_SCALE)
     weights_low = weights.astype(BF)
     grad_weights = dot_nt(stack_heads(grad, piece_lanes(-inner, 0.0)), values)
@@ -306,8 +310,7 @@
     values_ref,
     shift_ref,
 ):
-    rows, width, kept, key_rows, chunk = dims
-    tokens = rows * width
+    rows, width, kept, key_rows = dims
     image = pl.program_id(0)
     ranks = rank_row(mask_ref[pl.ds(image + first, 1)].astype(F32), width)
     select = one_hot(iota((kept, width), 0).astype(F32) == ranks)
@@ -332,37 +335,20 @@
     def _():
         shift_ref[...] = jnp.zeros_like(shift_ref)
 
-    def rows_of(step):
-        return pl.ds(pl.multiple_of(step * chunk, 16), chunk)
-
     @pl.when(large)
     def _():
-        def highest(step, carry):
-            span = rows_of(step)
+        def highest(row, carry):
+            span = pl.ds(pl.multiple_of(row * width, 16), width)
             shift_ref[span] = highest_scores(across_ref[0, span, :HALF].astype(F32), keys_ref[0])
             return carry
 
-        lax.fori_loop(0, tokens // chunk, highest, 0)
-
-    def attend(step, carry):
-        span = rows_of(step)
-        attended, log_total = attend_heads(
-            across_ref[0, span, :HALF].astype(F32), shift_ref[span], keys_ref[0], values_ref[0]
-        )
-        attended_ref[0, span] = attended
-        total_ref[0, span] = log_total
-        return carry
-
-    lax.fori_loop(0, tokens // chunk, attend, 0, unroll=True)
-
-    @pl.when(large)
-    def _():
-        shift_ref[...] = jnp.zeros_like(shift_ref)
+        lax.fori_loop(0, rows, highest, 0)
 
     def value_row(row):
         return across_ref[0, row * width : (row + 1) * width, 2 * HALF :].astype(F32)
 
     for row in range(rows):
+        span = slice(row * width, (row + 1) * width)
         sums = [jnp.zeros((width, HALF), F32) for _ in range(3)]
         for tap_row in range(3):
             source = row + tap_row - 1
@@ -372,8 +358,15 @@
                     tap = 3 * tap_row + tap_col
                     sums[tap_col] = sums[tap_col] + values * small_ref[tap : tap + 1, :HALF]
         local = shift_down(sums[0]) + sums[1] + shift_up(sums[2]) + small_ref[11:12, :HALF]
-        span = slice(row * width, (row + 1) * width)
-        joined_ref[0, span] = (attended_ref[0, span] + local).astype(BF)
+        queries = across_ref[0, span, :HALF].astype(F32)
+        attended, log_total = attend_heads(queries, shift_ref[span], keys_ref[0], values_ref[0])
+        attended_ref[0, span] = attended
+        total_ref[0, span] = log_total
+        joined_ref[0, span] = (attended + local).astype(BF)
+
+    @pl.when(large)
+    def _():
+        shift_ref[...] = jnp.zeros_like(shift_ref)
 
 
 def assemble(me_ref, pieces, target_ref, dim, step):
@@ -428,7 +421,7 @@
     me_ref, mask_ref, small_ref, weight_ref = refs[:4]
     pieces_in = refs[4 : 4 + ways]
     joined_refs = refs[4 + ways : 4 + 2 * ways]
-    attended_ref, total_ref, saved_ref, normed_out, mixed_ref, joined_ref, column_ref, shift_ref = refs[
+    attended_ref, total_ref, saved_ref, normed_out, mixed_ref, joined_ref, column_ref = refs[
         4 + 2 * ways :
     ]
     normed_ref = normed_out.at[0]
@@ -443,16 +436,12 @@
     saved_ref[0] = mixed_low
     mixed_ref[...] = mixed_low.astype(F32)
 
-    @pl.when(pl.program_id(0) == 0)
-    def _():
-        shift_ref[...] = jnp.zeros_like(shift_ref)
-
     everything = mixed_ref[...].reshape(height * wide_part, 3 * HALF)
     large = exceeds(
         head_norms(everything[:, :HALF] * (SCALE * LOG2E)), head_norms(everything[:, HALF : 2 * HALF])
     )
 
-    def one_window(window, carry):
+    def one_window(shifted, window, carry):
         span = pl.ds(pl.multiple_of(window * GROUP, GROUP), GROUP)
         grid = mixed_ref[:, span]
         flat = grid.reshape(tokens, 3 * HALF)
@@ -460,11 +449,8 @@
         bias = window_bias(column_ref, start, window, height)
         keys_in, values_in = window_operands(keys, values, bias, spare)
 
-        @pl.when(large)
-        def _():
-            shift_ref[...] = highest_scores(queries, keys_in)
-
-        attended, log_total = attend_heads(queries, shift_ref[...], keys_in, values_in)
+        shift = highest_scores(queries, keys_in) if shifted else None
+        attended, log_total = attend_heads(queries, shift, keys_in, values_in)
         attended_ref[0, :, span] = attended.reshape(height, GROUP, HALF)
         total_ref[0, :, span] = log_total.reshape(height, GROUP, HALF)
         stacked = grid_stack(values.reshape(height, GROUP, HALF))
@@ -480,11 +466,13 @@
         joined_ref[:, span] = attended.reshape(height, GROUP, HALF) + local
         return carry
 
-    lax.fori_loop(0, windows, one_window, 0, unroll=min(windows, 4))
+    @pl.when(jnp.logical_not(large))
+    def _():
+        lax.fori_loop(0, windows, functools.partial(one_window, False), 0, unroll=min(windows, 8))
 
     @pl.when(large)
     def _():
-        shift_ref[...] = jnp.zeros_like(shift_ref)
+        lax.fori_loop(0, windows, functools.partial(one_window, True), 0)
 
     for distance in range(ways):
         place = me_ref[0] ^ distance
@@ -563,19 +551,36 @@
         back = cot_ref[0, span]
         result = middle + small_ref[15:16]
         grad_normed = jnp.zeros((chunk, 2 * HALF), F32)
+
+        def products(part):
+            lanes = slice(part, part + hidden_part)
+            return dot(normed_low, expand_ref[:, lanes]), dot_nt(back, shrink_ref[lanes])
+
+        def follow(result, grad_normed, behind):
+            lanes, active, grad_hidden = behind
+            return (
+                result + dot(active, shrink_ref[lanes]),
+                grad_normed + dot_nt(grad_hidden, expand_ref[:, lanes]),
+            )
+
+        ahead, behind = products(0), None
         for part in range(0, hidden_width, hidden_part):
             lanes = slice(part, part + hidden_part)
-            hidden = dot(normed_low, expand_ref[:, lanes]) + bias_ref[:, lanes]
+            hidden, grad_active = ahead
+            if part + hidden_part < hidden_width:
+                ahead = products(part + hidden_part)
+            hidden = hidden + bias_ref[:, lanes]
             upper, density = gelu_parts(hidden)
             active = (hidden * upper).astype(BF)
             active_ref[span, lanes] = active
-            result = result + dot(active, shrink_ref[lanes])
-            grad_active = dot_nt(back, shrink_ref[lanes])
             grad_hidden = grad_active * (upper + hidden * density)
             grad_hidden = grad_hidden.astype(BF)
             hidden_ref[span, lanes] = grad_hidden
             dbias_ref[:, lanes] += fold_rows(grad_hidden.astype(F32))
-            grad_normed = grad_normed + dot_nt(grad_hidden, expand_ref[:, lanes])
+            if part:
+                result, grad_normed = follow(result, grad_normed, behind)
+            behind = (lanes, active, grad_hidden)
+        result, grad_normed = follow(result, grad_normed, behind)
         block_ref[0, span] = result
         back_wide = back.astype(F32)
         grad_middle = back_wide + normalize_back(grad_normed, scaled, recip, small_ref[13:14])
@@ -761,7 +766,7 @@
         out_ref[:, span, 2 * HALF :] = grad_values.reshape(shape) + local
         return carry
 
-    lax.fori_loop(0, windows, one_window, 0, unroll=min(windows, 4))
+    lax.fori_loop(0, windows, one_window, 0, unroll=min(windows, 8))
     mixed_grad = out_ref[...].reshape(height * wide_part, 3 * HALF).astype(BF)
     grad_normed = dot_nt(mixed_grad, weight_ref[:, 3 * HALF :]).astype(BF)
     turned_ref[...] = grad_normed.reshape(height, wide_part, 2 * HALF)
@@ -1013,7 +1018,6 @@
     shard = qkv_weight.shape[0]
     hidden_width = expand_weight.shape[1]
     blocks = hidden_width // channels
-    chunk = width
     pair = count // 2
     chip_steps = [2 << bit for bit in range((lax.axis_size("img") // 2).bit_length() - 1)][::-1]
 
@@ -1086,7 +1090,7 @@
     across_mixed, normed = whole_images
     small_in, qkv_in = whole(small_full), whole(qkv_low)
 
-    attention_dims = (rows, width, kept, key_rows, chunk)
+    attention_dims = (rows, width, kept, key_rows)
     key_shape = (key_rows, channels)
     across = []
 
@@ -1138,7 +1142,6 @@
                 pltpu.VMEM(mixed_grid, F32),
                 pltpu.VMEM(grid_f32, F32),
                 pltpu.VMEM((wide, HALF), F32),
-                pltpu.VMEM((window_tokens, HALF), F32),
             ],
             15,
             after=(token,),
@@ -1195,7 +1198,7 @@
     def run_across_back(first, images_in, sums, after):
         results, token = run_kernel(
             functools.partial(
-                across_back_kernel, (rows, width, kept, key_rows, tokens // 2), first, sums is not None
+                across_back_kernel, (*attention_dims, tokens // 2), first, sums is not None
             ),
             images_in,
             [

time: 384 us -> 372 us (0.969)
  Pallas kernels: 290 us -> 274 us
  starting transfers between devices: 52 us -> 57.6 us
    pallas_call x16, Pallas kernels: 290 us -> 274 us  [run_kernel(): pl.pallas_call(wrapped, grid=(images,), in_specs=[spec for _, spec in inp...]
    ppermute x44, starting transfers between devices: 52 us -> 57.6 us  [swap(): lax.ppermute(value, axis, [(place, place ^ distance) for place in range(l...]
  transfers between devices with their start and end apart: 44 -> 44, of which waited for: 11 -> 10; matrix products, arithmetic and copies ran while one was open for 2% -> 2% of each run, Pallas kernels for 62% -> 59%
where the time goes in v5:
time: 372 us
  Pallas kernels  274 us (74%)
  starting transfers between devices  57.6 us (15%)
  waiting for transfers between devices  22 us (6%)
  other arithmetic  9.34 us (3%)
  local copies, waits for them, and re-layouts  5.44 us (1%)
    pallas_call x16, Pallas kernels, run_kernel(): pl.pallas_call(wrapped, grid=(images,), in_specs=[spec for _, spec in inp...  274 us
    ppermute x44, starting transfers between devices, swap(): lax.ppermute(value, axis, [(place, place ^ distance) for place in range(l...  57.6 us
    ppermute x44, waiting for transfers between devices, swap(): lax.ppermute(value, axis, [(place, place ^ distance) for place in range(l...  22 us
  transfers between devices with their start and end apart: 44, of which 10 were waited for; matrix products, arithmetic and copies ran while one was open for 2% of the time, Pallas kernels for 59%

profile of v5, /device:TPU:0, one launch (start us, length us, event | category | flops | bytes accessed | tf_op | source)
XLA Modules:
  0.0 371.6 jit_solution(2513648171729065158)
XLA Ops:
  2.3 2.9 collective-permute-start
  6.8 2.5 collective-permute-done.refs_3_
  9.3 3.7 collective-permute-done.1.refs_4_
  13.7 6.2 %shard_map.365 = (bf16[4,1568,384]{2,1,0:T(8,128)(2,1)}, bf16[4,1568,256]{2,1,0:T(8,128)(2,1)}, bf16[2,7,64,256]{3,2,1,0:T(8,128)(2,1)}, bf16[2,7,64,256]{3,2,1,...) custom-call(s32[1]{0:T(128)} %bitcast.refs_0_, ...), custom_call_target="tpu_custom_call" | custom-call | flops 6000000000 | bytes 6000000 | tf_op jit(solution)/shard_map/pallas_call | solution.py:936
  23.5 5.4 %shard_map.366 = (bf16[4,1568,384]{2,1,0:T(8,128)(2,1)}, bf16[4,1568,256]{2,1,0:T(8,128)(2,1)}, bf16[2,7,64,256]{3,2,1,0:T(8,128)(2,1)}, bf16[2,7,64,256]{3,2,1,...) custom-call(s32[1]{0:T(128)} %bitcast.refs_0_, ...), custom_call_target="tpu_custom_call", output_to_operand_aliasing={{0}: (4, {}), {1}: (5, {})} | custom-call | flops 6000000000 | bytes 6000000 | tf_op jit(solution)/shard_map/pallas_call | solution.py:936
  30.9 2.8 collective-permute-done.3.refs_5_
  35.0 32.9 %shard_map.367 = (bf16[4,1568,128]{2,1,0:T(8,128)(2,1)}, f32[4,1568,128]{2,1,0:T(8,128)}, f32[4,1568,128]{2,1,0:T(8,128)}, bf16[4,1280,256]{2,1,0:T(8,128)(2,1)}...) custom-call(bf16[4,1568,384]{2,1,0:T(8,128)(2,1)} %get-tuple-element.175.refs_0_, s32[4,224]{1,0:T(4,128)} %refs_7_.5, ...), custom_call_target="tpu_custom_call" | custom-call | flops 32999999488 | bytes 33000000 | tf_op jit(solution)/shard_map/pallas_call | solution.py:936
  68.0 1.8 shard_map.368
  73.4 11.7 %shard_map.369 = (bf16[2,7,64,128]{3,2,1,0:T(8,128)(2,1)}, bf16[2,7,64,128]{3,2,1,0:T(8,128)(2,1)}, bf16[2,7,64,128]{3,2,1,0:T(8,128)(2,1)}, bf16[2,7,64,128]{3,...) custom-call(s32[1]{0:T(128)} %bitcast.refs_0_, ...), custom_call_target="tpu_custom_call" | custom-call | flops 15000000512 | bytes 15000000 | tf_op jit(solution)/shard_map/pallas_call | solution.py:936
  86.7 4.7 %collective-permute-start.10 = (bf16[2,7,64,128]{3,2,1,0:T(8,128)(2,1)}, bf16[2,7,64,128]{3,2,1,0:T(8,128)(2,1)S(1)}, u32[]{:S(2)}, u32[]{:S(2)}) collective-permute-start(bf16[2,7,64,128]{3,2,1,0:T(8,128)(2,1)} %get-tuple-element.210), channel_id=1, source_target_pairs={{0,2},{1,3},{2,0},{3,1},{4,6},{5,7},{6,4},{7,5},{8,10},{9,11},{10,... | collective-permute-start | bytes 688136 | tf_op jit(solution)/shard_map/ppermute | solution.py:964
  91.4 11.5 %shard_map.370 = (bf16[2,7,64,128]{3,2,1,0:T(8,128)(2,1)}, bf16[2,7,64,128]{3,2,1,0:T(8,128)(2,1)}, bf16[2,7,64,128]{3,2,1,0:T(8,128)(2,1)}, bf16[2,7,64,128]{3,...) custom-call(s32[1]{0:T(128)} %bitcast.refs_0_, ...), custom_call_target="tpu_custom_call", output_to_operand_aliasing={{4}: (9, {}), {5}: (10, {}), {6}: (11, {}), {7}: (12, {})} | custom-call | flops 15000000512 | bytes 15000000 | tf_op jit(solution)/shard_map/pallas_call | solution.py:936
  104.5 2.0 collective-permute-start.13
  106.6 13.5 %shard_map.371 = (bf16[4,1568,128]{2,1,0:T(8,128)(2,1)}, f32[4,1568,128]{2,1,0:T(8,128)}, f32[4,1568,128]{2,1,0:T(8,128)}, bf16[4,1280,256]{2,1,0:T(8,128)(2,1)}...) custom-call(bf16[4,1568,384]{2,1,0:T(8,128)(2,1)} %get-tuple-element, ...), custom_call_target="tpu_custom_call", output_to_operand_aliasing={{0}: (4, {}), {1}: (5, {}), {2}: (6, {}), {3}: (7, {}), {4}... | custom-call | flops 11000000512 | bytes 11000000 | tf_op jit(solution)/shard_map/pallas_call | solution.py:936
  121.1 42.6 %shard_map.372 = (f32[4,1568,256]{2,1,0:T(8,128)}, f32[4,1568,256]{2,1,0:T(8,128)}, bf16[4,1568,128]{2,1,0:T(8,128)(2,1)}, bf16[4,7,64,128]{3,2,1,0:T(8,128)(2,1...) custom-call(s32[1]{0:T(128)} %bitcast.refs_0_, ...), custom_call_target="tpu_custom_call" | custom-call | flops 44999999488 | bytes 45000000 | tf_op jit(solution)/shard_map/pallas_call | solution.py:936
  165.3 1.9 collective-permute-start.22
  167.3 24.0 %shard_map.373 = (bf16[4,1568,384]{2,1,0:T(8,128)(2,1)}, f32[80,128]{1,0:T(8,128)}, f32[256,384]{1,0:T(8,128)}, f32[8,128]{1,0:T(8,128)}) custom-call(bf16[4,1568,384]{2,1,0:T(8,128)(2,1)} %get-tuple-element.175.refs_0_, bf16[4,1568,128]{2,1,0:T(8,128)(2,1)} %get-tuple-element.221.refs_1_, f32[4,1568,128]{2,1,0:T(8,128)} %get-tuple-element.222.refs_2_, ...), custom_call_target="tpu_custom_call" | custom-call | flops 23000000512 | bytes 23000000 | tf_op jit(solution)/shard_map/pallas_call | solution.py:936
  192.8 1.9 collective-permute-start.19
  195.8 33.3 %shard_map.374 = (bf16[4,7,64,256]{3,2,1,0:T(8,128)(2,1)}, bf16[4,7,64,256]{3,2,1,0:T(8,128)(2,1)}, bf16[4,7,64,256]{3,2,1,0:T(8,128)(2,1)}, bf16[4,7,64,256]{3,...) custom-call(s32[1]{0:T(128)} %bitcast.refs_0_, ...), custom_call_target="tpu_custom_call" | custom-call | flops 38000001024 | bytes 38000000 | tf_op jit(solution)/shard_map/pallas_call | solution.py:936
  230.6 1.9 collective-permute-start.25
  234.9 1.9 collective-permute-start.29
  236.9 2.0 add_add_fusion.refs_12_
  238.9 45.0 %shard_map.375 = (bf16[4,1568,384]{2,1,0:T(8,128)(2,1)}, f32[80,128]{1,0:T(8,128)}, f32[256,384]{1,0:T(8,128)}, f32[8,128]{1,0:T(8,128)}) custom-call(bf16[4,1568,384]{2,1,0:T(8,128)(2,1)} %get-tuple-element.175.refs_0_, bf16[4,1568,128]{2,1,0:T(8,128)(2,1)} %get-tuple-element.221.refs_1_, ...), custom_call_target="tpu_custom_call", output_to_operand_aliasing={{0}: (13, {})} | custom-call | flops 46000001024 | bytes 46000000 | tf_op jit(solution)/shard_map/pallas_call | solution.py:936
  287.3 10.9 %shard_map.376 = (f32[4,1568,256]{2,1,0:T(8,128)}, f32[16,256]{1,0:T(8,128)}, f32[8,128]{1,0:T(8,128)}) custom-call(s32[1]{0:T(128)} %bitcast.refs_0_, bf16[4,1568,256]{2,1,0:T(8,128)(2,1)} %bitcast.17, f32[4,1568,256]{2,1,0:T(8,128)} %get-tuple-element.220.refs_2_, bf16[4,1568,384]{2,1,0:T(8,128)(2,1)} %get-tuple-element.267.refs_3_.refs_12_, ...), custom_call_target="tpu_custom_call" | custom-call | flops 12000000000 | bytes 12000000 | tf_op jit(solution)/shard_map/pallas_call | solution.py:936
  298.3 24.1 %shard_map.377 = (bf16[4,1568,384]{2,1,0:T(8,128)(2,1)}, f32[80,128]{1,0:T(8,128)}, f32[256,384]{1,0:T(8,128)}, f32[8,128]{1,0:T(8,128)}) custom-call(bf16[4,1568,384]{2,1,0:T(8,128)(2,1)} %get-tuple-element.175.refs_0_, bf16[4,1568,128]{2,1,0:T(8,128)(2,1)} %get-tuple-element.221.refs_1_, ...), custom_call_target="tpu_custom_call", output_to_operand_aliasing={{0}: (12, {})} | custom-call | flops 23000000512 | bytes 23000000 | tf_op jit(solution)/shard_map/pallas_call | solution.py:936
  322.4 7.0 %collective-permute-start.35 = (f32[32,2688]{1,0:T(8,128)S(1)}, f32[32,2688]{1,0:T(8,128)S(1)}, u32[]{:S(2)}, u32[]{:S(2)}) collective-permute-start(f32[32,2688]{1,0:T(8,128)S(1)} %add.74), channel_id=1, source_target_pairs={{0,8},{4,12},{8,0},{12,4},{16,24},{20,28},{24,16},{28,20},{1,9},{5... | collective-permute-start | bytes 1032200 | tf_op jit(solution)/shard_map/ppermute | solution.py:964
  329.4 5.4 %shard_map.378 = (f32[4,1568,256]{2,1,0:T(8,128)}, f32[16,256]{1,0:T(8,128)}, bf16[96,384]{1,0:T(8,128)(2,1)}, bf16[96,384]{1,0:T(8,128)(2,1)}, bf16[96,384]{1,0...) custom-call(s32[1]{0:T(128)} %bitcast.refs_0_, ...), custom_call_target="tpu_custom_call", output_to_operand_aliasing={{0}: (17, {})} | custom-call | flops 4000000000 | bytes 4000000 | tf_op jit(solution)/shard_map/pallas_call | solution.py:936
  336.3 1.9 collective-permute-start.33
  339.4 2.5 collective-permute-done.33
  346.9 2.4 collective-permute-start.40
  353.3 3.9 %collective-permute-done.39 = bf16[96,384]{1,0:T(8,128)(2,1)S(1)} collective-permute-done((bf16[96,384]{1,0:T(8,128)(2,1)S(1)}, bf16[96,384]{1,0:T(8,128)(2,1)S(1)}, u32[]{:S(2)}, u32[]{:S(2)}) %collective-permute-start.39) | collective-permute-done | bytes 73760 | tf_op jit(solution)/shard_map/ppermute | solution.py:964
  362.3 2.7 collective-permute-start.43
  367.4 3.9 %shard_map.379 = (f32[1,1]{1,0:T(1,128)}, f32[64,768]{1,0:T(8,128)}, f32[64,256]{1,0:T(8,128)}, f32[64,1024]{1,0:T(8,128)}, f32[256,256]{1,0:T(8,128)}, /*index=...) custom-call(s32[2]{0:T(128)} %pad_add_fusion.refs_0_, ...), custom_call_target="tpu_custom_call" | custom-call | flops 4000000000 | bytes 4000000 | tf_op jit(solution)/shard_map/pallas_call | solution.py:936
  (157 shorter events, 47.1 us)
Async XLA Ops:
  5.3 7.7 %collective-permute-start.1 = (bf16[80,768]{1,0:T(8,128)(2,1)}, bf16[80,768]{1,0:T(8,128)(2,1)S(1)}, u32[]{:S(2)}, u32[]{:S(2)}) collective-permute-start(bf16[80,768]{1,0:T(8,128)(2,1)} %get-tuple-element.170.refs_2_), channel_id=1, source_target_pairs={{0,2},{1,3},{2,0},{3,1},{4,6},{5,7},{6,4},{7,5},{8,10},{9,11},{10,... | collective-permute-start | bytes 368648 | tf_op jit(solution)/shard_map/ppermute | solution.py:964
  19.9 13.7 %collective-permute-start.3 = (bf16[2,7,64,256]{3,2,1,0:T(8,128)(2,1)}, bf16[2,7,64,256]{3,2,1,0:T(8,128)(2,1)S(1)}, u32[]{:S(2)}, u32[]{:S(2)}) collective-permute-start(bf16[2,7,64,256]{3,2,1,0:T(8,128)(2,1)} %get-tuple-element.177), channel_id=1, source_target_pairs={{0,1},{1,0},{2,3},{3,2},{4,5},{5,4},{6,7},{7,6},{8,9},{9,8},{10,11... | collective-permute-start | bytes 1376264 | tf_op jit(solution)/shard_map/ppermute | solution.py:964
  21.1 48.7 %collective-permute-start.4 = (bf16[2,7,64,256]{3,2,1,0:T(8,128)(2,1)}, bf16[2,7,64,256]{3,2,1,0:T(8,128)(2,1)S(1)}, u32[]{:S(2)}, u32[]{:S(2)}) collective-permute-start(bf16[2,7,64,256]{3,2,1,0:T(8,128)(2,1)} %get-tuple-element.178), channel_id=1, source_target_pairs={{0,2},{1,3},{2,0},{3,1},{4,6},{5,7},{6,4},{7,5},{8,10},{9,11},{10,... | collective-permute-start | bytes 1376264 | tf_op jit(solution)/shard_map/ppermute | solution.py:964
  21.9 49.4 %collective-permute-start.5 = (bf16[2,7,64,256]{3,2,1,0:T(8,128)(2,1)}, bf16[2,7,64,256]{3,2,1,0:T(8,128)(2,1)S(1)}, u32[]{:S(2)}, u32[]{:S(2)}) collective-permute-start(bf16[2,7,64,256]{3,2,1,0:T(8,128)(2,1)} %get-tuple-element.179), channel_id=1, source_target_pairs={{0,3},{1,2},{2,1},{3,0},{4,7},{5,6},{6,5},{7,4},{8,11},{9,10},{10,... | collective-permute-start | bytes 1376264 | tf_op jit(solution)/shard_map/ppermute | solution.py:964
  28.9 43.0 %collective-permute-start.6 = (bf16[2,7,64,256]{3,2,1,0:T(8,128)(2,1)}, bf16[2,7,64,256]{3,2,1,0:T(8,128)(2,1)S(1)}, u32[]{:S(2)}, u32[]{:S(2)}) collective-permute-start(bf16[2,7,64,256]{3,2,1,0:T(8,128)(2,1)} %get-tuple-element.181), channel_id=1, source_target_pairs={{0,1},{1,0},{2,3},{3,2},{4,5},{5,4},{6,7},{7,6},{8,9},{9,8},{10,11... | collective-permute-start | bytes 1376264 | tf_op jit(solution)/shard_map/ppermute | solution.py:964
  30.0 43.3 %collective-permute-start.7 = (bf16[2,7,64,256]{3,2,1,0:T(8,128)(2,1)}, bf16[2,7,64,256]{3,2,1,0:T(8,128)(2,1)S(1)}, u32[]{:S(2)}, u32[]{:S(2)}) collective-permute-start(bf16[2,7,64,256]{3,2,1,0:T(8,128)(2,1)} %get-tuple-element.182), channel_id=1, source_target_pairs={{0,2},{1,3},{2,0},{3,1},{4,6},{5,7},{6,4},{7,5},{8,10},{9,11},{10,... | collective-permute-start | bytes 1376264 | tf_op jit(solution)/shard_map/ppermute | solution.py:964
  33.7 39.7 %collective-permute-start.8 = (bf16[2,7,64,256]{3,2,1,0:T(8,128)(2,1)}, bf16[2,7,64,256]{3,2,1,0:T(8,128)(2,1)S(1)}, u32[]{:S(2)}, u32[]{:S(2)}) collective-permute-start(bf16[2,7,64,256]{3,2,1,0:T(8,128)(2,1)} %get-tuple-element.183), channel_id=1, source_target_pairs={{0,3},{1,2},{2,1},{3,0},{4,7},{5,6},{6,5},{7,4},{8,11},{9,10},{10,... | collective-permute-start | bytes 1376264 | tf_op jit(solution)/shard_map/ppermute | solution.py:964
  69.8 33.2 %collective-permute-start.15 = (bf16[64,2304]{1,0:T(8,128)(2,1)}, bf16[64,2304]{1,0:T(8,128)(2,1)S(1)}, u32[]{:S(2)}, u32[]{:S(2)}) collective-permute-start(bf16[64,2304]{1,0:T(8,128)(2,1)} %get-tuple-element.216.refs_12_), channel_id=1, source_target_pairs={{0,1},{1,0},{2,3},{3,2},{4,5},{5,4},{6,7},{7,6},{8,9},{9,8},{10,11... | collective-permute-start | bytes 884744 | tf_op jit(solution)/shard_map/ppermute | solution.py:964
  71.3 31.7 %collective-permute-start.16 = (bf16[64,2304]{1,0:T(8,128)(2,1)}, bf16[64,2304]{1,0:T(8,128)(2,1)S(1)}, u32[]{:S(2)}, u32[]{:S(2)}) collective-permute-start(bf16[64,2304]{1,0:T(8,128)(2,1)} %get-tuple-element.216.refs_12_), channel_id=1, source_target_pairs={{0,2},{1,3},{2,0},{3,1},{4,6},{5,7},{6,4},{7,5},{8,10},{9,11},{10,... | collective-permute-start | bytes 884744 | tf_op jit(solution)/shard_map/ppermute | solution.py:964
  71.9 32.6 %collective-permute-start.17 = (bf16[64,2304]{1,0:T(8,128)(2,1)}, bf16[64,2304]{1,0:T(8,128)(2,1)S(1)}, u32[]{:S(2)}, u32[]{:S(2)}) collective-permute-start(bf16[64,2304]{1,0:T(8,128)(2,1)} %get-tuple-element.216.refs_12_), channel_id=1, source_target_pairs={{0,3},{1,2},{2,1},{3,0},{4,7},{5,6},{6,5},{7,4},{8,11},{9,10},{10,... | collective-permute-start | bytes 884744 | tf_op jit(solution)/shard_map/ppermute | solution.py:964
  85.2 21.4 %collective-permute-start.9 = (bf16[2,7,64,128]{3,2,1,0:T(8,128)(2,1)}, bf16[2,7,64,128]{3,2,1,0:T(8,128)(2,1)S(1)}, u32[]{:S(2)}, u32[]{:S(2)}) collective-permute-start(bf16[2,7,64,128]{3,2,1,0:T(8,128)(2,1)} %get-tuple-element.209), channel_id=1, source_target_pairs={{0,1},{1,0},{2,3},{3,2},{4,5},{5,4},{6,7},{7,6},{8,9},{9,8},{10,11... | collective-permute-start | bytes 688136 | tf_op jit(solution)/shard_map/ppermute | solution.py:964
  86.7 33.4 %collective-permute-start.10 = (bf16[2,7,64,128]{3,2,1,0:T(8,128)(2,1)}, bf16[2,7,64,128]{3,2,1,0:T(8,128)(2,1)S(1)}, u32[]{:S(2)}, u32[]{:S(2)}) collective-permute-start(bf16[2,7,64,128]{3,2,1,0:T(8,128)(2,1)} %get-tuple-element.210), channel_id=1, source_target_pairs={{0,2},{1,3},{2,0},{3,1},{4,6},{5,7},{6,4},{7,5},{8,10},{9,11},{10,... | collective-permute-start | bytes 688136 | tf_op jit(solution)/shard_map/ppermute | solution.py:964
  103.0 17.2 %collective-permute-start.11 = (bf16[2,7,64,128]{3,2,1,0:T(8,128)(2,1)S(1)}, bf16[2,7,64,128]{3,2,1,0:T(8,128)(2,1)S(1)}, u32[]{:S(2)}, u32[]{:S(2)}) collective-permute-start(bf16[2,7,64,128]{3,2,1,0:T(8,128)(2,1)S(1)} %copy-done.26), channel_id=1, source_target_pairs={{0,3},{1,2},{2,1},{3,0},{4,7},{5,6},{6,5},{7,4},{8,11},{9,10},{10,... | collective-permute-start | bytes 688136 | tf_op jit(solution)/shard_map/ppermute | solution.py:964
  103.1 17.1 %collective-permute-start.12 = (bf16[2,7,64,128]{3,2,1,0:T(8,128)(2,1)}, bf16[2,7,64,128]{3,2,1,0:T(8,128)(2,1)S(1)}, u32[]{:S(2)}, u32[]{:S(2)}) collective-permute-start(bf16[2,7,64,128]{3,2,1,0:T(8,128)(2,1)} %get-tuple-element.213), channel_id=1, source_target_pairs={{0,1},{1,0},{2,3},{3,2},{4,5},{5,4},{6,7},{7,6},{8,9},{9,8},{10,11... | collective-permute-start | bytes 688136 | tf_op jit(solution)/shard_map/ppermute | solution.py:964
  104.5 15.7 %collective-permute-start.13 = (bf16[2,7,64,128]{3,2,1,0:T(8,128)(2,1)}, bf16[2,7,64,128]{3,2,1,0:T(8,128)(2,1)S(1)}, u32[]{:S(2)}, u32[]{:S(2)}) collective-permute-start(bf16[2,7,64,128]{3,2,1,0:T(8,128)(2,1)} %get-tuple-element.214), channel_id=1, source_target_pairs={{0,2},{1,3},{2,0},{3,1},{4,6},{5,7},{6,4},{7,5},{8,10},{9,11},{10,... | collective-permute-start | bytes 688136 | tf_op jit(solution)/shard_map/ppermute | solution.py:964
  106.5 13.7 %collective-permute-start.14 = (bf16[2,7,64,128]{3,2,1,0:T(8,128)(2,1)}, bf16[2,7,64,128]{3,2,1,0:T(8,128)(2,1)S(1)}, u32[]{:S(2)}, u32[]{:S(2)}) collective-permute-start(bf16[2,7,64,128]{3,2,1,0:T(8,128)(2,1)} %get-tuple-element.215), channel_id=1, source_target_pairs={{0,3},{1,2},{2,1},{3,0},{4,7},{5,6},{6,5},{7,4},{8,11},{9,10},{10,... | collective-permute-start | bytes 688136 | tf_op jit(solution)/shard_map/ppermute | solution.py:964
  163.7 31.0 %collective-permute-start.21 = (bf16[4,7,64,128]{3,2,1,0:T(8,128)(2,1)}, bf16[4,7,64,128]{3,2,1,0:T(8,128)(2,1)}, u32[]{:S(2)}, u32[]{:S(2)}) collective-permute-start(bf16[4,7,64,128]{3,2,1,0:T(8,128)(2,1)} %get-tuple-element.244), channel_id=1, source_target_pairs={{0,1},{1,0},{2,3},{3,2},{4,5},{5,4},{6,7},{7,6},{8,9},{9,8},{10,11... | collective-permute-start | bytes 1376264 | tf_op jit(solution)/shard_map/ppermute | solution.py:964
  165.3 29.6 %collective-permute-start.22 = (bf16[4,7,64,128]{3,2,1,0:T(8,128)(2,1)}, bf16[4,7,64,128]{3,2,1,0:T(8,128)(2,1)S(1)}, u32[]{:S(2)}, u32[]{:S(2)}) collective-permute-start(bf16[4,7,64,128]{3,2,1,0:T(8,128)(2,1)} %get-tuple-element.245), channel_id=1, source_target_pairs={{0,2},{1,3},{2,0},{3,1},{4,6},{5,7},{6,4},{7,5},{8,10},{9,11},{10,... | collective-permute-start | bytes 1376264 | tf_op jit(solution)/shard_map/ppermute | solution.py:964
  167.2 27.6 %collective-permute-start.23 = (bf16[4,7,64,128]{3,2,1,0:T(8,128)(2,1)}, bf16[4,7,64,128]{3,2,1,0:T(8,128)(2,1)S(1)}, u32[]{:S(2)}, u32[]{:S(2)}) collective-permute-start(bf16[4,7,64,128]{3,2,1,0:T(8,128)(2,1)} %get-tuple-element.246), channel_id=1, source_target_pairs={{0,3},{1,2},{2,1},{3,0},{4,7},{5,6},{6,5},{7,4},{8,11},{9,10},{10,... | collective-permute-start | bytes 1376264 | tf_op jit(solution)/shard_map/ppermute | solution.py:964
  191.3 41.2 %collective-permute-start.18 = (f32[64,2304]{1,0:T(8,128)}, f32[64,2304]{1,0:T(8,128)S(1)}, u32[]{:S(2)}, u32[]{:S(2)}) collective-permute-start(f32[64,2304]{1,0:T(8,128)} %get-tuple-element.236), channel_id=1, source_target_pairs={{0,1},{1,0},{2,3},{3,2},{4,5},{5,4},{6,7},{7,6},{8,9},{9,8},{10,11... | collective-permute-start | bytes 1769480 | tf_op jit(solution)/shard_map/ppermute | solution.py:964
  192.8 39.8 %collective-permute-start.19 = (f32[64,2304]{1,0:T(8,128)S(1)}, f32[64,2304]{1,0:T(8,128)S(1)}, u32[]{:S(2)}, u32[]{:S(2)}) collective-permute-start(f32[64,2304]{1,0:T(8,128)S(1)} %copy-done.11), channel_id=1, source_target_pairs={{0,2},{1,3},{2,0},{3,1},{4,6},{5,7},{6,4},{7,5},{8,10},{9,11},{10,... | collective-permute-start | bytes 1769480 | tf_op jit(solution)/shard_map/ppermute | solution.py:964
  194.7 39.4 %collective-permute-start.20 = (f32[64,2304]{1,0:T(8,128)}, f32[64,2304]{1,0:T(8,128)S(1)}, u32[]{:S(2)}, u32[]{:S(2)}) collective-permute-start(f32[64,2304]{1,0:T(8,128)} %get-tuple-element.238), channel_id=1, source_target_pairs={{0,3},{1,2},{2,1},{3,0},{4,7},{5,6},{6,5},{7,4},{8,11},{9,10},{10,... | collective-permute-start | bytes 1769480 | tf_op jit(solution)/shard_map/ppermute | solution.py:964
  229.1 9.8 %collective-permute-start.24 = (f32[64,384]{1,0:T(8,128)}, f32[64,384]{1,0:T(8,128)S(1)}, u32[]{:S(2)}, u32[]{:S(2)}) collective-permute-start(f32[64,384]{1,0:T(8,128)} %get-tuple-element.258), channel_id=1, source_target_pairs={{0,1},{1,0},{2,3},{3,2},{4,5},{5,4},{6,7},{7,6},{8,9},{9,8},{10,11... | collective-permute-start | bytes 294920 | tf_op jit(solution)/shard_map/ppermute | solution.py:964
  230.6 53.3 %collective-permute-start.25 = (f32[64,384]{1,0:T(8,128)}, f32[64,384]{1,0:T(8,128)}, u32[]{:S(2)}, u32[]{:S(2)}) collective-permute-start(f32[64,384]{1,0:T(8,128)} %get-tuple-element.259), channel_id=1, source_target_pairs={{0,2},{1,3},{2,0},{3,1},{4,6},{5,7},{6,4},{7,5},{8,10},{9,11},{10,... | collective-permute-start | bytes 294920 | tf_op jit(solution)/shard_map/ppermute | solution.py:964
  232.5 51.4 %collective-permute-start.26 = (f32[64,384]{1,0:T(8,128)}, f32[64,384]{1,0:T(8,128)}, u32[]{:S(2)}, u32[]{:S(2)}) collective-permute-start(f32[64,384]{1,0:T(8,128)} %get-tuple-element.260), channel_id=1, source_target_pairs={{0,3},{1,2},{2,1},{3,0},{4,7},{5,6},{6,5},{7,4},{8,11},{9,10},{10,... | collective-permute-start | bytes 294920 | tf_op jit(solution)/shard_map/ppermute | solution.py:964
  232.6 53.1 %collective-permute-start.28 = (bf16[4,7,64,256]{3,2,1,0:T(8,128)(2,1)}, bf16[4,7,64,256]{3,2,1,0:T(8,128)(2,1)S(1)}, u32[]{:S(2)}, u32[]{:S(2)}) collective-permute-start(bf16[4,7,64,256]{3,2,1,0:T(8,128)(2,1)} %get-tuple-element.269), channel_id=1, source_target_pairs={{0,1},{1,0},{2,3},{3,2},{4,5},{5,4},{6,7},{7,6},{8,9},{9,8},{10,11... | collective-permute-start | bytes 2752520 | tf_op jit(solution)/shard_map/ppermute | solution.py:964
  234.9 50.8 %collective-permute-start.29 = (bf16[4,7,64,256]{3,2,1,0:T(8,128)(2,1)}, bf16[4,7,64,256]{3,2,1,0:T(8,128)(2,1)S(1)}, u32[]{:S(2)}, u32[]{:S(2)}) collective-permute-start(bf16[4,7,64,256]{3,2,1,0:T(8,128)(2,1)} %get-tuple-element.270), channel_id=1, source_target_pairs={{0,2},{1,3},{2,0},{3,1},{4,6},{5,7},{6,4},{7,5},{8,10},{9,11},{10,... | collective-permute-start | bytes 2752520 | tf_op jit(solution)/shard_map/ppermute | solution.py:964
  238.8 46.9 %collective-permute-start.30 = (bf16[4,7,64,256]{3,2,1,0:T(8,128)(2,1)}, bf16[4,7,64,256]{3,2,1,0:T(8,128)(2,1)S(1)}, u32[]{:S(2)}, u32[]{:S(2)}) collective-permute-start(bf16[4,7,64,256]{3,2,1,0:T(8,128)(2,1)} %get-tuple-element.271), channel_id=1, source_target_pairs={{0,3},{1,2},{2,1},{3,0},{4,7},{5,6},{6,5},{7,4},{8,11},{9,10},{10,... | collective-permute-start | bytes 2752520 | tf_op jit(solution)/shard_map/ppermute | solution.py:964
  285.7 12.4 %collective-permute-start.27 = (f32[32,2688]{1,0:T(8,128)}, f32[32,2688]{1,0:T(8,128)S(1)}, u32[]{:S(2)}, u32[]{:S(2)}) collective-permute-start(f32[32,2688]{1,0:T(8,128)} %get-tuple-element.321), channel_id=1, source_target_pairs={{0,4},{4,0},{8,12},{12,8},{16,20},{20,16},{24,28},{28,24},{1,5},{5... | collective-permute-start | bytes 1032200 | tf_op jit(solution)/shard_map/ppermute | solution.py:964
  298.2 24.2 %collective-permute-start.31 = (f32[32,2688]{1,0:T(8,128)S(1)}, f32[32,2688]{1,0:T(8,128)S(1)}, u32[]{:S(2)}, u32[]{:S(2)}) collective-permute-start(f32[32,2688]{1,0:T(8,128)S(1)} %add.73), channel_id=1, source_target_pairs={{0,16},{4,20},{8,24},{12,28},{16,0},{20,4},{24,8},{28,12},{1,17},{... | collective-permute-start | bytes 1032200 | tf_op jit(solution)/shard_map/ppermute | solution.py:964
  322.4 21.3 %collective-permute-start.35 = (f32[32,2688]{1,0:T(8,128)S(1)}, f32[32,2688]{1,0:T(8,128)S(1)}, u32[]{:S(2)}, u32[]{:S(2)}) collective-permute-start(f32[32,2688]{1,0:T(8,128)S(1)} %add.74), channel_id=1, source_target_pairs={{0,8},{4,12},{8,0},{12,4},{16,24},{20,28},{24,16},{28,20},{1,9},{5... | collective-permute-start | bytes 1032200 | tf_op jit(solution)/shard_map/ppermute | solution.py:964
  349.3 7.9 %collective-permute-start.39 = (bf16[96,384]{1,0:T(8,128)(2,1)S(1)}, bf16[96,384]{1,0:T(8,128)(2,1)S(1)}, u32[]{:S(2)}, u32[]{:S(2)}) collective-permute-start(bf16[96,384]{1,0:T(8,128)(2,1)S(1)} %fusion.3), channel_id=1, source_target_pairs={{0,16},{4,20},{8,24},{12,28},{16,0},{20,4},{24,8},{28,12},{1,17},{... | collective-permute-start | bytes 221192 | tf_op jit(solution)/shard_map/ppermute | solution.py:964
  (48 other events, 427.5 us)
